TPU v7x, 512 devices: a whole 4x8x8 slice. The times are simulated.
512 devices in a mesh: az: 64 (over z, x, y_hi), rad: 8 (over y_lo, core).
Axes of the slice: x: 4, y: 8 (y_hi: 2, y_lo: 4; y = y_hi * 4 + y_lo), z: 8, core: 2. Of those that a mesh axis runs over, the one named last changes fastest.
Arguments:
- fields: float32 [5, 2, 768, 16384], P(None, None, 'rad', 'az'), as said below
- shifts: int32 [768], P('rad'), may hold values from 0 to 16383, as said below
- cycle_area: float32 [768], P('rad'), may hold values from 0.5 to 2
- gravity: float32 [768], P('rad'), may hold values from 0.00013020834 to 0.0013020834
- kappa_az: float32 [768], P('rad'), may hold values from 0.05 to 0.24
- kappa_rad: float32 [768], P('rad'), may hold values from 0.05 to 0.24
Outputs:
- updated: float32 [5, 2, 768, 16384], P(None, None, 'rad', 'az')
- enclosed: float32 [768], P('rad')
Inputs may be any that keep to these rules, and one draw needn't show every extreme that they name: shifts[r] is the whole number of cells by which row r moves toward higher azimuth. fields[0] is positive.
All inputs are finite; a program needn't handle non-finite values.
Results may differ from a plain program's by a relative error of at most 0.00002.
Values sent between devices are 32-bit elements; how exact they have to be, the bound alone decides.
No kernel may reach another device: no remote copies, remote signals or barrier semaphores. Data moves between devices by JAX's collectives and lax.ppermute only.
A program may use at most 64 MiB of HBM per device.

v0:
```python
import jax
import jax.numpy as jnp
from jax import lax
from jax.sharding import PartitionSpec as P

star_mass = 1.0


def entering(part, axis, combine, identity):
    place = lax.axis_index(axis)
    gathered = lax.all_gather(part, axis)
    state = jnp.zeros_like(part) + jnp.asarray(identity, part.dtype)

    def one(lap, state):
        return combine(state, lax.dynamic_index_in_dim(gathered, lap, 0, False))

    return lax.fori_loop(0, place, one, state)


def passed_along(value, axis, steps):
    count = lax.axis_size(axis)
    pairs = [(source, (source + steps) % count) for source in range(count)]
    return lax.ppermute(value, axis, pairs)


def with_halo(cells, sides, width, closed):
    for axis, dim in sides:
        count = lax.axis_size(axis)
        ends = count if closed else count - 1
        head = lax.slice_in_dim(cells, 0, width, axis=dim)
        tail = lax.slice_in_dim(cells, cells.shape[dim] - width, cells.shape[dim], axis=dim)
        cells = jnp.concatenate(
            [
                lax.ppermute(tail, axis, [(i, (i + 1) % count) for i in range(ends)]),
                cells,
                lax.ppermute(head, axis, [((i + 1) % count, i) for i in range(ends)]),
            ],
            axis=dim,
        )
    return cells


def add_totals(earlier, later):
    return earlier + later


def roll_by_bits(values, amounts, bit_total, axis):
    for bit_level in range(bit_total):
        rolled = jnp.roll(values, 1 << bit_level, axis=axis)
        chosen = amounts >> bit_level & 1 == 1
        values = jnp.where(chosen, rolled, values)
    return values


def cross_cells(current, previous, remain):
    cells_dev = current.shape[3]
    joined = jnp.concatenate([previous, current], axis=3)
    bit_total = max((cells_dev - 1).bit_length(), 1)
    moved = roll_by_bits(joined, remain[None, None, :, None], bit_total, 3)
    return moved[:, :, :, cells_dev:]


def shards(fields, shifts, cycle_area, gravity, kappa_az, kappa_rad):
    cells_dev = fields.shape[3]
    cycle_size = lax.axis_size("az")
    cycle_cells = cells_dev * cycle_size
    density = fields[0]
    local_mass = jnp.sum(density, axis=(0, 2))
    row_mass = cycle_area * lax.psum(local_mass, "az") / (2.0 * cycle_cells)
    before = jnp.cumsum(row_mass) - row_mass
    block_mass = jnp.sum(row_mass)
    offset = entering(block_mass, "rad", add_totals, jnp.float32(0.0))
    enclosed = star_mass + offset + before + 0.5 * row_mass
    pull_rate = (gravity * enclosed)[None, :, None]
    momentum = fields[1] - pull_rate * density
    energy = fields[3] - pull_rate * fields[1]
    current = jnp.stack([density, momentum, fields[2], energy, fields[4]])
    device_steps = shifts // cells_dev
    remain = shifts - device_steps * cells_dev
    bit_count = cycle_size.bit_length() - 1
    for bit_level in range(bit_count):
        rolled = passed_along(current, "az", 1 << bit_level)
        chosen = device_steps >> bit_level & 1 == 1
        current = jnp.where(chosen[None, None, :, None], rolled, current)
    previous = passed_along(current, "az", 1)
    advected = cross_cells(current, previous, remain)
    cycle_pad = with_halo(advected, (("az", 3),), 1, True)
    beside_all = cycle_pad[:, :, :, 2:] + cycle_pad[:, :, :, :-2] - 2.0 * advected
    radial_pad = with_halo(advected, (("rad", 2),), 1, False)
    across = radial_pad[:, :, 2:] + radial_pad[:, :, :-2] - 2.0 * advected
    updated = (
        advected
        + kappa_az[None, None, :, None] * beside_all
        + kappa_rad[None, None, :, None] * across
    )
    return (updated, enclosed)


def solution(mesh):
    placed = (P(None, None, "rad", "az"), P("rad"), P("rad"), P("rad"), P("rad"), P("rad"))
    return jax.shard_map(
        shards,
        mesh=mesh,
        in_specs=placed,
        out_specs=(P(None, None, "rad", "az"), P("rad")),
        check_vma=False,
    )
```

profile of v0, /device:TPU:18, one launch (start us, length us, event | category | flops | bytes accessed | tf_op | source)
XLA Modules:
  0.0 626.3 jit_solution(10465843969026784065)
XLA Ops:
  0.7 1.1 slice_reduce_fusion
  1.8 226.0 %psum.7 = f32[96]{0:T(128)S(1)} all-reduce(f32[96]{0:T(128)S(1)} %get-tuple-element.43), channel_id=1, replica_groups=mesh['az'=64,'rad'=8] {'az'}, use_global_device_ids=true, to_apply=%region_1.0 | all-reduce | flops 96 | bytes 768 | tf_op jit(solution)/shard_map/psum | solution.py:69
  227.8 1.3 dynamic-slice
  229.1 1.3 fusion.11
  230.3 1.3 dynamic-update-slice
  231.6 10.0 %all-reduce = f32[8]{0:T(128)S(1)} all-reduce(f32[8]{0:T(128)S(1)} %dynamic-update-slice), channel_id=1, replica_groups=mesh['az'=64,'rad'=8] {'rad'}, use_global_device_ids=true, to_apply=%add | all-reduce | flops 8 | bytes 64
  241.6 4.7 while.10
  241.6 0.6 dynamic_slice.5
  242.8 0.6 dynamic_slice.5
  244.0 0.6 dynamic_slice.5
  245.1 0.6 dynamic_slice.5
  246.6 1.2 fusion.12
  247.8 1.1 subtract_dynamic-update-slice_fusion.1
  248.9 0.9 slice_dynamic-update-slice_fusion.1
  250.0 1.9 collective-permute-start
  252.0 50.4 %collective-permute-done = f32[5,2,96,256]{3,2,1,0:T(8,128)S(1)} collective-permute-done((f32[5,2,96,256]{3,2,1,0:T(8,128)S(1)}, f32[5,2,96,256]{3,2,1,0:T(8,128)S(1)}, u32[]{:S(2)}, u32[]{:S(2)}) %collective-permute-start) | collective-permute-done | bytes 983072 | tf_op jit(solution)/shard_map/ppermute | solution.py:23
  302.5 1.9 collective-permute-start.1
  304.5 25.2 %collective-permute-done.1 = f32[5,2,96,256]{3,2,1,0:T(8,128)S(1)} collective-permute-done((f32[5,2,96,256]{3,2,1,0:T(8,128)S(1)}, f32[5,2,96,256]{3,2,1,0:T(8,128)S(1)}, u32[]{:S(2)}, u32[]{:S(2)}) %collective-permute-start.1) | collective-permute-done | bytes 983072 | tf_op jit(solution)/shard_map/ppermute | solution.py:23
  329.8 1.9 collective-permute-start.2
  331.8 40.8 %collective-permute-done.2 = f32[5,2,96,256]{3,2,1,0:T(8,128)S(1)} collective-permute-done((f32[5,2,96,256]{3,2,1,0:T(8,128)S(1)}, f32[5,2,96,256]{3,2,1,0:T(8,128)S(1)}, u32[]{:S(2)}, u32[]{:S(2)}) %collective-permute-start.2) | collective-permute-done | bytes 983072 | tf_op jit(solution)/shard_map/ppermute | solution.py:23
  372.7 1.9 collective-permute-start.3
  374.6 23.5 %collective-permute-done.3 = f32[5,2,96,256]{3,2,1,0:T(8,128)S(1)} collective-permute-done((f32[5,2,96,256]{3,2,1,0:T(8,128)S(1)}, f32[5,2,96,256]{3,2,1,0:T(8,128)S(1)}, u32[]{:S(2)}, u32[]{:S(2)}) %collective-permute-start.3) | collective-permute-done | bytes 983072 | tf_op jit(solution)/shard_map/ppermute | solution.py:23
  398.3 1.9 collective-permute-start.4
  400.2 42.6 %collective-permute-done.4 = f32[5,2,96,256]{3,2,1,0:T(8,128)S(1)} collective-permute-done((f32[5,2,96,256]{3,2,1,0:T(8,128)S(1)}, f32[5,2,96,256]{3,2,1,0:T(8,128)S(1)}, u32[]{:S(2)}, u32[]{:S(2)}) %collective-permute-start.4) | collective-permute-done | bytes 983072 | tf_op jit(solution)/shard_map/ppermute | solution.py:23
  443.0 3.7 collective-permute-start.5
  446.8 44.3 %collective-permute-done.5 = f32[5,2,96,256]{3,2,1,0:T(8,128)S(1)} collective-permute-done((f32[5,2,96,256]{3,2,1,0:T(8,128)S(1)}, f32[5,2,96,256]{3,2,1,0:T(8,128)S(1)}, u32[]{:S(2)}, u32[]{:S(2)}) %collective-permute-start.5) | collective-permute-done | bytes 983072 | tf_op jit(solution)/shard_map/ppermute | solution.py:23
  491.3 4.7 collective-permute-start.6
  495.9 0.2 slice.146
  496.1 25.1 %collective-permute-done.6 = f32[5,2,96,256]{3,2,1,0:T(8,128)S(1)} collective-permute-done((f32[5,2,96,256]{3,2,1,0:T(8,128)S(1)}, f32[5,2,96,256]{3,2,1,0:T(8,128)S(1)}, u32[]{:S(2)}, u32[]{:S(2)}) %collective-permute-start.6) | collective-permute-done | bytes 983072 | tf_op jit(solution)/shard_map/ppermute | solution.py:23
  521.2 0.3 fusion
  521.5 0.6 fusion.1
  522.1 0.2 slice.149
  522.3 0.6 maximum_select_fusion
  522.9 0.2 slice.151
  523.1 0.6 maximum_select_fusion.1
  523.9 0.6 maximum_select_fusion.2
  524.7 0.6 maximum_select_fusion.3
  525.6 0.6 maximum_select_fusion.4
  526.4 0.6 maximum_select_fusion.5
  527.3 0.4 maximum_select_fusion.6
  527.7 11.1 %collective-permute-start.9 = (f32[5,2,1,256]{3,2,1,0:T(1,128)S(1)}, f32[5,2,1,256]{3,2,1,0:T(1,128)S(1)}, u32[]{:S(2)}, u32[]{:S(2)}) collective-permute-start(f32[5,2,1,256]{3,2,1,0:T(1,128)S(1)} %get-tuple-element.41), channel_id=1, source_target_pairs={{1,0},{2,1},{3,2},{4,3},{5,4},{6,5},{7,6},{9,8},{10,9},{11,10},{12... | collective-permute-start | bytes 30728 | tf_op jit(solution)/shard_map/ppermute | solution.py:36
  538.8 1.9 collective-permute-start.10
  540.7 0.2 fusion.13
  540.9 1.9 collective-permute-start.7
  542.8 10.5 %collective-permute-start.8 = (f32[5,2,96,1]{3,2,1,0:T(8,128)S(1)}, f32[5,2,96,1]{3,2,1,0:T(8,128)S(1)}, u32[]{:S(2)}, u32[]{:S(2)}) collective-permute-start(f32[5,2,96,1]{3,2,1,0:T(8,128)S(1)} %get-tuple-element.40), channel_id=1, source_target_pairs={{0,8},{8,16},{16,24},{24,32},{32,40},{40,48},{48,56},{56,64},{64,7... | collective-permute-start | bytes 11528 | tf_op jit(solution)/shard_map/ppermute | solution.py:34
  553.5 4.9 collective-permute-done.7
  558.3 66.1 %collective-permute-done.8 = f32[5,2,96,1]{3,2,1,0:T(8,128)S(1)} collective-permute-done((f32[5,2,96,1]{3,2,1,0:T(8,128)S(1)}, f32[5,2,96,1]{3,2,1,0:T(8,128)S(1)}, u32[]{:S(2)}, u32[]{:S(2)}) %collective-permute-start.8) | collective-permute-done | bytes 3872 | tf_op jit(solution)/shard_map/ppermute | solution.py:34
  624.4 1.9 fusion.5
  (33 shorter events, 2.7 us)
Async XLA Ops:
  0.6 249.3 %copy-start = (f32[5,2,96,256]{3,2,1,0:T(8,128)S(1)}, f32[5,2,96,256]{3,2,1,0:T(8,128)}, u32[]{:S(2)}) copy-start(f32[5,2,96,256]{3,2,1,0:T(8,128)} %param.8) | copy-start | bytes 2949124
  0.6 251.3 %copy-start.1 = (s32[96]{0:T(128)S(1)}, s32[96]{0:T(128)}, u32[]{:S(2)}) copy-start(s32[96]{0:T(128)} %param.9) | copy-start | bytes 1156
  250.0 52.3 %collective-permute-start = (f32[5,2,96,256]{3,2,1,0:T(8,128)S(1)}, f32[5,2,96,256]{3,2,1,0:T(8,128)S(1)}, u32[]{:S(2)}, u32[]{:S(2)}) collective-permute-start(f32[5,2,96,256]{3,2,1,0:T(8,128)S(1)} %slice_dynamic-update-slice_fusion), channel_id=1, source_target_pairs={{0,8},{8,16},{16,24},{24,32},{32,40},{40,48},{48,56},{56,64},{64,7... | collective-permute-start | bytes 2949128 | tf_op jit(solution)/shard_map/ppermute | solution.py:23
  302.5 27.1 %collective-permute-start.1 = (f32[5,2,96,256]{3,2,1,0:T(8,128)S(1)}, f32[5,2,96,256]{3,2,1,0:T(8,128)S(1)}, u32[]{:S(2)}, u32[]{:S(2)}) collective-permute-start(f32[5,2,96,256]{3,2,1,0:T(8,128)S(1)} %broadcast_select_fusion), channel_id=1, source_target_pairs={{0,16},{8,24},{16,32},{24,40},{32,48},{40,56},{48,64},{56,72},{64,... | collective-permute-start | bytes 2949128 | tf_op jit(solution)/shard_map/ppermute | solution.py:23
  329.8 42.7 %collective-permute-start.2 = (f32[5,2,96,256]{3,2,1,0:T(8,128)S(1)}, f32[5,2,96,256]{3,2,1,0:T(8,128)S(1)}, u32[]{:S(2)}, u32[]{:S(2)}) collective-permute-start(f32[5,2,96,256]{3,2,1,0:T(8,128)S(1)} %broadcast_select_fusion.1), channel_id=1, source_target_pairs={{0,32},{8,40},{16,48},{24,56},{32,64},{40,72},{48,80},{56,88},{64,... | collective-permute-start | bytes 2949128 | tf_op jit(solution)/shard_map/ppermute | solution.py:23
  372.7 25.4 %collective-permute-start.3 = (f32[5,2,96,256]{3,2,1,0:T(8,128)S(1)}, f32[5,2,96,256]{3,2,1,0:T(8,128)S(1)}, u32[]{:S(2)}, u32[]{:S(2)}) collective-permute-start(f32[5,2,96,256]{3,2,1,0:T(8,128)S(1)} %broadcast_select_fusion.2), channel_id=1, source_target_pairs={{0,64},{8,72},{16,80},{24,88},{32,96},{40,104},{48,112},{56,120},{... | collective-permute-start | bytes 2949128 | tf_op jit(solution)/shard_map/ppermute | solution.py:23
  398.3 44.6 %collective-permute-start.4 = (f32[5,2,96,256]{3,2,1,0:T(8,128)S(1)}, f32[5,2,96,256]{3,2,1,0:T(8,128)S(1)}, u32[]{:S(2)}, u32[]{:S(2)}) collective-permute-start(f32[5,2,96,256]{3,2,1,0:T(8,128)S(1)} %broadcast_select_fusion.3), channel_id=1, source_target_pairs={{0,128},{8,136},{16,144},{24,152},{32,160},{40,168},{48,176},{56,1... | collective-permute-start | bytes 2949128 | tf_op jit(solution)/shard_map/ppermute | solution.py:23
  443.0 48.0 %collective-permute-start.5 = (f32[5,2,96,256]{3,2,1,0:T(8,128)S(1)}, f32[5,2,96,256]{3,2,1,0:T(8,128)S(1)}, u32[]{:S(2)}, u32[]{:S(2)}) collective-permute-start(f32[5,2,96,256]{3,2,1,0:T(8,128)S(1)} %broadcast_select_fusion.4), channel_id=1, source_target_pairs={{0,256},{8,264},{16,272},{24,280},{32,288},{40,296},{48,304},{56,3... | collective-permute-start | bytes 2949128 | tf_op jit(solution)/shard_map/ppermute | solution.py:23
  491.3 29.9 %collective-permute-start.6 = (f32[5,2,96,256]{3,2,1,0:T(8,128)S(1)}, f32[5,2,96,256]{3,2,1,0:T(8,128)S(1)}, u32[]{:S(2)}, u32[]{:S(2)}) collective-permute-start(f32[5,2,96,256]{3,2,1,0:T(8,128)S(1)} %broadcast_select_fusion.5), channel_id=1, source_target_pairs={{0,8},{8,16},{16,24},{24,32},{32,40},{40,48},{48,56},{56,64},{64,7... | collective-permute-start | bytes 2949128 | tf_op jit(solution)/shard_map/ppermute | solution.py:23
  527.7 96.7 %collective-permute-start.9 = (f32[5,2,1,256]{3,2,1,0:T(1,128)S(1)}, f32[5,2,1,256]{3,2,1,0:T(1,128)S(1)}, u32[]{:S(2)}, u32[]{:S(2)}) collective-permute-start(f32[5,2,1,256]{3,2,1,0:T(1,128)S(1)} %get-tuple-element.41), channel_id=1, source_target_pairs={{1,0},{2,1},{3,2},{4,3},{5,4},{6,5},{7,6},{9,8},{10,9},{11,10},{12... | collective-permute-start | bytes 30728 | tf_op jit(solution)/shard_map/ppermute | solution.py:36
  538.8 85.7 %copy-start.2 = (f32[96]{0:T(128)S(1)}, f32[96]{0:T(128)}, u32[]{:S(2)}) copy-start(f32[96]{0:T(128)} %param.13) | copy-start | bytes 1156
  538.8 85.7 %copy-start.3 = (f32[96]{0:T(128)S(1)}, f32[96]{0:T(128)}, u32[]{:S(2)}) copy-start(f32[96]{0:T(128)} %param.12) | copy-start | bytes 1156
  538.8 85.6 %collective-permute-start.10 = (f32[5,2,1,256]{3,2,1,0:T(1,128)S(1)}, f32[5,2,1,256]{3,2,1,0:T(1,128)S(1)}, u32[]{:S(2)}, u32[]{:S(2)}) collective-permute-start(f32[5,2,1,256]{3,2,1,0:T(1,128)S(1)} %get-tuple-element.42), channel_id=1, source_target_pairs={{0,1},{1,2},{2,3},{3,4},{4,5},{5,6},{6,7},{8,9},{9,10},{10,11},{11... | collective-permute-start | bytes 30728 | tf_op jit(solution)/shard_map/ppermute | solution.py:34
  540.9 17.4 %collective-permute-start.7 = (f32[5,2,96,1]{3,2,1,0:T(8,128)S(1)}, f32[5,2,96,1]{3,2,1,0:T(8,128)S(1)}, u32[]{:S(2)}, u32[]{:S(2)}) collective-permute-start(f32[5,2,96,1]{3,2,1,0:T(8,128)S(1)} %get-tuple-element.39), channel_id=1, source_target_pairs={{8,0},{16,8},{24,16},{32,24},{40,32},{48,40},{56,48},{64,56},{72,6... | collective-permute-start | bytes 11528 | tf_op jit(solution)/shard_map/ppermute | solution.py:36
  542.8 81.6 %collective-permute-start.8 = (f32[5,2,96,1]{3,2,1,0:T(8,128)S(1)}, f32[5,2,96,1]{3,2,1,0:T(8,128)S(1)}, u32[]{:S(2)}, u32[]{:S(2)}) collective-permute-start(f32[5,2,96,1]{3,2,1,0:T(8,128)S(1)} %get-tuple-element.40), channel_id=1, source_target_pairs={{0,8},{8,16},{16,24},{24,32},{32,40},{40,48},{48,56},{56,64},{64,7... | collective-permute-start | bytes 11528 | tf_op jit(solution)/shard_map/ppermute | solution.py:34
where the time goes:
time: 627 us; the launch traced here: 626 us
  waiting for transfers between devices  323 us (52%)
  blocking collectives  236 us (38%)
  starting transfers between devices  43.4 us (7%)
  other arithmetic  13 us (2%)
  local copies, waits for them, and re-layouts  7.84 us (1%)
    ppermute x7, waiting for transfers between devices, passed_along(): return lax.ppermute(value, axis, pairs)  252 us
    psum x1, blocking collectives, shards(): row_mass = cycle_area * lax.psum(local_mass, 'az') / (2.0 * cycle_cells)  226 us
    ppermute x2, waiting for transfers between devices, with_halo(): lax.ppermute(tail, axis, [(i, (i + 1) % count) for i in range(ends)])  66.1 us
    ppermute x7, starting transfers between devices, passed_along(): return lax.ppermute(value, axis, pairs)  18 us
    ppermute x2, starting transfers between devices, with_halo(): lax.ppermute(head, axis, [((i + 1) % count, i) for i in range(ends)])  13 us
  transfers between devices with their start and end apart: 11, of which 9 were waited for; matrix products, arithmetic and copies ran while one was open for 0% of the time, Pallas kernels for 0%

commit v1 on v0

v1 whole, which is shorter than its diff:
```python
import jax
import jax.numpy as jnp
from jax import lax
from jax.experimental import pallas as pl
from jax.experimental.pallas import tpu as pltpu
from jax.sharding import PartitionSpec as P

star_mass = 1.0

ORDER = (0, 1, 3, 2, 4)
RING = 64
GROUPS = 3
ROWS = 96
SPAN = ROWS // GROUPS
HALF = 16
BLOCK = 2 * HALF
PIECES = 2 * RING
VMEM_LIMIT = 24 * 1024 * 1024

TILES = ((0, 1, 5), (1, 2, 2))


def iotas():
    lane = lax.broadcasted_iota(jnp.int32, (8, 128), 1)
    line = lax.broadcasted_iota(jnp.int32, (8, 128), 0)
    return lane, line


def pack_kernel(fields, packed):
    for place, field in enumerate(ORDER):
        for layer in range(2):
            for group in range(GROUPS):
                for half in range(2):
                    first = BLOCK * layer + HALF * half + 5 * group + place
                    packed[pl.ds(first, SPAN, stride=2 * BLOCK), :] = fields[
                        field, layer, pl.ds(SPAN * group, SPAN), pl.ds(128 * half, 128)
                    ]
    cells = [fields[0, z, :, pl.ds(128 * h, 128)] for z in range(2) for h in range(2)]
    total = (cells[0] + cells[1]) + (cells[2] + cells[3])
    square = jnp.concatenate([total, jnp.zeros((128 - ROWS, 128), jnp.float32)], axis=0)
    mass = jnp.sum(square.T, axis=0, keepdims=True)
    packed[pl.ds(15, RING, stride=BLOCK), :] = jnp.broadcast_to(mass, (RING, 128))
    packed[pl.ds(31, RING, stride=BLOCK), :] = jnp.zeros((RING, 128), jnp.float32)


def shift_kernel(place, shifts, lines, moved, mass):
    lane, line = iotas()
    row = place[0] >> 1
    whole, part, early = [], [], []
    for group in range(GROUPS):
        shift = shifts[SPAN * group + row]
        whole.append(shift >> 7)
        part.append(shift & 127)
        early.append(lane < part[group])

    def turned(piece, tile, group):
        at = pl.multiple_of(((piece - whole[group]) & (PIECES - 1)) * HALF + 8 * tile, 8)
        return pltpu.roll(lines[pl.ds(at, 8), :], part[group], 1)

    def one(ring, state):
        before, edges = state
        for half in range(2):
            piece = 2 * ring + half
            now, kept = [], []
            for tile, (first, second, split) in enumerate(TILES):
                a, b = turned(piece, tile, first), turned(piece, tile, second)
                pa, pb = before[tile]
                value = jnp.where(
                    line < split, jnp.where(early[first], pa, a), jnp.where(early[second], pb, b)
                )
                at = pl.multiple_of(piece * HALF + 8 * tile, 8)
                moved[pl.ds(at, 8), :] = value
                now.append((a, b))
                if half == 0:
                    owner = (ring + RING - 1) & (RING - 1)
                    slot = RING + owner
                    kept.append(jnp.where(lane == slot, pltpu.roll(value, slot, 1), edges[tile]))
                else:
                    owner = (ring + 1) & (RING - 1)
                    kept.append(jnp.where(lane == owner, pltpu.roll(value, owner + 1, 1), edges[tile]))
            before, edges = tuple(now), tuple(kept)
        return before, edges

    before = tuple(
        (turned(PIECES - 1, tile, first), turned(PIECES - 1, tile, second))
        for tile, (first, second, _) in enumerate(TILES)
    )
    zero = jnp.zeros((8, 128), jnp.float32)
    _, edges = lax.fori_loop(0, RING, one, (before, (zero, zero)), unroll=4)
    square = jnp.concatenate([edges[0], edges[1], jnp.zeros((112, 128), jnp.float32)], axis=0).T
    moved[pl.ds(15, RING, stride=BLOCK), :] = square[:RING]
    moved[pl.ds(31, RING, stride=BLOCK), :] = square[RING:]
    parts = lines[pl.ds(15, RING, stride=BLOCK), :]
    mass[...] = jnp.broadcast_to(jnp.sum(parts, axis=0, keepdims=True), (8, 128))


def spread_kernel(kappa_az, kappa_rad, pull, lines, below, above, updated, sourced, partial):
    lane, line = iotas()
    square = jnp.concatenate(
        [lines[pl.ds(15, RING, stride=BLOCK), :], lines[pl.ds(31, RING, stride=BLOCK), :]], axis=0
    ).T
    edges = (square[0:8], square[8:16])
    takes = (((line == 1) | (line == 2), (line == 6) | (line == 7)), (line < 0, (line == 3) | (line == 4)))

    def spread(values, row, tile):
        first, second, split = TILES[tile]
        return jnp.where(line < split, values[SPAN * first + row], values[SPAN * second + row])

    def source(value, rate):
        return value - rate * pltpu.roll(value, 1, 0)

    def one(row, carry):
        for tile, (first, second, _) in enumerate(TILES):
            az = spread(kappa_az, row, tile)
            rad = spread(kappa_rad, row, tile)
            rate = jnp.where(
                takes[tile][0],
                pull[SPAN * first + row + 1],
                jnp.where(takes[tile][1], pull[SPAN * second + row + 1], 0.0),
            )
            for layer in range(2):
                ring = 2 * row + layer
                base = pl.multiple_of(ring * BLOCK + 8 * tile, 8)
                low = lines[pl.ds(base, 8), :]
                high = lines[pl.ds(base + HALF, 8), :]
                low_up, high_up = pltpu.roll(low, 1, 1), pltpu.roll(high, 1, 1)
                low_down, high_down = pltpu.roll(low, 127, 1), pltpu.roll(high, 127, 1)
                left = pltpu.roll(edges[tile], (128 - ring) & 127, 1)
                right = pltpu.roll(edges[tile], 63 - ring, 1)
                sides = (
                    jnp.where(lane == 0, left, low_up) + jnp.where(lane == 127, high_down, low_down),
                    jnp.where(lane == 0, low_up, high_up) + jnp.where(lane == 127, right, high_down),
                )
                for half, value in enumerate((low, high)):
                    closed = value + az * (sides[half] - 2.0 * value)
                    full = source(value, rate)
                    sourced[pl.ds(base + 2 * BLOCK + HALF * half, 8), :] = full
                    partial[pl.ds(base + HALF * half, 8), :] = source(closed, rate) - 2.0 * rad * full
        return carry

    lax.fori_loop(0, SPAN, one, 0, unroll=2)

    for layer in range(2):
        for half in range(2):
            at = BLOCK * layer + HALF * half
            under = source(below[pl.ds(at + 8, 8), :], jnp.where(takes[1][1], pull[0], 0.0))
            over = source(above[pl.ds(at, 8), :], jnp.where(takes[0][0], pull[ROWS + 1], 0.0))
            sourced[pl.ds(at, 5), :] = under[2:7]
            sourced[pl.ds(at + 5, 10), :] = sourced[pl.ds(RING * BLOCK + at, 10), :]
            top = (RING + 2) * BLOCK + at
            sourced[pl.ds(top, 10), :] = sourced[pl.ds(2 * BLOCK + at + 5, 10), :]
            sourced[pl.ds(top + 10, 5), :] = over[0:5]

    def two(row, carry):
        for tile in range(2):
            rad = spread(kappa_rad, row, tile)
            for layer in range(2):
                for half in range(2):
                    base = pl.multiple_of((2 * row + layer) * BLOCK + HALF * half + 8 * tile, 8)
                    beside = sourced[pl.ds(base, 8), :] + sourced[pl.ds(base + 4 * BLOCK, 8), :]
                    partial[pl.ds(base, 8), :] = partial[pl.ds(base, 8), :] + rad * beside
        return carry

    lax.fori_loop(0, SPAN, two, 0, unroll=4)

    for place, field in enumerate(ORDER):
        for layer in range(2):
            for group in range(GROUPS):
                for half in range(2):
                    first = BLOCK * layer + HALF * half + 5 * group + place
                    updated[field, layer, pl.ds(SPAN * group, SPAN), pl.ds(128 * half, 128)] = partial[
                        pl.ds(first, SPAN, stride=2 * BLOCK), :
                    ]


def specs(*kinds):
    return [pl.BlockSpec(memory_space=kind) for kind in kinds]


def shards(fields, shifts, cycle_area, gravity, kappa_az, kappa_rad):
    vmem, smem = pltpu.VMEM, pltpu.SMEM
    params = pltpu.CompilerParams(vmem_limit_bytes=VMEM_LIMIT)
    blocks = jax.ShapeDtypeStruct((RING * BLOCK, 128), jnp.float32)

    def dealt(lines):
        lines = lines.reshape(RING, BLOCK, 128)
        return lax.all_to_all(lines, "az", 0, 0, tiled=True).reshape(RING * BLOCK, 128)

    packed = pl.pallas_call(
        pack_kernel,
        out_shape=blocks,
        in_specs=specs(vmem),
        out_specs=specs(vmem)[0],
        compiler_params=params,
        name="pack",
    )(fields)
    whole = dealt(packed)
    place = lax.axis_index("az").astype(jnp.int32)[None]
    moved, mass = pl.pallas_call(
        shift_kernel,
        out_shape=(blocks, jax.ShapeDtypeStruct((8, 128), jnp.float32)),
        in_specs=specs(smem, smem, vmem),
        out_specs=specs(vmem, vmem),
        compiler_params=params,
        name="shift",
    )(place, shifts, whole)
    lines = dealt(moved)

    row_mass = cycle_area * mass[0, :ROWS] / (2.0 * RING * 256)
    mine = jnp.stack([row_mass, gravity])
    everyone = lax.all_gather(mine, "rad")
    ranks = everyone.shape[0]
    masses = everyone[:, 0, :]
    totals = jnp.sum(masses, axis=1)
    rank = jnp.arange(ranks)
    offset = jnp.sum(jnp.where(rank[None, :] < rank[:, None], totals[None, :], 0.0), axis=1)
    row = jnp.arange(ROWS)
    before = jnp.sum(jnp.where(row[None, None, :] < row[None, :, None], masses[:, None, :], 0.0), axis=2)
    reach = star_mass + offset[:, None] + before + 0.5 * masses
    pulls = (everyone[:, 1, :] * reach).reshape(ranks * ROWS)
    me = lax.axis_index("rad")
    pull = lax.dynamic_slice(jnp.pad(pulls, (1, 1)), (me * ROWS,), (ROWS + 2,))
    enclosed = lax.dynamic_slice(reach.reshape(ranks * ROWS), (me * ROWS,), (ROWS,))

    up = [(i, i + 1) for i in range(ranks - 1)]
    down = [(i + 1, i) for i in range(ranks - 1)]
    below = lax.ppermute(lines[(RING - 2) * BLOCK :], "rad", up)
    above = lax.ppermute(lines[: 2 * BLOCK], "rad", down)
    updated = pl.pallas_call(
        spread_kernel,
        out_shape=jax.ShapeDtypeStruct(fields.shape, jnp.float32),
        in_specs=specs(smem, smem, smem, vmem, vmem, vmem),
        out_specs=specs(vmem)[0],
        scratch_shapes=[
            pltpu.VMEM(((RING + 4) * BLOCK, 128), jnp.float32),
            pltpu.VMEM((RING * BLOCK, 128), jnp.float32),
        ],
        compiler_params=params,
        name="spread",
    )(kappa_az, kappa_rad, pull, lines, below, above)
    return updated, enclosed


def solution(mesh):
    placed = (P(None, None, "rad", "az"), P("rad"), P("rad"), P("rad"), P("rad"), P("rad"))
    return jax.shard_map(
        shards,
        mesh=mesh,
        in_specs=placed,
        out_specs=(P(None, None, "rad", "az"), P("rad")),
        check_vma=False,
    )
```

time: 627 us -> 115 us (0.18)
  the two profiles are of different devices: /device:TPU:18 before, /device:TPU:1 now
where the time goes in v1:
time: 115 us
  starting transfers between devices  43.3 us (38%)
  waiting for transfers between devices  28.4 us (25%)
  blocking collectives  26.8 us (23%)
  Pallas kernels  10.7 us (9%)
  local copies, waits for them, and re-layouts  4.06 us (4%)
    all_to_all x2, starting transfers between devices, dealt(): lax.all_to_all(lines, 'az', 0, 0, tiled=True).reshape(RING * BLOCK, 128)  32.2 us
    all_gather x1, blocking collectives, shards(): everyone = lax.all_gather(mine, 'rad')  26.8 us
    all_to_all x2, waiting for transfers between devices, dealt(): lax.all_to_all(lines, 'az', 0, 0, tiled=True).reshape(RING * BLOCK, 128)  25.8 us
    ppermute x1, starting transfers between devices, shards(): below = lax.ppermute(lines[(RING - 2) * BLOCK:], 'rad', up)  9.17 us
    pallas_call x1, Pallas kernels, shards(): pl.pallas_call(shift_kernel, out_shape=(blocks, jax.ShapeDtypeStruct((8,...  4.43 us
    pallas_call x1, Pallas kernels, shards(): pl.pallas_call(spread_kernel, out_shape=jax.ShapeDtypeStruct(fields.shape...  4.38 us
    unnamed x12, local copies, waits for them, and re-layouts  3.16 us
    ppermute x1, waiting for transfers between devices, shards(): above = lax.ppermute(lines[:2 * BLOCK], 'rad', down)  2.63 us
  transfers between devices with their start and end apart: 4, of which 2 were waited for; matrix products, arithmetic and copies ran while one was open for 1% of the time, Pallas kernels for 0%

profile of v1, /device:TPU:1, one launch (start us, length us, event | category | flops | bytes accessed | tf_op | source)
XLA Modules:
  0.0 114.6 jit_solution(5864893377880592639)
XLA Ops:
  0.6 0.0 copy-start
  0.6 1.2 %copy-done = f32[5,2,96,256]{3,2,1,0:T(8,128)S(1)} copy-done((f32[5,2,96,256]{3,2,1,0:T(8,128)S(1)}, f32[5,2,96,256]{3,2,1,0:T(8,128)}, u32[]{:S(2)}) %copy-start) | copy-done | bytes 983064
  1.8 1.9 %pack.1 = f32[2048,128]{1,0:T(8,128)} custom-call(f32[5,2,96,256]{3,2,1,0:T(8,128)S(1)} %copy-done), custom_call_target="tpu_custom_call" | custom-call | tf_op jit(solution)/shard_map/pack/pallas_call | solution.py:189
  3.8 19.6 %all-to-all-start = ((f32[64,32,128]{2,1,0:T(8,128)}), f32[64,32,128]{2,1,0:T(8,128)S(1)}, u32[]{:S(2)}, u32[]{:S(2)}) async-start(f32[64,32,128]{2,1,0:T(8,128)} %bitcast.1), calls=%async_computation | async-start | bytes 2097152 | tf_op jit(solution)/shard_map/all_to_all | solution.py:187
  23.4 25.7 %all-to-all-done = f32[64,32,128]{2,1,0:T(8,128)S(1)} async-done(((f32[64,32,128]{2,1,0:T(8,128)}), f32[64,32,128]{2,1,0:T(8,128)S(1)}, u32[]{:S(2)}, u32[]{:S(2)}) %all-to-all-start) | async-done | bytes 1048608 | tf_op jit(solution)/shard_map/all_to_all | solution.py:187
  49.1 0.0 copy-start.1
  49.1 0.7 copy-done.1
  49.8 4.4 %shift.1 = (f32[2048,128]{1,0:T(8,128)}, f32[8,128]{1,0:T(8,128)S(1)}) custom-call(s32[1]{0:T(128)} %bitcast.place, s32[96]{0:T(128)S(1)} %copy-done.1, f32[2048,128]{1,0:T(8,128)S(1)} %bitcast.20), custom_call_target="tpu_custom_call" | custom-call | tf_op jit(solution)/shard_map/shift/pallas_call | solution.py:199
  54.2 12.6 %all-to-all-start.1 = ((f32[64,32,128]{2,1,0:T(8,128)}), f32[64,32,128]{2,1,0:T(8,128)S(1)}, u32[]{:S(2)}, u32[]{:S(2)}) async-start(f32[64,32,128]{2,1,0:T(8,128)} %bitcast.8), calls=%async_computation.1 | async-start | bytes 2097152 | tf_op jit(solution)/shard_map/all_to_all | solution.py:187
  66.9 0.0 copy-start.5
  66.9 0.6 copy-done.5
  67.5 0.0 copy-start.4
  67.5 0.7 copy-done.4
  68.2 26.8 %all-gather.1 = f32[8,2,96]{2,1,0:T(2,128)S(1)} all-gather(f32[1,2,96]{2,1,0:T(2,128)S(1)} %maximum_bitcast_fusion), channel_id=2, replica_groups=mesh['az'=64,'rad'=8] {'rad'}, dimensions={0}, use_global_device_ids=true | all-gather | bytes 6912 | tf_op jit(solution)/shard_map/all_gather | solution.py:211
  95.0 0.2 multiply_reduce_fusion
  95.2 0.1 select_reduce_fusion.1
  95.3 0.2 select_reduce_fusion
  95.5 0.1 broadcast_add_fusion
  95.6 0.1 add.37
  95.6 0.1 mul.25
  95.7 0.1 squeeze.8
  95.8 0.0 all-to-all-done.1
  95.8 9.2 %collective-permute-start = (f32[64,128]{1,0:T(8,128)S(1)}, f32[64,128]{1,0:T(8,128)S(1)}, u32[]{:S(2)}, u32[]{:S(2)}) collective-permute-start(f32[64,128]{1,0:T(8,128)S(1)} %bitcast.22), channel_id=1, source_target_pairs={{0,1},{1,2},{2,3},{3,4},{4,5},{5,6},{6,7},{8,9},{9,10},{10,11},{11... | collective-permute-start | bytes 98312 | tf_op jit(solution)/shard_map/ppermute | solution.py:227
  105.0 1.9 %collective-permute-start.1 = (f32[64,128]{1,0:T(8,128)S(1)}, f32[64,128]{1,0:T(8,128)S(1)}, u32[]{:S(2)}, u32[]{:S(2)}) collective-permute-start(f32[64,128]{1,0:T(8,128)S(1)} %bitcast.21), channel_id=1, source_target_pairs={{1,0},{2,1},{3,2},{4,3},{5,4},{6,5},{7,6},{9,8},{10,9},{11,10},{12... | collective-permute-start | bytes 98312 | tf_op jit(solution)/shard_map/ppermute | solution.py:228
  106.9 0.1 pad_dynamic-slice_fusion.pull
  107.0 0.6 dynamic_slice.7
  107.6 0.0 copy-start.2
  107.6 0.0 copy-start.3
  107.6 0.0 collective-permute-done.below
  107.6 2.6 %collective-permute-done.1.above = f32[64,128]{1,0:T(8,128)S(1)} collective-permute-done((f32[64,128]{1,0:T(8,128)S(1)}, f32[64,128]{1,0:T(8,128)S(1)}, u32[]{:S(2)}, u32[]{:S(2)}) %collective-permute-start.1) | collective-permute-done | bytes 32800 | tf_op jit(solution)/shard_map/ppermute | solution.py:228
  110.2 0.0 copy-done.2
  110.2 0.0 copy-done.3
  110.2 4.4 %spread.1 = f32[5,2,96,256]{3,2,1,0:T(8,128)} custom-call(f32[96]{0:T(128)S(1)} %copy-done.2, f32[96]{0:T(128)S(1)} %copy-done.3, f32[98]{0:T(128)S(1)} %pad_dynamic-slice_fusion.pull, f32[2048,128]{1,0:T(8,128)S(1)} %bitcast.19, f32[64,128]{1,0:T(8,128)S(1)} %collective-permute-done.below, f32[64,128]{1,0:T(8,128)S(1)} %collective-permute-done.1.above), custom_call_target="tpu_custom_call" | custom-call | tf_op jit(solution)/shard_map/spread/pallas_call | solution.py:229
  (6 shorter events, 0.0 us)
Async XLA Ops:
  0.6 1.2 %copy-start = (f32[5,2,96,256]{3,2,1,0:T(8,128)S(1)}, f32[5,2,96,256]{3,2,1,0:T(8,128)}, u32[]{:S(2)}) copy-start(f32[5,2,96,256]{3,2,1,0:T(8,128)} %fields.1) | copy-start | bytes 2949124
  3.8 45.4 %all-to-all-start = ((f32[64,32,128]{2,1,0:T(8,128)}), f32[64,32,128]{2,1,0:T(8,128)S(1)}, u32[]{:S(2)}, u32[]{:S(2)}) async-start(f32[64,32,128]{2,1,0:T(8,128)} %bitcast.1), calls=%async_computation | async-start | bytes 2097152 | tf_op jit(solution)/shard_map/all_to_all | solution.py:187
  49.1 0.7 copy-start.1
  54.2 41.6 %all-to-all-start.1 = ((f32[64,32,128]{2,1,0:T(8,128)}), f32[64,32,128]{2,1,0:T(8,128)S(1)}, u32[]{:S(2)}, u32[]{:S(2)}) async-start(f32[64,32,128]{2,1,0:T(8,128)} %bitcast.8), calls=%async_computation.1 | async-start | bytes 2097152 | tf_op jit(solution)/shard_map/all_to_all | solution.py:187
  66.9 0.7 copy-start.5
  67.5 0.7 copy-start.4
  95.8 11.8 %collective-permute-start = (f32[64,128]{1,0:T(8,128)S(1)}, f32[64,128]{1,0:T(8,128)S(1)}, u32[]{:S(2)}, u32[]{:S(2)}) collective-permute-start(f32[64,128]{1,0:T(8,128)S(1)} %bitcast.22), channel_id=1, source_target_pairs={{0,1},{1,2},{2,3},{3,4},{4,5},{5,6},{6,7},{8,9},{9,10},{10,11},{11... | collective-permute-start | bytes 98312 | tf_op jit(solution)/shard_map/ppermute | solution.py:227
  105.0 5.2 %collective-permute-start.1 = (f32[64,128]{1,0:T(8,128)S(1)}, f32[64,128]{1,0:T(8,128)S(1)}, u32[]{:S(2)}, u32[]{:S(2)}) collective-permute-start(f32[64,128]{1,0:T(8,128)S(1)} %bitcast.21), channel_id=1, source_target_pairs={{1,0},{2,1},{3,2},{4,3},{5,4},{6,5},{7,6},{9,8},{10,9},{11,10},{12... | collective-permute-start | bytes 98312 | tf_op jit(solution)/shard_map/ppermute | solution.py:228
  107.6 2.6 %copy-start.2 = (f32[96]{0:T(128)S(1)}, f32[96]{0:T(128)}, u32[]{:S(2)}) copy-start(f32[96]{0:T(128)} %kappa_az.1) | copy-start | bytes 1156
  107.6 2.6 %copy-start.3 = (f32[96]{0:T(128)S(1)}, f32[96]{0:T(128)}, u32[]{:S(2)}) copy-start(f32[96]{0:T(128)} %kappa_rad.1) | copy-start | bytes 1156

commit v2 on v1

--- a/solution.py
+++ b/solution.py
@@ -26,7 +26,15 @@
     return lane, line
 
 
-def pack_kernel(fields, packed):
+def windows():
+    for side in range(2):
+        for layer in range(2):
+            for half in range(2):
+                yield side, layer, half, BLOCK * (32 * side + 16 * layer + 8 * half) + 31
+
+
+def pack_kernel(fields, below, above, packed):
+    lane, line = iotas()
     for place, field in enumerate(ORDER):
         for layer in range(2):
             for group in range(GROUPS):
@@ -40,10 +48,18 @@
     square = jnp.concatenate([total, jnp.zeros((128 - ROWS, 128), jnp.float32)], axis=0)
     mass = jnp.sum(square.T, axis=0, keepdims=True)
     packed[pl.ds(15, RING, stride=BLOCK), :] = jnp.broadcast_to(mass, (RING, 128))
-    packed[pl.ds(31, RING, stride=BLOCK), :] = jnp.zeros((RING, 128), jnp.float32)
-
-
-def shift_kernel(place, shifts, lines, moved, mass):
+    for side, layer, half, first in windows():
+        tile = jnp.zeros((8, 128), jnp.float32)
+        for place, field in enumerate(ORDER):
+            cells = (below, above)[side][pl.ds(2 * field + layer, 1), pl.ds(128 * half, 128)]
+            turned = pltpu.roll(jnp.broadcast_to(cells, (8, 128)), 16 * (place + 1), 1)
+            for bit in (1, 2, 4):
+                turned = jnp.where(line & bit == 0, turned, pltpu.roll(turned, 128 - 16 * bit, 1))
+            tile = jnp.where(lane >> 4 == place + 1, turned, tile)
+        packed[pl.ds(first, 8, stride=BLOCK), :] = tile
+
+
+def shift_kernel(place, shifts, near, lines, moved, mass, twice):
     lane, line = iotas()
     row = place[0] >> 1
     whole, part, early = [], [], []
@@ -89,12 +105,20 @@
     _, edges = lax.fori_loop(0, RING, one, (before, (zero, zero)), unroll=4)
     square = jnp.concatenate([edges[0], edges[1], jnp.zeros((112, 128), jnp.float32)], axis=0).T
     moved[pl.ds(15, RING, stride=BLOCK), :] = square[:RING]
-    moved[pl.ds(31, RING, stride=BLOCK), :] = square[RING:]
+    ends = lines[pl.ds(31, RING, stride=BLOCK), :]
+    twice[pl.ds(0, RING), :] = ends
+    twice[pl.ds(RING, RING), :] = ends
+    shift = near[place[0] >> 5]
+    wide = lax.broadcasted_iota(jnp.int32, (RING, 128), 1)
+    crosses = (wide & 15) + 16 * (place[0] & 15) + (shift & 255) >= 256
+    blocks = shift >> 8
+    ends = jnp.where(crosses, twice[pl.ds(RING - 1 - blocks, RING), :], twice[pl.ds(RING - blocks, RING), :])
+    moved[pl.ds(31, RING, stride=BLOCK), :] = jnp.where(wide < 16, square[RING:], ends)
     parts = lines[pl.ds(15, RING, stride=BLOCK), :]
     mass[...] = jnp.broadcast_to(jnp.sum(parts, axis=0, keepdims=True), (8, 128))
 
 
-def spread_kernel(kappa_az, kappa_rad, pull, lines, below, above, updated, sourced, partial):
+def spread_kernel(near, kappa_az, kappa_rad, pull, lines, updated, sourced, partial, ends):
     lane, line = iotas()
     square = jnp.concatenate(
         [lines[pl.ds(15, RING, stride=BLOCK), :], lines[pl.ds(31, RING, stride=BLOCK), :]], axis=0
@@ -140,16 +164,31 @@
 
     lax.fori_loop(0, SPAN, one, 0, unroll=2)
 
-    for layer in range(2):
-        for half in range(2):
-            at = BLOCK * layer + HALF * half
-            under = source(below[pl.ds(at + 8, 8), :], jnp.where(takes[1][1], pull[0], 0.0))
-            over = source(above[pl.ds(at, 8), :], jnp.where(takes[0][0], pull[ROWS + 1], 0.0))
-            sourced[pl.ds(at, 5), :] = under[2:7]
-            sourced[pl.ds(at + 5, 10), :] = sourced[pl.ds(RING * BLOCK + at, 10), :]
-            top = (RING + 2) * BLOCK + at
-            sourced[pl.ds(top, 10), :] = sourced[pl.ds(2 * BLOCK + at + 5, 10), :]
-            sourced[pl.ds(top + 10, 5), :] = over[0:5]
+    ends[...] = jnp.zeros(ends.shape, jnp.float32)
+    for side, layer, half, first in windows():
+        tile = lines[pl.ds(first, 8, stride=BLOCK), :]
+        for place in range(5):
+            turned = pltpu.roll(pltpu.roll(tile, 112 - 16 * place, 1), 0, 1, stride=16, stride_axis=0)
+            cells = jnp.sum(jnp.where(lane >> 4 == line, turned, 0.0), axis=0, keepdims=True)
+            ends[pl.ds(8 * (4 * side + 2 * layer + half) + place, 1), :] = cells
+    for side in range(2):
+        part, odd = near[side] & 127, near[side] & 128
+        rate = jnp.where(takes[0][0], pull[(ROWS + 1) * side], 0.0)
+        for layer in range(2):
+            at = 8 * (4 * side + 2 * layer)
+            low = pltpu.roll(ends[pl.ds(at, 8), :], part, 1)
+            high = pltpu.roll(ends[pl.ds(at + 8, 8), :], part, 1)
+            even = jnp.where(lane < part, high, low), jnp.where(lane < part, low, high)
+            for half in range(2):
+                row = BLOCK * layer + HALF * half
+                full = source(jnp.where(odd == 0, even[half], even[1 - half]), rate)
+                if side == 0:
+                    sourced[pl.ds(row, 5), :] = full[0:5]
+                    sourced[pl.ds(row + 5, 10), :] = sourced[pl.ds(RING * BLOCK + row, 10), :]
+                else:
+                    top = (RING + 2) * BLOCK + row
+                    sourced[pl.ds(top, 10), :] = sourced[pl.ds(2 * BLOCK + row + 5, 10), :]
+                    sourced[pl.ds(top + 10, 5), :] = full[0:5]
 
     def two(row, carry):
         for tile in range(2):
@@ -186,30 +225,36 @@
         lines = lines.reshape(RING, BLOCK, 128)
         return lax.all_to_all(lines, "az", 0, 0, tiled=True).reshape(RING * BLOCK, 128)
 
+    ranks = lax.axis_size("rad")
+    up = [(i, i + 1) for i in range(ranks - 1)]
+    down = [(i + 1, i) for i in range(ranks - 1)]
+    below = lax.ppermute(fields[:, :, ROWS - 1, :].reshape(10, 256), "rad", up)
+    above = lax.ppermute(fields[:, :, 0, :].reshape(10, 256), "rad", down)
     packed = pl.pallas_call(
         pack_kernel,
         out_shape=blocks,
-        in_specs=specs(vmem),
+        in_specs=specs(vmem, vmem, vmem),
         out_specs=specs(vmem)[0],
         compiler_params=params,
         name="pack",
-    )(fields)
+    )(fields, below, above)
+    near = jnp.concatenate([lax.ppermute(shifts[ROWS - 1 :], "rad", up), lax.ppermute(shifts[:1], "rad", down)])
     whole = dealt(packed)
     place = lax.axis_index("az").astype(jnp.int32)[None]
     moved, mass = pl.pallas_call(
         shift_kernel,
         out_shape=(blocks, jax.ShapeDtypeStruct((8, 128), jnp.float32)),
-        in_specs=specs(smem, smem, vmem),
+        in_specs=specs(smem, smem, smem, vmem),
         out_specs=specs(vmem, vmem),
+        scratch_shapes=[pltpu.VMEM((2 * RING, 128), jnp.float32)],
         compiler_params=params,
         name="shift",
-    )(place, shifts, whole)
+    )(place, shifts, near, whole)
     lines = dealt(moved)
 
     row_mass = cycle_area * mass[0, :ROWS] / (2.0 * RING * 256)
     mine = jnp.stack([row_mass, gravity])
     everyone = lax.all_gather(mine, "rad")
-    ranks = everyone.shape[0]
     masses = everyone[:, 0, :]
     totals = jnp.sum(masses, axis=1)
     rank = jnp.arange(ranks)
@@ -222,22 +267,19 @@
     pull = lax.dynamic_slice(jnp.pad(pulls, (1, 1)), (me * ROWS,), (ROWS + 2,))
     enclosed = lax.dynamic_slice(reach.reshape(ranks * ROWS), (me * ROWS,), (ROWS,))
 
-    up = [(i, i + 1) for i in range(ranks - 1)]
-    down = [(i + 1, i) for i in range(ranks - 1)]
-    below = lax.ppermute(lines[(RING - 2) * BLOCK :], "rad", up)
-    above = lax.ppermute(lines[: 2 * BLOCK], "rad", down)
     updated = pl.pallas_call(
         spread_kernel,
         out_shape=jax.ShapeDtypeStruct(fields.shape, jnp.float32),
-        in_specs=specs(smem, smem, smem, vmem, vmem, vmem),
+        in_specs=specs(smem, smem, smem, smem, vmem),
         out_specs=specs(vmem)[0],
         scratch_shapes=[
             pltpu.VMEM(((RING + 4) * BLOCK, 128), jnp.float32),
             pltpu.VMEM((RING * BLOCK, 128), jnp.float32),
+            pltpu.VMEM((64, 128), jnp.float32),
         ],
         compiler_params=params,
         name="spread",
-    )(kappa_az, kappa_rad, pull, lines, below, above)
+    )(near, kappa_az, kappa_rad, pull, lines)
     return updated, enclosed
 
 

time: 115 us -> 114 us (level)
  the two profiles are of different devices: /device:TPU:1 before, /device:TPU:16 now
where the time goes in v2:
time: 114 us; the launch traced here: 113 us
  waiting for transfers between devices  40.6 us (36%)
  starting transfers between devices  33.5 us (29%)
  blocking collectives  20.2 us (18%)
  Pallas kernels  11.3 us (10%)
  local copies, waits for them, and re-layouts  5 us (4%)
  other arithmetic  1.85 us (2%)
    all_to_all x2, waiting for transfers between devices, dealt(): lax.all_to_all(lines, 'az', 0, 0, tiled=True).reshape(RING * BLOCK, 128)  37.8 us
    all_to_all x2, starting transfers between devices, dealt(): lax.all_to_all(lines, 'az', 0, 0, tiled=True).reshape(RING * BLOCK, 128)  22.4 us
    all_gather x1, blocking collectives, shards(): everyone = lax.all_gather(mine, 'rad')  20.2 us
    pallas_call x1, Pallas kernels, shards(): pl.pallas_call(spread_kernel, out_shape=jax.ShapeDtypeStruct(fields.shape...  4.66 us
    pallas_call x1, Pallas kernels, shards(): pl.pallas_call(shift_kernel, out_shape=(blocks, jax.ShapeDtypeStruct((8,...  4.45 us
    ppermute x1, starting transfers between devices, shards(): above = lax.ppermute(fields[:, :, 0, :].reshape(10, 256), 'rad', down)  3.64 us
    ppermute x1, starting transfers between devices, shards(): lax.ppermute(shifts[:1], 'rad', down)  3.17 us
    unnamed x12, local copies, waits for them, and re-layouts  2.52 us
  transfers between devices with their start and end apart: 6, of which 4 were waited for; matrix products, arithmetic and copies ran while one was open for 3% of the time, Pallas kernels for 0%

profile of v2, /device:TPU:16, one launch (start us, length us, event | category | flops | bytes accessed | tf_op | source)
XLA Modules:
  0.0 113.3 jit_solution(4269712692800390755)
XLA Ops:
  0.6 1.0 slice_reduce_fusion
  1.6 1.9 %collective-permute-start.2 = (f32[10,256]{1,0:T(8,128)S(1)}, f32[10,256]{1,0:T(8,128)S(1)}, u32[]{:S(2)}, u32[]{:S(2)}) collective-permute-start(f32[10,256]{1,0:T(8,128)S(1)} %reshape_squeeze.6), channel_id=1, source_target_pairs={{0,1},{1,2},{2,3},{3,4},{4,5},{5,6},{6,7},{8,9},{9,10},{10,11},{11... | collective-permute-start | bytes 30728 | tf_op jit(solution)/shard_map/ppermute | solution.py:231
  3.6 3.6 %collective-permute-start.3 = (f32[10,256]{1,0:T(8,128)S(1)}, f32[10,256]{1,0:T(8,128)S(1)}, u32[]{:S(2)}, u32[]{:S(2)}) collective-permute-start(f32[10,256]{1,0:T(8,128)S(1)} %reshape_squeeze.7), channel_id=1, source_target_pairs={{1,0},{2,1},{3,2},{4,3},{5,4},{6,5},{7,6},{9,8},{10,9},{11,10},{12... | collective-permute-start | bytes 30728 | tf_op jit(solution)/shard_map/ppermute | solution.py:232
  7.2 0.0 collective-permute-done.2.below
  7.2 1.4 %collective-permute-done.3.above = f32[10,256]{1,0:T(8,128)S(1)} collective-permute-done((f32[10,256]{1,0:T(8,128)S(1)}, f32[10,256]{1,0:T(8,128)S(1)}, u32[]{:S(2)}, u32[]{:S(2)}) %collective-permute-start.3) | collective-permute-done | bytes 10272 | tf_op jit(solution)/shard_map/ppermute | solution.py:232
  8.7 0.0 copy-start
  8.7 1.2 %copy-done = f32[5,2,96,256]{3,2,1,0:T(8,128)S(1)} copy-done((f32[5,2,96,256]{3,2,1,0:T(8,128)S(1)}, f32[5,2,96,256]{3,2,1,0:T(8,128)}, u32[]{:S(2)}) %copy-start) | copy-done | bytes 983064
  9.9 2.2 %pack.1 = f32[2048,128]{1,0:T(8,128)} custom-call(f32[5,2,96,256]{3,2,1,0:T(8,128)S(1)} %copy-done, f32[10,256]{1,0:T(8,128)S(1)} %collective-permute-done.2.below, f32[10,256]{1,0:T(8,128)S(1)} %collective-permute-done.3.above), custom_call_target="tpu_custom_call" | custom-call | tf_op jit(solution)/shard_map/pack/pallas_call | solution.py:233
  12.1 0.0 copy-start.1
  12.1 17.4 %all-to-all-start = ((f32[64,32,128]{2,1,0:T(8,128)}), f32[64,32,128]{2,1,0:T(8,128)S(1)}, u32[]{:S(2)}, u32[]{:S(2)}) async-start(f32[64,32,128]{2,1,0:T(8,128)} %bitcast.1), calls=%async_computation | async-start | bytes 2097152 | tf_op jit(solution)/shard_map/all_to_all | solution.py:226
  29.5 0.0 copy-done.1
  29.5 0.6 fusion.3
  30.1 2.4 %collective-permute-start = (s32[1]{0:T(128)}, s32[1]{0:T(128)}, u32[]{:S(2)}, u32[]{:S(2)}) collective-permute-start(s32[1]{0:T(128)} %get-tuple-element.14), channel_id=1, source_target_pairs={{0,1},{1,2},{2,3},{3,4},{4,5},{5,6},{6,7},{8,9},{9,10},{10,11},{11... | collective-permute-start | bytes 20 | tf_op jit(solution)/shard_map/ppermute | solution.py:241
  32.5 3.2 %collective-permute-start.1 = (s32[1]{0:T(128)}, s32[1]{0:T(128)}, u32[]{:S(2)}, u32[]{:S(2)}) collective-permute-start(s32[1]{0:T(128)} %get-tuple-element.15), channel_id=1, source_target_pairs={{1,0},{2,1},{3,2},{4,3},{5,4},{6,5},{7,6},{9,8},{10,9},{11,10},{12... | collective-permute-start | bytes 20 | tf_op jit(solution)/shard_map/ppermute | solution.py:241
  35.7 0.0 collective-permute-done
  35.7 1.4 %collective-permute-done.1 = s32[1]{0:T(128)} collective-permute-done((s32[1]{0:T(128)}, s32[1]{0:T(128)}, u32[]{:S(2)}, u32[]{:S(2)}) %collective-permute-start.1) | collective-permute-done | bytes 36 | tf_op jit(solution)/shard_map/ppermute | solution.py:241
  37.1 1.3 %pad_add_fusion.near = s32[2]{0:T(128)S(1)} fusion(s32[1]{0:T(128)} %collective-permute-done.1, s32[1]{0:T(128)} %collective-permute-done), kind=kLoop, calls=%fused_computation.11 | loop fusion | flops 2 | bytes 16 | tf_op jit(solution)/shard_map/concatenate | solution.py:241
  38.3 26.7 %all-to-all-done = f32[64,32,128]{2,1,0:T(8,128)S(1)} async-done(((f32[64,32,128]{2,1,0:T(8,128)}), f32[64,32,128]{2,1,0:T(8,128)S(1)}, u32[]{:S(2)}, u32[]{:S(2)}) %all-to-all-start) | async-done | bytes 1048608 | tf_op jit(solution)/shard_map/all_to_all | solution.py:226
  65.0 4.5 %shift.1 = (f32[2048,128]{1,0:T(8,128)}, f32[8,128]{1,0:T(8,128)S(1)}) custom-call(s32[1]{0:T(128)} %bitcast.place, s32[96]{0:T(128)S(1)} %copy-done.1, s32[2]{0:T(128)S(1)} %pad_add_fusion.near, f32[2048,128]{1,0:T(8,128)S(1)} %bitcast.18), custom_call_target="tpu_custom_call" | custom-call | tf_op jit(solution)/shard_map/shift/pallas_call | solution.py:244
  69.5 5.1 %all-to-all-start.1 = ((f32[64,32,128]{2,1,0:T(8,128)}), f32[64,32,128]{2,1,0:T(8,128)S(1)}, u32[]{:S(2)}, u32[]{:S(2)}) async-start(f32[64,32,128]{2,1,0:T(8,128)} %bitcast.8), calls=%async_computation.1 | async-start | bytes 2097152 | tf_op jit(solution)/shard_map/all_to_all | solution.py:226
  74.6 0.0 copy-start.5
  74.6 0.6 copy-done.5
  75.2 0.0 copy-start.4
  75.2 0.7 copy-done.4
  75.9 20.2 %all-gather.1 = f32[8,2,96]{2,1,0:T(2,128)S(1)} all-gather(f32[1,2,96]{2,1,0:T(2,128)S(1)} %maximum_bitcast_fusion), channel_id=2, replica_groups=mesh['az'=64,'rad'=8] {'rad'}, dimensions={0}, use_global_device_ids=true | all-gather | bytes 6912 | tf_op jit(solution)/shard_map/all_gather | solution.py:257
  96.0 0.2 multiply_reduce_fusion
  96.2 0.1 select_reduce_fusion.1
  96.3 0.2 select_reduce_fusion
  96.5 0.1 broadcast_add_fusion
  96.6 0.1 add.37
  96.7 0.1 mul.25
  96.8 0.1 squeeze.8
  96.8 0.6 dynamic_slice.7
  97.4 0.1 pad_dynamic-slice_fusion.pull
  97.5 0.0 copy-start.2
  97.5 0.0 copy-start.3
  97.5 11.1 %all-to-all-done.1 = f32[64,32,128]{2,1,0:T(8,128)S(1)} async-done(((f32[64,32,128]{2,1,0:T(8,128)}), f32[64,32,128]{2,1,0:T(8,128)S(1)}, u32[]{:S(2)}, u32[]{:S(2)}) %all-to-all-start.1) | async-done | bytes 1048608 | tf_op jit(solution)/shard_map/all_to_all | solution.py:226
  108.6 0.0 copy-done.2
  108.6 0.0 copy-done.3
  108.6 4.7 %spread.1 = f32[5,2,96,256]{3,2,1,0:T(8,128)} custom-call(s32[2]{0:T(128)S(1)} %pad_add_fusion.near, f32[96]{0:T(128)S(1)} %copy-done.2, f32[96]{0:T(128)S(1)} %copy-done.3, f32[98]{0:T(128)S(1)} %pad_dynamic-slice_fusion.pull, f32[2048,128]{1,0:T(8,128)S(1)} %bitcast.17), custom_call_target="tpu_custom_call" | custom-call | tf_op jit(solution)/shard_map/spread/pallas_call | solution.py:270
  (7 shorter events, 0.1 us)
Async XLA Ops:
  1.6 5.6 %collective-permute-start.2 = (f32[10,256]{1,0:T(8,128)S(1)}, f32[10,256]{1,0:T(8,128)S(1)}, u32[]{:S(2)}, u32[]{:S(2)}) collective-permute-start(f32[10,256]{1,0:T(8,128)S(1)} %reshape_squeeze.6), channel_id=1, source_target_pairs={{0,1},{1,2},{2,3},{3,4},{4,5},{5,6},{6,7},{8,9},{9,10},{10,11},{11... | collective-permute-start | bytes 30728 | tf_op jit(solution)/shard_map/ppermute | solution.py:231
  3.6 5.1 %collective-permute-start.3 = (f32[10,256]{1,0:T(8,128)S(1)}, f32[10,256]{1,0:T(8,128)S(1)}, u32[]{:S(2)}, u32[]{:S(2)}) collective-permute-start(f32[10,256]{1,0:T(8,128)S(1)} %reshape_squeeze.7), channel_id=1, source_target_pairs={{1,0},{2,1},{3,2},{4,3},{5,4},{6,5},{7,6},{9,8},{10,9},{11,10},{12... | collective-permute-start | bytes 30728 | tf_op jit(solution)/shard_map/ppermute | solution.py:232
  8.7 1.2 %copy-start = (f32[5,2,96,256]{3,2,1,0:T(8,128)S(1)}, f32[5,2,96,256]{3,2,1,0:T(8,128)}, u32[]{:S(2)}) copy-start(f32[5,2,96,256]{3,2,1,0:T(8,128)} %fields.1) | copy-start | bytes 2949124
  12.1 17.4 %copy-start.1 = (s32[96]{0:T(128)S(1)}, s32[96]{0:T(128)}, u32[]{:S(2)}) copy-start(s32[96]{0:T(128)} %shifts.1) | copy-start | bytes 1156
  12.1 52.9 %all-to-all-start = ((f32[64,32,128]{2,1,0:T(8,128)}), f32[64,32,128]{2,1,0:T(8,128)S(1)}, u32[]{:S(2)}, u32[]{:S(2)}) async-start(f32[64,32,128]{2,1,0:T(8,128)} %bitcast.1), calls=%async_computation | async-start | bytes 2097152 | tf_op jit(solution)/shard_map/all_to_all | solution.py:226
  30.1 5.6 %collective-permute-start = (s32[1]{0:T(128)}, s32[1]{0:T(128)}, u32[]{:S(2)}, u32[]{:S(2)}) collective-permute-start(s32[1]{0:T(128)} %get-tuple-element.14), channel_id=1, source_target_pairs={{0,1},{1,2},{2,3},{3,4},{4,5},{5,6},{6,7},{8,9},{9,10},{10,11},{11... | collective-permute-start | bytes 20 | tf_op jit(solution)/shard_map/ppermute | solution.py:241
  32.5 4.6 %collective-permute-start.1 = (s32[1]{0:T(128)}, s32[1]{0:T(128)}, u32[]{:S(2)}, u32[]{:S(2)}) collective-permute-start(s32[1]{0:T(128)} %get-tuple-element.15), channel_id=1, source_target_pairs={{1,0},{2,1},{3,2},{4,3},{5,4},{6,5},{7,6},{9,8},{10,9},{11,10},{12... | collective-permute-start | bytes 20 | tf_op jit(solution)/shard_map/ppermute | solution.py:241
  69.5 39.1 %all-to-all-start.1 = ((f32[64,32,128]{2,1,0:T(8,128)}), f32[64,32,128]{2,1,0:T(8,128)S(1)}, u32[]{:S(2)}, u32[]{:S(2)}) async-start(f32[64,32,128]{2,1,0:T(8,128)} %bitcast.8), calls=%async_computation.1 | async-start | bytes 2097152 | tf_op jit(solution)/shard_map/all_to_all | solution.py:226
  74.6 0.7 copy-start.5
  75.2 0.7 copy-start.4
  97.5 11.1 %copy-start.2 = (f32[96]{0:T(128)S(1)}, f32[96]{0:T(128)}, u32[]{:S(2)}) copy-start(f32[96]{0:T(128)} %kappa_az.1) | copy-start | bytes 1156
  97.5 11.1 %copy-start.3 = (f32[96]{0:T(128)S(1)}, f32[96]{0:T(128)}, u32[]{:S(2)}) copy-start(f32[96]{0:T(128)} %kappa_rad.1) | copy-start | bytes 1156

commit v3 on v2

--- a/solution.py
+++ b/solution.py
@@ -3,9 +3,10 @@
 from jax import lax
 from jax.experimental import pallas as pl
 from jax.experimental.pallas import tpu as pltpu
-from jax.sharding import PartitionSpec as P
+from jax.sharding import Mesh, PartitionSpec as P
 
 star_mass = 1.0
+RAD = ("chip", "core")
 
 ORDER = (0, 1, 3, 2, 4)
 RING = 64
@@ -33,12 +34,17 @@
                 yield side, layer, half, BLOCK * (32 * side + 16 * layer + 8 * half) + 31
 
 
-def pack_kernel(fields, below, above, packed):
-    lane, line = iotas()
+def late(half, line):
+    return half == 1 and line >= 8
+
+
+def pack_kernel(fields, packed):
     for place, field in enumerate(ORDER):
         for layer in range(2):
             for group in range(GROUPS):
                 for half in range(2):
+                    if late(half, 5 * group + place):
+                        continue
                     first = BLOCK * layer + HALF * half + 5 * group + place
                     packed[pl.ds(first, SPAN, stride=2 * BLOCK), :] = fields[
                         field, layer, pl.ds(SPAN * group, SPAN), pl.ds(128 * half, 128)
@@ -48,6 +54,17 @@
     square = jnp.concatenate([total, jnp.zeros((128 - ROWS, 128), jnp.float32)], axis=0)
     mass = jnp.sum(square.T, axis=0, keepdims=True)
     packed[pl.ds(15, RING, stride=BLOCK), :] = jnp.broadcast_to(mass, (RING, 128))
+
+
+def finish_kernel(fields, below, above, begun, packed, rows, sem):
+    lane, line = iotas()
+    for place, field in enumerate(ORDER):
+        for layer in range(2):
+            for group in range(GROUPS):
+                if late(1, 5 * group + place):
+                    rows[pl.ds(8 * layer + 5 * group + place - 8, SPAN, stride=16), :] = fields[
+                        field, layer, pl.ds(SPAN * group, SPAN), pl.ds(128, 128)
+                    ]
     for side, layer, half, first in windows():
         tile = jnp.zeros((8, 128), jnp.float32)
         for place, field in enumerate(ORDER):
@@ -56,7 +73,10 @@
             for bit in (1, 2, 4):
                 turned = jnp.where(line & bit == 0, turned, pltpu.roll(turned, 128 - 16 * bit, 1))
             tile = jnp.where(lane >> 4 == place + 1, turned, tile)
-        packed[pl.ds(first, 8, stride=BLOCK), :] = tile
+        rows[pl.ds(first // BLOCK * 8 + 7, 8, stride=8), :] = tile
+    copy = pltpu.make_async_copy(rows.reshape(RING, 8, 128), packed.at[:, pl.ds(24, 8), :], sem)
+    copy.start()
+    copy.wait()
 
 
 def shift_kernel(place, shifts, near, lines, moved, mass, twice):
@@ -225,20 +245,33 @@
         lines = lines.reshape(RING, BLOCK, 128)
         return lax.all_to_all(lines, "az", 0, 0, tiled=True).reshape(RING * BLOCK, 128)
 
-    ranks = lax.axis_size("rad")
-    up = [(i, i + 1) for i in range(ranks - 1)]
-    down = [(i + 1, i) for i in range(ranks - 1)]
-    below = lax.ppermute(fields[:, :, ROWS - 1, :].reshape(10, 256), "rad", up)
-    above = lax.ppermute(fields[:, :, 0, :].reshape(10, 256), "rad", down)
-    packed = pl.pallas_call(
+    ranks = lax.axis_size(RAD)
+
+    def message(row):
+        cells = fields[:, :, row, :].reshape(10, 256)
+        return jnp.concatenate([cells, jnp.full((6, 256), shifts[row].astype(jnp.float32))])
+
+    below = lax.ppermute(message(ROWS - 1), RAD, [(i, i + 1) for i in range(ranks - 1)])
+    above = lax.ppermute(message(0), RAD, [(i + 1, i) for i in range(ranks - 1)])
+    begun = pl.pallas_call(
         pack_kernel,
         out_shape=blocks,
-        in_specs=specs(vmem, vmem, vmem),
+        in_specs=specs(vmem),
         out_specs=specs(vmem)[0],
         compiler_params=params,
         name="pack",
-    )(fields, below, above)
-    near = jnp.concatenate([lax.ppermute(shifts[ROWS - 1 :], "rad", up), lax.ppermute(shifts[:1], "rad", down)])
+    )(fields)
+    packed = pl.pallas_call(
+        finish_kernel,
+        out_shape=jax.ShapeDtypeStruct((RING, BLOCK, 128), jnp.float32),
+        in_specs=specs(vmem, vmem, vmem, pl.ANY),
+        out_specs=specs(pl.ANY)[0],
+        scratch_shapes=[pltpu.VMEM((RING * 8, 128), jnp.float32), pltpu.SemaphoreType.DMA],
+        input_output_aliases={3: 0},
+        compiler_params=params,
+        name="finish",
+    )(fields, below, above, begun.reshape(RING, BLOCK, 128))
+    near = jnp.stack([below[10, 0], above[10, 0]]).astype(jnp.int32)
     whole = dealt(packed)
     place = lax.axis_index("az").astype(jnp.int32)[None]
     moved, mass = pl.pallas_call(
@@ -254,7 +287,7 @@
 
     row_mass = cycle_area * mass[0, :ROWS] / (2.0 * RING * 256)
     mine = jnp.stack([row_mass, gravity])
-    everyone = lax.all_gather(mine, "rad")
+    everyone = lax.all_gather(lax.all_gather(mine, "core"), "chip").reshape(ranks, 2, ROWS)
     masses = everyone[:, 0, :]
     totals = jnp.sum(masses, axis=1)
     rank = jnp.arange(ranks)
@@ -263,7 +296,7 @@
     before = jnp.sum(jnp.where(row[None, None, :] < row[None, :, None], masses[:, None, :], 0.0), axis=2)
     reach = star_mass + offset[:, None] + before + 0.5 * masses
     pulls = (everyone[:, 1, :] * reach).reshape(ranks * ROWS)
-    me = lax.axis_index("rad")
+    me = lax.axis_index(RAD)
     pull = lax.dynamic_slice(jnp.pad(pulls, (1, 1)), (me * ROWS,), (ROWS + 2,))
     enclosed = lax.dynamic_slice(reach.reshape(ranks * ROWS), (me * ROWS,), (ROWS,))
 
@@ -284,11 +317,12 @@
 
 
 def solution(mesh):
-    placed = (P(None, None, "rad", "az"), P("rad"), P("rad"), P("rad"), P("rad"), P("rad"))
+    split = Mesh(mesh.devices.reshape(mesh.shape["az"], -1, 2), ("az",) + RAD)
+    placed = (P(None, None, RAD, "az"), P(RAD), P(RAD), P(RAD), P(RAD), P(RAD))
     return jax.shard_map(
         shards,
-        mesh=mesh,
+        mesh=split,
         in_specs=placed,
-        out_specs=(P(None, None, "rad", "az"), P("rad")),
+        out_specs=(P(None, None, RAD, "az"), P(RAD)),
         check_vma=False,
     )

time: 114 us -> 114 us (level)
  the two profiles are of different devices: /device:TPU:16 before, /device:TPU:8 now
where the time goes in v3:
time: 114 us; the launch traced here: 113 us
  waiting for transfers between devices  34.9 us (31%)
  starting transfers between devices  28.7 us (25%)
  blocking collectives  27.1 us (24%)
  Pallas kernels  11.9 us (10%)
  local copies, waits for them, and re-layouts  6.66 us (6%)
  between operations  2.07 us (2%)
  other arithmetic  1.95 us (2%)
    all_to_all x2, waiting for transfers between devices, dealt(): lax.all_to_all(lines, 'az', 0, 0, tiled=True).reshape(RING * BLOCK, 128)  34.9 us
    all_gather x1, blocking collectives, shards(): lax.all_gather(lax.all_gather(mine, 'core'), 'chip').reshape(ranks, 2, ROWS)  25.3 us
    all_to_all x2, starting transfers between devices, dealt(): lax.all_to_all(lines, 'az', 0, 0, tiled=True).reshape(RING * BLOCK, 128)  23.1 us
    pallas_call x1, Pallas kernels, shards(): pl.pallas_call(spread_kernel, out_shape=jax.ShapeDtypeStruct(fields.shape...  4.66 us
    pallas_call x1, Pallas kernels, shards(): pl.pallas_call(shift_kernel, out_shape=(blocks, jax.ShapeDtypeStruct((8,...  4.45 us
    ppermute x1, starting transfers between devices, shards(): lax.ppermute(message(0), RAD, [(i + 1, i) for i in range(ranks - 1)])  3.64 us
    unnamed x12, local copies, waits for them, and re-layouts  3.14 us
  transfers between devices with their start and end apart: 4, of which 2 were waited for; matrix products, arithmetic and copies ran while one was open for 3% of the time, Pallas kernels for 2%

profile of v3, /device:TPU:8, one launch (start us, length us, event | category | flops | bytes accessed | tf_op | source)
XLA Modules:
  0.0 113.3 jit_solution(15144788775063062577)
XLA Ops:
  0.6 1.0 slice_reduce_fusion.1
  1.6 0.0 copy-start.1
  1.7 0.6 copy-done.1
  2.3 0.6 fusion.3
  3.5 1.9 %collective-permute-start = (f32[16,256]{1,0:T(8,128)S(1)}, f32[16,256]{1,0:T(8,128)S(1)}, u32[]{:S(2)}, u32[]{:S(2)}) collective-permute-start(f32[16,256]{1,0:T(8,128)S(1)} %concatenate.6), channel_id=1, source_target_pairs={{0,1},{1,2},{2,3},{3,4},{4,5},{5,6},{6,7},{8,9},{9,10},{10,11},{11... | collective-permute-start | bytes 49160 | tf_op jit(solution)/shard_map/ppermute | solution.py:254
  6.1 3.6 %collective-permute-start.1 = (f32[16,256]{1,0:T(8,128)S(1)}, f32[16,256]{1,0:T(8,128)S(1)}, u32[]{:S(2)}, u32[]{:S(2)}) collective-permute-start(f32[16,256]{1,0:T(8,128)S(1)} %concatenate.7), channel_id=1, source_target_pairs={{1,0},{2,1},{3,2},{4,3},{5,4},{6,5},{7,6},{9,8},{10,9},{11,10},{12... | collective-permute-start | bytes 49160 | tf_op jit(solution)/shard_map/ppermute | solution.py:255
  9.8 0.0 copy-start
  9.8 1.2 %copy-done = f32[5,2,96,256]{3,2,1,0:T(8,128)S(1)} copy-done((f32[5,2,96,256]{3,2,1,0:T(8,128)S(1)}, f32[5,2,96,256]{3,2,1,0:T(8,128)}, u32[]{:S(2)}) %copy-start) | copy-done | bytes 983064
  11.0 1.7 %pack.1 = f32[2048,128]{1,0:T(8,128)} custom-call(f32[5,2,96,256]{3,2,1,0:T(8,128)S(1)} %copy-done), custom_call_target="tpu_custom_call" | custom-call | tf_op jit(solution)/shard_map/pack/pallas_call | solution.py:256
  12.7 0.0 collective-permute-done.below
  12.7 0.0 collective-permute-done.1.above
  12.7 1.1 finish.1
  13.8 18.2 %all-to-all-start = ((f32[64,32,128]{2,1,0:T(8,128)}), f32[64,32,128]{2,1,0:T(8,128)S(1)}, u32[]{:S(2)}, u32[]{:S(2)}) async-start(f32[64,32,128]{2,1,0:T(8,128)} %finish.1), calls=%async_computation | async-start | bytes 2097152 | tf_op jit(solution)/shard_map/all_to_all | solution.py:246
  32.0 0.5 slice.36
  32.5 0.5 slice.37
  33.0 1.4 %maximum_convert_fusion.near = s32[2]{0:T(128)S(1)} fusion(f32[1]{0:T(128)} %bitcast.3, f32[1]{0:T(128)} %bitcast.1), kind=kLoop, calls=%fused_computation.11 | loop fusion | flops 4 | bytes 16 | tf_op jit(solution)/shard_map/convert_element_type | solution.py:274
  34.4 31.5 %all-to-all-done = f32[64,32,128]{2,1,0:T(8,128)S(1)} async-done(((f32[64,32,128]{2,1,0:T(8,128)}), f32[64,32,128]{2,1,0:T(8,128)S(1)}, u32[]{:S(2)}, u32[]{:S(2)}) %all-to-all-start) | async-done | bytes 1048608 | tf_op jit(solution)/shard_map/all_to_all | solution.py:246
  65.9 4.5 %shift.1 = (f32[2048,128]{1,0:T(8,128)}, f32[8,128]{1,0:T(8,128)S(1)}) custom-call(s32[1]{0:T(128)} %bitcast.4.place, s32[96]{0:T(128)S(1)} %copy-done.1, s32[2]{0:T(128)S(1)} %maximum_convert_fusion.near, f32[2048,128]{1,0:T(8,128)S(1)} %bitcast.22), custom_call_target="tpu_custom_call" | custom-call | tf_op jit(solution)/shard_map/shift/pallas_call | solution.py:277
  70.4 4.9 %all-to-all-start.1 = ((f32[64,32,128]{2,1,0:T(8,128)}), f32[64,32,128]{2,1,0:T(8,128)S(1)}, u32[]{:S(2)}, u32[]{:S(2)}) async-start(f32[64,32,128]{2,1,0:T(8,128)} %bitcast.12), calls=%async_computation.1 | async-start | bytes 2097152 | tf_op jit(solution)/shard_map/all_to_all | solution.py:246
  75.3 0.0 copy-start.5
  75.4 0.6 copy-done.5
  76.0 0.0 copy-start.4
  76.0 0.7 copy-done.4
  76.7 1.8 %all-gather.2 = f32[2,2,96]{2,1,0:T(2,128)S(1)} all-gather(f32[1,2,96]{2,1,0:T(2,128)S(1)} %maximum_bitcast_fusion), channel_id=2, replica_groups=mesh['az'=64,'chip'=4,'core'=2] {'core'}, dimensions={0}, use_global_device_ids=true | all-gather | bytes 2304 | tf_op jit(solution)/shard_map/all_gather | solution.py:290
  78.4 25.3 %all-gather.1 = f32[8,2,96]{2,1,0:T(2,128)S(1)} all-gather(f32[2,2,96]{2,1,0:T(2,128)S(1)} %all-gather.2), channel_id=3, replica_groups=mesh['az'=64,'chip'=4,'core'=2] {'chip'}, dimensions={0}, use_global_device_ids=true | all-gather | bytes 7680 | tf_op jit(solution)/shard_map/all_gather | solution.py:290
  103.7 0.2 multiply_reduce_fusion
  103.9 0.1 select_reduce_fusion.1
  104.0 0.2 select_reduce_fusion
  104.2 0.1 broadcast_add_fusion
  104.3 0.1 add.44
  104.4 0.1 mul.28
  104.5 0.1 squeeze.10
  104.5 0.6 dynamic_slice.7
  105.1 0.1 pad_dynamic-slice_fusion.pull
  105.2 0.0 copy-start.2
  105.2 0.0 copy-start.3
  105.2 3.4 %all-to-all-done.1 = f32[64,32,128]{2,1,0:T(8,128)S(1)} async-done(((f32[64,32,128]{2,1,0:T(8,128)}), f32[64,32,128]{2,1,0:T(8,128)S(1)}, u32[]{:S(2)}, u32[]{:S(2)}) %all-to-all-start.1) | async-done | bytes 1048608 | tf_op jit(solution)/shard_map/all_to_all | solution.py:246
  108.6 0.0 copy-done.2
  108.6 0.0 copy-done.3
  108.6 4.7 %spread.1 = f32[5,2,96,256]{3,2,1,0:T(8,128)} custom-call(s32[2]{0:T(128)S(1)} %maximum_convert_fusion.near, f32[96]{0:T(128)S(1)} %copy-done.2, f32[96]{0:T(128)S(1)} %copy-done.3, f32[98]{0:T(128)S(1)} %pad_dynamic-slice_fusion.pull, f32[2048,128]{1,0:T(8,128)S(1)} %bitcast.21), custom_call_target="tpu_custom_call" | custom-call | tf_op jit(solution)/shard_map/spread/pallas_call | solution.py:303
  (9 shorter events, 0.1 us)
Async XLA Ops:
  1.6 0.7 copy-start.1
  3.5 9.2 %collective-permute-start = (f32[16,256]{1,0:T(8,128)S(1)}, f32[16,256]{1,0:T(8,128)S(1)}, u32[]{:S(2)}, u32[]{:S(2)}) collective-permute-start(f32[16,256]{1,0:T(8,128)S(1)} %concatenate.6), channel_id=1, source_target_pairs={{0,1},{1,2},{2,3},{3,4},{4,5},{5,6},{6,7},{8,9},{9,10},{10,11},{11... | collective-permute-start | bytes 49160 | tf_op jit(solution)/shard_map/ppermute | solution.py:254
  6.1 6.6 %collective-permute-start.1 = (f32[16,256]{1,0:T(8,128)S(1)}, f32[16,256]{1,0:T(8,128)S(1)}, u32[]{:S(2)}, u32[]{:S(2)}) collective-permute-start(f32[16,256]{1,0:T(8,128)S(1)} %concatenate.7), channel_id=1, source_target_pairs={{1,0},{2,1},{3,2},{4,3},{5,4},{6,5},{7,6},{9,8},{10,9},{11,10},{12... | collective-permute-start | bytes 49160 | tf_op jit(solution)/shard_map/ppermute | solution.py:255
  9.8 1.2 %copy-start = (f32[5,2,96,256]{3,2,1,0:T(8,128)S(1)}, f32[5,2,96,256]{3,2,1,0:T(8,128)}, u32[]{:S(2)}) copy-start(f32[5,2,96,256]{3,2,1,0:T(8,128)} %fields.3) | copy-start | bytes 2949124
  13.8 52.1 %all-to-all-start = ((f32[64,32,128]{2,1,0:T(8,128)}), f32[64,32,128]{2,1,0:T(8,128)S(1)}, u32[]{:S(2)}, u32[]{:S(2)}) async-start(f32[64,32,128]{2,1,0:T(8,128)} %finish.1), calls=%async_computation | async-start | bytes 2097152 | tf_op jit(solution)/shard_map/all_to_all | solution.py:246
  70.4 38.2 %all-to-all-start.1 = ((f32[64,32,128]{2,1,0:T(8,128)}), f32[64,32,128]{2,1,0:T(8,128)S(1)}, u32[]{:S(2)}, u32[]{:S(2)}) async-start(f32[64,32,128]{2,1,0:T(8,128)} %bitcast.12), calls=%async_computation.1 | async-start | bytes 2097152 | tf_op jit(solution)/shard_map/all_to_all | solution.py:246
  75.3 0.7 copy-start.5
  76.0 0.7 copy-start.4
  105.2 3.4 %copy-start.2 = (f32[96]{0:T(128)S(1)}, f32[96]{0:T(128)}, u32[]{:S(2)}) copy-start(f32[96]{0:T(128)} %kappa_az.1) | copy-start | bytes 1156
  105.2 3.4 %copy-start.3 = (f32[96]{0:T(128)S(1)}, f32[96]{0:T(128)}, u32[]{:S(2)}) copy-start(f32[96]{0:T(128)} %kappa_rad.1) | copy-start | bytes 1156

commit v4 on v1

v4 whole, which is shorter than its diff:
```python
import jax
import jax.numpy as jnp
from jax import lax
from jax.experimental import pallas as pl
from jax.experimental.pallas import tpu as pltpu
from jax.sharding import Mesh, PartitionSpec as P

star_mass = 1.0
RAD = ("chip", "core")

ORDER = (0, 1, 3, 2, 4)
RING = 64
GROUPS = 3
ROWS = 96
SPAN = ROWS // GROUPS
HALF = 16
BLOCK = 2 * HALF
PIECES = 2 * RING
STEP = 8
VMEM_LIMIT = 24 * 1024 * 1024

TILES = ((0, 1, 5), (1, 2, 2))


def iotas():
    lane = lax.broadcasted_iota(jnp.int32, (8, 128), 1)
    line = lax.broadcasted_iota(jnp.int32, (8, 128), 0)
    return lane, line


def windows():
    for side in range(2):
        for layer in range(2):
            for half in range(2):
                yield side, layer, half, BLOCK * (32 * side + 16 * layer + 8 * half) + 31


def pack_kernel(given, fields, packed, cells, shifts, sems):
    lane, line = iotas()
    shift_copy = pltpu.make_async_copy(given, shifts, sems.at[5])
    shift_copy.start()
    copies = [pltpu.make_async_copy(fields.at[f], cells.at[f], sems.at[f]) for f in ORDER]
    for copy in copies:
        copy.start()
    for place, field in enumerate(ORDER):
        copies[place].wait()
        for layer in range(2):
            for group in range(GROUPS):
                for half in range(2):
                    first = BLOCK * layer + HALF * half + 5 * group + place
                    packed[pl.ds(first, SPAN, stride=2 * BLOCK), :] = cells[
                        field, layer, pl.ds(SPAN * group, SPAN), pl.ds(128 * half, 128)
                    ]
        if place == 0:
            halves = [cells[0, z, :, pl.ds(128 * h, 128)] for z in range(2) for h in range(2)]
            total = (halves[0] + halves[1]) + (halves[2] + halves[3])
            square = jnp.concatenate([total, jnp.zeros((128 - ROWS, 128), jnp.float32)], axis=0)
            mass = jnp.sum(square.T, axis=0, keepdims=True)
            packed[pl.ds(15, RING, stride=BLOCK), :] = jnp.broadcast_to(mass, (RING, 128))
    shift_copy.wait()
    for side, layer, half, first in windows():
        row = (ROWS - 1) * (1 - side)
        part, odd = shifts[row] & 127, shifts[row] & 128
        tile = jnp.zeros((8, 128), jnp.float32)
        for place, field in enumerate(ORDER):
            low, high = (
                pltpu.roll(jnp.broadcast_to(cells[field, layer, pl.ds(row, 1), pl.ds(at, 128)], (8, 128)), part, 1)
                for at in (0, 128)
            )
            chosen = jnp.where((lane < part) ^ (odd != 0) ^ (half == 1), high, low)
            turned = pltpu.roll(chosen, 16 * (place + 1), 1)
            for bit in (1, 2, 4):
                turned = jnp.where(line & bit == 0, turned, pltpu.roll(turned, 128 - 16 * bit, 1))
            tile = jnp.where(lane >> 4 == place + 1, turned, tile)
        packed[pl.ds(first, 8, stride=BLOCK), :] = tile


def ends_kernel(steps, lines, moved, twice):
    cells = lines[pl.ds(31, RING, stride=BLOCK), :]
    twice[pl.ds(0, RING), :] = cells
    twice[pl.ds(RING, RING), :] = cells
    shift = steps[3]
    lane = lax.broadcasted_iota(jnp.int32, (RING, 128), 1)
    crossed = (lane & 15) + 16 * (steps[4] & 15) < (shift & 255)
    blocks = shift >> 8
    moved[...] = jnp.where(crossed, twice[pl.ds(RING - 1 - blocks, RING), :], twice[pl.ds(RING - blocks, RING), :])


def join_kernel(tail, ends, begun, moved, rows, sem):
    rows[...] = tail[...]
    lane = lax.broadcasted_iota(jnp.int32, (RING, 128), 1)
    last = pl.ds(7, RING, stride=8)
    rows[last, :] = jnp.where(lane < 16, tail[last, :], ends[...])
    copy = pltpu.make_async_copy(rows.reshape(RING, 8, 128), moved.at[:, pl.ds(24, 8), :], sem)
    copy.start()
    copy.wait()


def shift_kernel(steps, lines, moved, tail, mass, twice):
    lane, line = iotas()
    whole, part, early = [], [], []
    for group in range(GROUPS):
        shift = steps[group]
        whole.append(shift >> 7)
        part.append(shift & 127)
        early.append(lane < part[group])

    def piece_of(piece, tile, group):
        at = pl.multiple_of(((piece - whole[group]) & (PIECES - 1)) * HALF + 8 * tile, 8)
        return lines[pl.ds(at, 8), :]

    def turned(value, group):
        return pltpu.roll(value, part[group], 1)

    def several(step, state):
        before, edges = state
        edges = list(edges)
        first_piece = step * STEP
        loaded = [
            [[piece_of(first_piece + i, tile, group) for group in TILES[tile][:2]] for tile in range(2)]
            for i in range(STEP)
        ]
        values = []
        for i in range(STEP):
            now, made = [], []
            for tile, (first, second, split) in enumerate(TILES):
                a, b = turned(loaded[i][tile][0], first), turned(loaded[i][tile][1], second)
                pa, pb = before[tile]
                made.append(
                    jnp.where(line < split, jnp.where(early[first], pa, a), jnp.where(early[second], pb, b))
                )
                now.append((a, b))
            before = tuple(now)
            values.append(made)
        for i in range(0, STEP, 2):
            ring = step * (STEP // 2) + i // 2
            for tile in range(2):
                both = jnp.where(lane == 127, values[i + 1][tile], values[i][tile])
                edges[tile] = jnp.where(lane >> 1 == ring, pltpu.roll(both, (2 * ring + 1) & 127, 1), edges[tile])
        for i in range(STEP):
            for tile in range(2):
                if i % 2 == 1 and tile == 1:
                    at = pl.multiple_of((first_piece + i) // 2 * 8, 8)
                    tail[pl.ds(at, 8), :] = values[i][tile]
                else:
                    at = pl.multiple_of((first_piece + i) * HALF + 8 * tile, 8)
                    moved[pl.ds(at, 8), :] = values[i][tile]
        return before, tuple(edges)

    before = tuple(
        tuple(turned(piece_of(PIECES - 1, tile, group), group) for group in TILES[tile][:2]) for tile in range(2)
    )
    zero = jnp.zeros((8, 128), jnp.float32)
    _, edges = lax.fori_loop(0, PIECES // STEP, several, (before, (zero, zero)))
    twice[...] = jnp.concatenate([edges[0], edges[1], jnp.zeros((112, 128), jnp.float32)], axis=0).T
    left = twice[pl.ds(0, RING, stride=2), :]
    right = twice[pl.ds(1, RING, stride=2), :]
    moved[pl.ds(BLOCK + 15, RING - 1, stride=BLOCK), :] = left[: RING - 1]
    moved[pl.ds(15, 1), :] = left[RING - 1 :]
    right = jnp.concatenate([right[1:], right[:1]], axis=0)
    tail[pl.ds(7, RING, stride=8), :] = right
    parts = lines[pl.ds(15, RING, stride=BLOCK), :]
    mass[...] = jnp.broadcast_to(jnp.sum(parts, axis=0, keepdims=True), (8, 128))


def spread_kernel(rates, lines, updated, done, ends, square):
    lane, line = iotas()
    square[pl.ds(0, RING, stride=2), :] = lines[pl.ds(15, RING, stride=BLOCK), :]
    square[pl.ds(1, RING - 1, stride=2), :] = lines[pl.ds(BLOCK + 31, RING - 1, stride=BLOCK), :]
    square[pl.ds(127, 1), :] = lines[pl.ds(31, 1), :]
    across = square[...].T
    edges = across[0:8], across[8:16]
    under_edges = tuple(pltpu.roll(value, 1, 0) for value in edges)
    takes = (((line == 1) | (line == 2), (line == 6) | (line == 7)), (None, (line == 3) | (line == 4)))

    def spread(first_rate, row, tile):
        first, second, split = TILES[tile]
        return jnp.where(
            line < split, rates[first_rate + SPAN * first + row], rates[first_rate + SPAN * second + row]
        )

    def pulls(row, tile):
        first, second, _ = TILES[tile]
        other = jnp.where(takes[tile][1], rates[2 * ROWS + 1 + SPAN * second + row], 0.0)
        if takes[tile][0] is None:
            return other
        return jnp.where(takes[tile][0], rates[2 * ROWS + 1 + SPAN * first + row], other)

    def source(value, rate):
        return value - rate * pltpu.roll(value, 1, 0)

    def spots():
        return ((tile, layer, half) for tile in range(2) for layer in range(2) for half in range(2))

    def place_of(row, tile, layer, half):
        return pl.multiple_of((2 * row + layer) * BLOCK + HALF * half + 8 * tile, 8)

    def begin(row):
        cells = {spot: lines[pl.ds(place_of(row, *spot), 8), :] for spot in spots()}
        full, partial = [], []
        for tile in range(2):
            az, rad, rate = spread(0, row, tile), spread(ROWS, row, tile), pulls(row, tile)
            keep = 1.0 - 2.0 * (az + rad)
            border = edges[tile] - rate * under_edges[tile]
            for layer in range(2):
                low, high = (source(cells[tile, layer, half], rate) for half in range(2))
                side = pltpu.roll(border, (128 - 4 * row - 2 * layer) & 127, 1)
                low_up, high_up = pltpu.roll(low, 1, 1), pltpu.roll(high, 1, 1)
                low_down, high_down = pltpu.roll(low, 127, 1), pltpu.roll(high, 127, 1)
                low_sum = jnp.where(lane == 0, side, low_up) + jnp.where(lane == 127, high_down, low_down)
                high_sum = jnp.where(lane == 0, low_up, high_up) + jnp.where(lane == 127, side, high_down)
                full += [low, high]
                partial += [keep * low + az * low_sum, keep * high + az * high_sum]
        return full, partial

    def end(row, partial, under, over):
        for tile in range(2):
            rad = spread(ROWS, row, tile)
            for layer in range(2):
                for half in range(2):
                    at = 4 * tile + 2 * layer + half
                    done[pl.ds(place_of(row, tile, layer, half), 8), :] = partial[at] + rad * (under[at] + over[at])

    ends[...] = jnp.zeros(ends.shape, jnp.float32)
    for side, layer, half, first in windows():
        tile = lines[pl.ds(first, 8, stride=BLOCK), :]
        for place in range(5):
            turned = pltpu.roll(pltpu.roll(tile, 112 - 16 * place, 1), 0, 1, stride=16, stride_axis=0)
            cells = jnp.sum(jnp.where(lane >> 4 == line, turned, 0.0), axis=0, keepdims=True)
            ends[pl.ds(8 * (4 * side + 2 * layer + half) + place, 1), :] = cells

    def outer(side):
        rate = jnp.where(takes[0][0], rates[2 * ROWS + (ROWS + 1) * side], 0.0)
        return [source(ends[pl.ds(32 * side + 8 * i, 8), :], rate) for i in range(4)]

    last, last_partial = begin(SPAN - 1)
    full, partial = begin(0)
    turned = [pltpu.roll(value, 5, 0) for value in last]
    under = [jnp.where(line < 5, value, turned[i]) for i, value in enumerate(outer(0))]
    under += [jnp.where(line < 5, turned[i], turned[4 + i]) for i in range(4)]
    turned = [pltpu.roll(value, 3, 0) for value in full]
    over = [jnp.where(line < 3, turned[i], turned[4 + i]) for i in range(4)]
    over += [jnp.where(line < 2, turned[4 + i], pltpu.roll(value, 2, 0)) for i, value in enumerate(outer(1))]
    for i in range(8):
        ends[pl.ds(64 + 8 * i, 8), :] = last[i]
        ends[pl.ds(128 + 8 * i, 8), :] = last_partial[i]
        ends[pl.ds(192 + 8 * i, 8), :] = over[i]

    def kept(first):
        return [ends[pl.ds(first + 8 * i, 8), :] for i in range(8)]

    def rows(pair, state):
        under, full, partial = state
        for row in (2 * pair + 1, 2 * pair + 2):
            over, later = begin(row)
            end(row - 1, partial, under, over)
            under, full, partial = full, over, later
        return under, full, partial

    under, full, partial = lax.fori_loop(0, SPAN // 2 - 1, rows, (under, full, partial))
    last = kept(64)
    end(SPAN - 2, partial, under, last)
    end(SPAN - 1, kept(128), full, kept(192))

    for place, field in enumerate(ORDER):
        for layer in range(2):
            for group in range(GROUPS):
                for half in range(2):
                    first = BLOCK * layer + HALF * half + 5 * group + place
                    updated[field, layer, pl.ds(SPAN * group, SPAN), pl.ds(128 * half, 128)] = done[
                        pl.ds(first, SPAN, stride=2 * BLOCK), :
                    ]


def specs(*kinds):
    return [pl.BlockSpec(memory_space=kind) for kind in kinds]


def shards(fields, shifts, cycle_area, gravity, kappa_az, kappa_rad):
    vmem, smem = pltpu.VMEM, pltpu.SMEM
    params = pltpu.CompilerParams(vmem_limit_bytes=VMEM_LIMIT)
    blocks = jax.ShapeDtypeStruct((RING * BLOCK, 128), jnp.float32)

    def dealt(lines):
        lines = lines.reshape(RING, BLOCK, 128)
        return lax.all_to_all(lines, "az", 0, 0, tiled=True).reshape(RING * BLOCK, 128)

    ranks = lax.axis_size(RAD)
    packed = pl.pallas_call(
        pack_kernel,
        out_shape=blocks,
        in_specs=specs(pltpu.HBM, pltpu.HBM),
        out_specs=specs(vmem)[0],
        scratch_shapes=[
            pltpu.VMEM(fields.shape, jnp.float32),
            pltpu.SMEM(shifts.shape, jnp.int32),
            pltpu.SemaphoreType.DMA((6,)),
        ],
        compiler_params=pltpu.CompilerParams(vmem_limit_bytes=60 * 1024 * 1024),
        name="pack",
    )(shifts, fields)
    whole = dealt(packed)
    place = lax.axis_index("az").astype(jnp.int32)
    mine = lax.dynamic_slice(shifts.reshape(GROUPS, SPAN), (0, place // 2), (GROUPS, 1))[:, 0]
    end = jnp.where(place < RING // 2, shifts[ROWS - 1 :], shifts[:1])
    steps = jnp.concatenate([mine, end, place[None]])
    ends = pl.pallas_call(
        ends_kernel,
        out_shape=jax.ShapeDtypeStruct((RING, 128), jnp.float32),
        in_specs=specs(smem, vmem),
        out_specs=specs(vmem)[0],
        scratch_shapes=[pltpu.VMEM((2 * RING, 128), jnp.float32)],
        compiler_params=params,
        name="ends",
    )(steps, whole)
    outward = [(q * ranks + i, q * ranks + i + 1) for q in range(RING // 2) for i in range(ranks - 1)]
    inward = [(q * ranks + i + 1, q * ranks + i) for q in range(RING // 2, RING) for i in range(ranks - 1)]
    ends = lax.ppermute(ends, ("az",) + RAD, outward + inward)
    begun, tail, mass = pl.pallas_call(
        shift_kernel,
        out_shape=(
            blocks,
            jax.ShapeDtypeStruct((RING * 8, 128), jnp.float32),
            jax.ShapeDtypeStruct((8, 128), jnp.float32),
        ),
        in_specs=specs(smem, vmem),
        out_specs=specs(vmem, vmem, vmem),
        scratch_shapes=[pltpu.VMEM((2 * RING, 128), jnp.float32)],
        compiler_params=params,
        name="shift",
    )(steps, whole)
    moved = pl.pallas_call(
        join_kernel,
        out_shape=jax.ShapeDtypeStruct((RING, BLOCK, 128), jnp.float32),
        in_specs=specs(vmem, vmem, pl.ANY),
        out_specs=specs(pl.ANY)[0],
        scratch_shapes=[pltpu.VMEM((RING * 8, 128), jnp.float32), pltpu.SemaphoreType.DMA],
        input_output_aliases={2: 0},
        compiler_params=params,
        name="join",
    )(tail, ends, begun.reshape(RING, BLOCK, 128))
    lines = dealt(moved)

    row_mass = cycle_area * mass[0, :ROWS] / (2.0 * RING * 256)
    mine = jnp.stack([row_mass, gravity])
    everyone = lax.all_gather(lax.all_gather(mine, "core"), "chip").reshape(ranks, 2, ROWS)
    masses = everyone[:, 0, :]
    totals = jnp.sum(masses, axis=1)
    rank = jnp.arange(ranks)
    offset = jnp.sum(jnp.where(rank[None, :] < rank[:, None], totals[None, :], 0.0), axis=1)
    row = jnp.arange(ROWS)
    before = jnp.sum(jnp.where(row[None, None, :] < row[None, :, None], masses[:, None, :], 0.0), axis=2)
    reach = star_mass + offset[:, None] + before + 0.5 * masses
    pulls = (everyone[:, 1, :] * reach).reshape(ranks * ROWS)
    me = lax.axis_index(RAD)
    pull = lax.dynamic_slice(jnp.pad(pulls, (1, 1)), (me * ROWS,), (ROWS + 2,))
    enclosed = lax.dynamic_slice(reach.reshape(ranks * ROWS), (me * ROWS,), (ROWS,))

    updated = pl.pallas_call(
        spread_kernel,
        out_shape=jax.ShapeDtypeStruct(fields.shape, jnp.float32),
        in_specs=specs(smem, vmem),
        out_specs=specs(vmem)[0],
        scratch_shapes=[
            pltpu.VMEM((RING * BLOCK, 128), jnp.float32),
            pltpu.VMEM((256, 128), jnp.float32),
            pltpu.VMEM((128, 128), jnp.float32),
        ],
        compiler_params=params,
        name="spread",
    )(jnp.concatenate([kappa_az, kappa_rad, pull]), lines)
    return updated, enclosed


def solution(mesh):
    split = Mesh(mesh.devices.reshape(mesh.shape["az"], -1, 2), ("az",) + RAD)
    placed = (P(None, None, RAD, "az"), P(RAD), P(RAD), P(RAD), P(RAD), P(RAD))
    return jax.shard_map(
        shards,
        mesh=split,
        in_specs=placed,
        out_specs=(P(None, None, RAD, "az"), P(RAD)),
        check_vma=False,
    )
```

time: 115 us -> 109 us (0.948)
  the two profiles are of different devices: /device:TPU:1 before, /device:TPU:8 now
where the time goes in v4:
time: 109 us
  waiting for transfers between devices  34.8 us (32%)
  blocking collectives  28.2 us (26%)
  starting transfers between devices  25.2 us (23%)
  Pallas kernels  13.5 us (12%)
  local copies, waits for them, and re-layouts  4.29 us (4%)
  between operations  1.99 us (2%)
    all_to_all x2, waiting for transfers between devices, dealt(): lax.all_to_all(lines, 'az', 0, 0, tiled=True).reshape(RING * BLOCK, 128)  34.8 us
    all_gather x1, blocking collectives, shards(): lax.all_gather(lax.all_gather(mine, 'core'), 'chip').reshape(ranks, 2, ROWS)  26.3 us
    all_to_all x2, starting transfers between devices, dealt(): lax.all_to_all(lines, 'az', 0, 0, tiled=True).reshape(RING * BLOCK, 128)  23.2 us
    pallas_call x1, Pallas kernels, shards(): pl.pallas_call(shift_kernel, out_shape=(blocks, jax.ShapeDtypeStruct((RIN...  4.45 us
    pallas_call x1, Pallas kernels, shards(): pl.pallas_call(spread_kernel, out_shape=jax.ShapeDtypeStruct(fields.shape...  4.22 us
    pallas_call x1, Pallas kernels, shards(): pl.pallas_call(pack_kernel, out_shape=blocks, in_specs=specs(pltpu.HBM, p...  3.51 us
    unnamed x10, local copies, waits for them, and re-layouts  2.55 us
  transfers between devices with their start and end apart: 3, of which 2 were waited for; matrix products, arithmetic and copies ran while one was open for 2% of the time, Pallas kernels for 4%

profile of v4, /device:TPU:8, one launch (start us, length us, event | category | flops | bytes accessed | tf_op | source)
XLA Modules:
  0.0 108.7 jit_solution(7282449109143481998)
XLA Ops:
  0.6 3.5 %pack.1 = f32[2048,128]{1,0:T(8,128)} custom-call(s32[96]{0:T(128)} %given.1, f32[5,2,96,256]{3,2,1,0:T(8,128)} %fields.1), custom_call_target="tpu_custom_call" | custom-call | tf_op jit(solution)/shard_map/pack/pallas_call | solution.py:289
  4.1 18.2 %all-to-all-start = ((f32[64,32,128]{2,1,0:T(8,128)}), f32[64,32,128]{2,1,0:T(8,128)S(1)}, u32[]{:S(2)}, u32[]{:S(2)}) async-start(f32[64,32,128]{2,1,0:T(8,128)} %bitcast.21), calls=%async_computation | async-start | bytes 2097152 | tf_op jit(solution)/shard_map/all_to_all | solution.py:286
  22.3 0.0 copy-start
  22.3 0.6 copy-done
  23.0 0.1 reshape.55
  23.1 0.2 dynamic-slice_reduce_fusion
  23.2 0.6 fusion.3
  25.1 0.1 pad_add_fusion.steps
  25.2 31.7 %all-to-all-done = f32[64,32,128]{2,1,0:T(8,128)S(1)} async-done(((f32[64,32,128]{2,1,0:T(8,128)}), f32[64,32,128]{2,1,0:T(8,128)S(1)}, u32[]{:S(2)}, u32[]{:S(2)}) %all-to-all-start) | async-done | bytes 1048608 | tf_op jit(solution)/shard_map/all_to_all | solution.py:286
  56.9 0.6 ends.1
  57.5 1.9 %collective-permute-start = (f32[64,128]{1,0:T(8,128)S(1)}, f32[64,128]{1,0:T(8,128)S(1)}, u32[]{:S(2)}, u32[]{:S(2)}) collective-permute-start(f32[64,128]{1,0:T(8,128)S(1)} %ends.1), channel_id=1, source_target_pairs={{0,1},{1,2},{2,3},{3,4},{4,5},{5,6},{6,7},{8,9},{9,10},{10,11},{11... | collective-permute-start | bytes 98312 | tf_op jit(solution)/shard_map/ppermute | solution.py:318
  59.4 4.5 %shift.1 = (f32[2048,128]{1,0:T(8,128)}, f32[512,128]{1,0:T(8,128)S(1)}, f32[8,128]{1,0:T(8,128)S(1)}) custom-call(s32[5]{0:T(128)S(1)} %pad_add_fusion.steps, f32[2048,128]{1,0:T(8,128)S(1)} %bitcast.19), custom_call_target="tpu_custom_call" | custom-call | tf_op jit(solution)/shard_map/shift/pallas_call | solution.py:319
  63.9 0.0 collective-permute-done.ends
  63.9 0.8 join.1
  64.6 5.1 %all-to-all-start.1 = ((f32[64,32,128]{2,1,0:T(8,128)}), f32[64,32,128]{2,1,0:T(8,128)S(1)}, u32[]{:S(2)}, u32[]{:S(2)}) async-start(f32[64,32,128]{2,1,0:T(8,128)} %join.1), calls=%async_computation.1 | async-start | bytes 2097152 | tf_op jit(solution)/shard_map/all_to_all | solution.py:286
  69.8 0.0 copy-start.4
  69.8 0.6 copy-done.4
  70.4 0.0 copy-start.3
  70.4 0.7 copy-done.3
  71.1 1.9 %all-gather.2 = f32[2,2,96]{2,1,0:T(2,128)S(1)} all-gather(f32[1,2,96]{2,1,0:T(2,128)S(1)} %maximum_bitcast_fusion), channel_id=2, replica_groups=mesh['az'=64,'chip'=4,'core'=2] {'core'}, dimensions={0}, use_global_device_ids=true | all-gather | bytes 2304 | tf_op jit(solution)/shard_map/all_gather | solution.py:346
  73.0 26.3 %all-gather.1 = f32[8,2,96]{2,1,0:T(2,128)S(1)} all-gather(f32[2,2,96]{2,1,0:T(2,128)S(1)} %all-gather.2), channel_id=3, replica_groups=mesh['az'=64,'chip'=4,'core'=2] {'chip'}, dimensions={0}, use_global_device_ids=true | all-gather | bytes 7680 | tf_op jit(solution)/shard_map/all_gather | solution.py:346
  99.3 0.2 multiply_reduce_fusion
  99.4 0.1 select_reduce_fusion.1
  99.5 0.2 select_reduce_fusion
  99.8 0.1 broadcast_add_fusion
  99.8 0.1 add.45
  99.9 0.1 mul.28
  100.0 0.1 squeeze.12
  100.1 0.6 dynamic_slice.11
  100.7 0.0 copy-start.1
  100.7 0.0 copy-start.2
  100.7 0.1 pad_dynamic-slice_fusion
  100.7 0.6 copy-done.1
  101.3 0.0 copy-done.2
  101.3 0.1 pad_maximum_fusion.rates
  101.4 3.1 %all-to-all-done.1 = f32[64,32,128]{2,1,0:T(8,128)S(1)} async-done(((f32[64,32,128]{2,1,0:T(8,128)}), f32[64,32,128]{2,1,0:T(8,128)S(1)}, u32[]{:S(2)}, u32[]{:S(2)}) %all-to-all-start.1) | async-done | bytes 1048608 | tf_op jit(solution)/shard_map/all_to_all | solution.py:286
  104.5 4.2 %spread.1 = f32[5,2,96,256]{3,2,1,0:T(8,128)} custom-call(f32[290]{0:T(512)S(1)} %pad_maximum_fusion.rates, f32[2048,128]{1,0:T(8,128)S(1)} %bitcast.20), custom_call_target="tpu_custom_call" | custom-call | tf_op jit(solution)/shard_map/spread/pallas_call | solution.py:359
  (5 shorter events, 0.0 us)
Async XLA Ops:
  4.1 52.8 %all-to-all-start = ((f32[64,32,128]{2,1,0:T(8,128)}), f32[64,32,128]{2,1,0:T(8,128)S(1)}, u32[]{:S(2)}, u32[]{:S(2)}) async-start(f32[64,32,128]{2,1,0:T(8,128)} %bitcast.21), calls=%async_computation | async-start | bytes 2097152 | tf_op jit(solution)/shard_map/all_to_all | solution.py:286
  22.3 0.7 copy-start
  57.5 6.4 %collective-permute-start = (f32[64,128]{1,0:T(8,128)S(1)}, f32[64,128]{1,0:T(8,128)S(1)}, u32[]{:S(2)}, u32[]{:S(2)}) collective-permute-start(f32[64,128]{1,0:T(8,128)S(1)} %ends.1), channel_id=1, source_target_pairs={{0,1},{1,2},{2,3},{3,4},{4,5},{5,6},{6,7},{8,9},{9,10},{10,11},{11... | collective-permute-start | bytes 98312 | tf_op jit(solution)/shard_map/ppermute | solution.py:318
  64.6 39.8 %all-to-all-start.1 = ((f32[64,32,128]{2,1,0:T(8,128)}), f32[64,32,128]{2,1,0:T(8,128)S(1)}, u32[]{:S(2)}, u32[]{:S(2)}) async-start(f32[64,32,128]{2,1,0:T(8,128)} %join.1), calls=%async_computation.1 | async-start | bytes 2097152 | tf_op jit(solution)/shard_map/all_to_all | solution.py:286
  69.8 0.7 copy-start.4
  70.4 0.7 copy-start.3
  100.7 0.7 copy-start.1
  100.7 0.7 copy-start.2

commit v5 on v4

--- a/solution.py
+++ b/solution.py
@@ -16,6 +16,7 @@
 HALF = 16
 BLOCK = 2 * HALF
 PIECES = 2 * RING
+PARTS = SPAN // 8
 STEP = 8
 VMEM_LIMIT = 24 * 1024 * 1024
 
@@ -35,28 +36,23 @@
                 yield side, layer, half, BLOCK * (32 * side + 16 * layer + 8 * half) + 31
 
 
-def pack_kernel(given, fields, packed, cells, shifts, sems):
+def pack_kernel(given, fields, packed, cells, lines, shifts, sems, sent):
     lane, line = iotas()
-    shift_copy = pltpu.make_async_copy(given, shifts, sems.at[5])
+    shift_copy = pltpu.make_async_copy(given, shifts, sems.at[GROUPS * PARTS])
     shift_copy.start()
-    copies = [pltpu.make_async_copy(fields.at[f], cells.at[f], sems.at[f]) for f in ORDER]
-    for copy in copies:
-        copy.start()
-    for place, field in enumerate(ORDER):
-        copies[place].wait()
-        for layer in range(2):
-            for group in range(GROUPS):
-                for half in range(2):
-                    first = BLOCK * layer + HALF * half + 5 * group + place
-                    packed[pl.ds(first, SPAN, stride=2 * BLOCK), :] = cells[
-                        field, layer, pl.ds(SPAN * group, SPAN), pl.ds(128 * half, 128)
-                    ]
-        if place == 0:
-            halves = [cells[0, z, :, pl.ds(128 * h, 128)] for z in range(2) for h in range(2)]
-            total = (halves[0] + halves[1]) + (halves[2] + halves[3])
-            square = jnp.concatenate([total, jnp.zeros((128 - ROWS, 128), jnp.float32)], axis=0)
-            mass = jnp.sum(square.T, axis=0, keepdims=True)
-            packed[pl.ds(15, RING, stride=BLOCK), :] = jnp.broadcast_to(mass, (RING, 128))
+    copies = {}
+    for part, group in sorted(
+        ((part, group) for part in range(PARTS) for group in range(GROUPS)),
+        key=lambda at: at not in ((0, 0), (PARTS - 1, GROUPS - 1)),
+    ):
+        rows = pl.ds(SPAN * group + 8 * part, 8)
+        copies[part, group] = pltpu.make_async_copy(
+            fields.at[:, :, rows, :], cells.at[:, :, rows, :], sems.at[GROUPS * part + group]
+        )
+        copies[part, group].start()
+    arrived = [(0, 0), (PARTS - 1, GROUPS - 1)]
+    for at in arrived:
+        copies[at].wait()
     shift_copy.wait()
     for side, layer, half, first in windows():
         row = (ROWS - 1) * (1 - side)
@@ -72,7 +68,37 @@
             for bit in (1, 2, 4):
                 turned = jnp.where(line & bit == 0, turned, pltpu.roll(turned, 128 - 16 * bit, 1))
             tile = jnp.where(lane >> 4 == place + 1, turned, tile)
-        packed[pl.ds(first, 8, stride=BLOCK), :] = tile
+        lines[pl.ds(first, 8, stride=BLOCK), :] = tile
+    blocks = lines.reshape(RING, BLOCK, 128)
+    sending = []
+
+    def send(first, count, low, high):
+        part = pl.ds(first, count), pl.ds(low, high - low)
+        copy = pltpu.make_async_copy(blocks.at[part[0], part[1], :], packed.at[part[0], part[1], :], sent.at[len(sending)])
+        copy.start()
+        sending.append(copy)
+
+    for part in range(PARTS):
+        for group in range(GROUPS):
+            if (part, group) not in arrived:
+                copies[part, group].wait()
+            for place, field in enumerate(ORDER):
+                for layer in range(2):
+                    for half in range(2):
+                        first = 16 * BLOCK * part + BLOCK * layer + HALF * half + 5 * group + place
+                        lines[pl.ds(first, 8, stride=2 * BLOCK), :] = cells[
+                            field, layer, pl.ds(SPAN * group + 8 * part, 8), pl.ds(128 * half, 128)
+                        ]
+        send(16 * part, 16, 0, 8)
+        send(16 * part, 16, 16, 32)
+    halves = [cells[0, z, :, pl.ds(128 * h, 128)] for z in range(2) for h in range(2)]
+    total = (halves[0] + halves[1]) + (halves[2] + halves[3])
+    square = jnp.concatenate([total, jnp.zeros((128 - ROWS, 128), jnp.float32)], axis=0)
+    mass = jnp.sum(square.T, axis=0, keepdims=True)
+    lines[pl.ds(15, RING, stride=BLOCK), :] = jnp.broadcast_to(mass, (RING, 128))
+    send(0, RING, 8, 16)
+    for copy in sending:
+        copy.wait()
 
 
 def ends_kernel(steps, lines, moved, twice):
@@ -90,14 +116,22 @@
     rows[...] = tail[...]
     lane = lax.broadcasted_iota(jnp.int32, (RING, 128), 1)
     last = pl.ds(7, RING, stride=8)
-    rows[last, :] = jnp.where(lane < 16, tail[last, :], ends[...])
+    rows[last, :] = jnp.where((lane < 16) | (lane >= 96), tail[last, :], ends[...])
     copy = pltpu.make_async_copy(rows.reshape(RING, 8, 128), moved.at[:, pl.ds(24, 8), :], sem)
     copy.start()
     copy.wait()
 
 
-def shift_kernel(steps, lines, moved, tail, mass, twice):
+def shift_kernel(steps, lines, begun, tail, mass, moved, square, sems):
     lane, line = iotas()
+    blocks = moved.reshape(RING, BLOCK, 128)
+
+    def copy_of(step):
+        part = pl.ds(step * (STEP // 2), STEP // 2)
+        return pltpu.make_async_copy(
+            blocks.at[part, pl.ds(0, 24), :], begun.at[part, pl.ds(0, 24), :], sems.at[step]
+        )
+
     whole, part, early = [], [], []
     for group in range(GROUPS):
         shift = steps[group]
@@ -145,6 +179,7 @@
                 else:
                     at = pl.multiple_of((first_piece + i) * HALF + 8 * tile, 8)
                     moved[pl.ds(at, 8), :] = values[i][tile]
+        copy_of(step).start()
         return before, tuple(edges)
 
     before = tuple(
@@ -152,20 +187,36 @@
     )
     zero = jnp.zeros((8, 128), jnp.float32)
     _, edges = lax.fori_loop(0, PIECES // STEP, several, (before, (zero, zero)))
-    twice[...] = jnp.concatenate([edges[0], edges[1], jnp.zeros((112, 128), jnp.float32)], axis=0).T
-    left = twice[pl.ds(0, RING, stride=2), :]
-    right = twice[pl.ds(1, RING, stride=2), :]
-    moved[pl.ds(BLOCK + 15, RING - 1, stride=BLOCK), :] = left[: RING - 1]
-    moved[pl.ds(15, 1), :] = left[RING - 1 :]
+    square[...] = jnp.concatenate([edges[0], edges[1], jnp.zeros((112, 128), jnp.float32)], axis=0).T
+    left = pltpu.roll(square[pl.ds(0, RING, stride=2), :], 96, 1)
+    right = square[pl.ds(1, RING, stride=2), :]
+    left = jnp.concatenate([left[RING - 1 :], left[: RING - 1]], axis=0)
     right = jnp.concatenate([right[1:], right[:1]], axis=0)
-    tail[pl.ds(7, RING, stride=8), :] = right
+    tail[pl.ds(7, RING, stride=8), :] = left + right
     parts = lines[pl.ds(15, RING, stride=BLOCK), :]
     mass[...] = jnp.broadcast_to(jnp.sum(parts, axis=0, keepdims=True), (8, 128))
 
-
-def spread_kernel(rates, lines, updated, done, ends, square):
+    @pl.loop(0, PIECES // STEP)
+    def _(step):
+        copy_of(step).wait()
+
+
+def spread_kernel(rank, rates, totals, local, lines, updated, enclosed, done, out, ends, square, sems):
     lane, line = iotas()
-    square[pl.ds(0, RING, stride=2), :] = lines[pl.ds(15, RING, stride=BLOCK), :]
+    here = rank[0]
+    base = jnp.float32(star_mass)
+    for other in range(totals.shape[0] // 8):
+        base = base + jnp.where(other < here, totals[8 * other], 0.0)
+    below = 8 * jnp.maximum(here - 1, 0)
+    above = 8 * jnp.minimum(here + 1, totals.shape[0] // 8 - 1)
+    outer_pull = (
+        totals[below + 4] * (base - totals[below + 3]),
+        totals[above + 2] * (base + totals[8 * here] + totals[above + 1]),
+    )
+    enclosed[...] = local[...] + base
+
+    borders = lines[pl.ds(31, RING, stride=BLOCK), :]
+    square[pl.ds(0, RING, stride=2), :] = pltpu.roll(borders, 32, 1)
     square[pl.ds(1, RING - 1, stride=2), :] = lines[pl.ds(BLOCK + 31, RING - 1, stride=BLOCK), :]
     square[pl.ds(127, 1), :] = lines[pl.ds(31, 1), :]
     across = square[...].T
@@ -179,12 +230,15 @@
             line < split, rates[first_rate + SPAN * first + row], rates[first_rate + SPAN * second + row]
         )
 
+    def pull(row):
+        return rates[2 * ROWS + row] * (base + rates[3 * ROWS + row])
+
     def pulls(row, tile):
         first, second, _ = TILES[tile]
-        other = jnp.where(takes[tile][1], rates[2 * ROWS + 1 + SPAN * second + row], 0.0)
+        other = jnp.where(takes[tile][1], pull(SPAN * second + row), 0.0)
         if takes[tile][0] is None:
             return other
-        return jnp.where(takes[tile][0], rates[2 * ROWS + 1 + SPAN * first + row], other)
+        return jnp.where(takes[tile][0], pull(SPAN * first + row), other)
 
     def source(value, rate):
         return value - rate * pltpu.roll(value, 1, 0)
@@ -230,7 +284,7 @@
             ends[pl.ds(8 * (4 * side + 2 * layer + half) + place, 1), :] = cells
 
     def outer(side):
-        rate = jnp.where(takes[0][0], rates[2 * ROWS + (ROWS + 1) * side], 0.0)
+        rate = jnp.where(takes[0][0], outer_pull[side], 0.0)
         return [source(ends[pl.ds(32 * side + 8 * i, 8), :], rate) for i in range(4)]
 
     last, last_partial = begin(SPAN - 1)
@@ -257,19 +311,36 @@
             under, full, partial = full, over, later
         return under, full, partial
 
-    under, full, partial = lax.fori_loop(0, SPAN // 2 - 1, rows, (under, full, partial))
-    last = kept(64)
-    end(SPAN - 2, partial, under, last)
-    end(SPAN - 1, kept(128), full, kept(192))
-
-    for place, field in enumerate(ORDER):
-        for layer in range(2):
-            for group in range(GROUPS):
-                for half in range(2):
-                    first = BLOCK * layer + HALF * half + 5 * group + place
-                    updated[field, layer, pl.ds(SPAN * group, SPAN), pl.ds(128 * half, 128)] = done[
-                        pl.ds(first, SPAN, stride=2 * BLOCK), :
-                    ]
+    def copies_of(part):
+        for group in range(GROUPS):
+            at = pl.ds(SPAN * group + 8 * part, 8)
+            yield pltpu.make_async_copy(
+                out.at[:, :, at, :], updated.at[:, :, at, :], sems.at[GROUPS * part + group]
+            )
+
+    def send(part):
+        for place, field in enumerate(ORDER):
+            for layer in range(2):
+                for group in range(GROUPS):
+                    for half in range(2):
+                        first = 16 * BLOCK * part + BLOCK * layer + HALF * half + 5 * group + place
+                        out[field, layer, pl.ds(SPAN * group + 8 * part, 8), pl.ds(128 * half, 128)] = done[
+                            pl.ds(first, 8, stride=2 * BLOCK), :
+                        ]
+        for copy in copies_of(part):
+            copy.start()
+
+    state = under, full, partial
+    for part in range(PARTS):
+        state = lax.fori_loop(4 * part, min(4 * part + 4, SPAN // 2 - 1), rows, state)
+        if part == PARTS - 1:
+            under, full, partial = state
+            end(SPAN - 2, partial, under, kept(64))
+            end(SPAN - 1, kept(128), full, kept(192))
+        send(part)
+    for part in range(PARTS):
+        for copy in copies_of(part):
+            copy.wait()
 
 
 def specs(*kinds):
@@ -279,10 +350,9 @@
 def shards(fields, shifts, cycle_area, gravity, kappa_az, kappa_rad):
     vmem, smem = pltpu.VMEM, pltpu.SMEM
     params = pltpu.CompilerParams(vmem_limit_bytes=VMEM_LIMIT)
-    blocks = jax.ShapeDtypeStruct((RING * BLOCK, 128), jnp.float32)
+    blocks = jax.ShapeDtypeStruct((RING, BLOCK, 128), jnp.float32)
 
     def dealt(lines):
-        lines = lines.reshape(RING, BLOCK, 128)
         return lax.all_to_all(lines, "az", 0, 0, tiled=True).reshape(RING * BLOCK, 128)
 
     ranks = lax.axis_size(RAD)
@@ -290,11 +360,13 @@
         pack_kernel,
         out_shape=blocks,
         in_specs=specs(pltpu.HBM, pltpu.HBM),
-        out_specs=specs(vmem)[0],
+        out_specs=specs(pl.ANY)[0],
         scratch_shapes=[
             pltpu.VMEM(fields.shape, jnp.float32),
+            pltpu.VMEM((RING * BLOCK, 128), jnp.float32),
             pltpu.SMEM(shifts.shape, jnp.int32),
-            pltpu.SemaphoreType.DMA((6,)),
+            pltpu.SemaphoreType.DMA((GROUPS * PARTS + 1,)),
+            pltpu.SemaphoreType.DMA((2 * PARTS + 1,)),
         ],
         compiler_params=pltpu.CompilerParams(vmem_limit_bytes=60 * 1024 * 1024),
         name="pack",
@@ -304,6 +376,9 @@
     mine = lax.dynamic_slice(shifts.reshape(GROUPS, SPAN), (0, place // 2), (GROUPS, 1))[:, 0]
     end = jnp.where(place < RING // 2, shifts[ROWS - 1 :], shifts[:1])
     steps = jnp.concatenate([mine, end, place[None]])
+    rates = jnp.concatenate([kappa_az, kappa_rad, gravity, cycle_area])
+    steps, rates = lax.optimization_barrier((steps, rates))
+    gravity, cycle_area = rates[2 * ROWS : 3 * ROWS], rates[3 * ROWS :]
     ends = pl.pallas_call(
         ends_kernel,
         out_shape=jax.ShapeDtypeStruct((RING, 128), jnp.float32),
@@ -324,51 +399,57 @@
             jax.ShapeDtypeStruct((8, 128), jnp.float32),
         ),
         in_specs=specs(smem, vmem),
-        out_specs=specs(vmem, vmem, vmem),
-        scratch_shapes=[pltpu.VMEM((2 * RING, 128), jnp.float32)],
+        out_specs=specs(pl.ANY, vmem, vmem),
+        scratch_shapes=[
+            pltpu.VMEM((RING * BLOCK, 128), jnp.float32),
+            pltpu.VMEM((128, 128), jnp.float32),
+            pltpu.SemaphoreType.DMA((PIECES // STEP,)),
+        ],
         compiler_params=params,
         name="shift",
     )(steps, whole)
     moved = pl.pallas_call(
         join_kernel,
-        out_shape=jax.ShapeDtypeStruct((RING, BLOCK, 128), jnp.float32),
+        out_shape=blocks,
         in_specs=specs(vmem, vmem, pl.ANY),
         out_specs=specs(pl.ANY)[0],
         scratch_shapes=[pltpu.VMEM((RING * 8, 128), jnp.float32), pltpu.SemaphoreType.DMA],
         input_output_aliases={2: 0},
         compiler_params=params,
         name="join",
-    )(tail, ends, begun.reshape(RING, BLOCK, 128))
+    )(tail, ends, begun)
     lines = dealt(moved)
 
     row_mass = cycle_area * mass[0, :ROWS] / (2.0 * RING * 256)
-    mine = jnp.stack([row_mass, gravity])
-    everyone = lax.all_gather(lax.all_gather(mine, "core"), "chip").reshape(ranks, 2, ROWS)
-    masses = everyone[:, 0, :]
-    totals = jnp.sum(masses, axis=1)
-    rank = jnp.arange(ranks)
-    offset = jnp.sum(jnp.where(rank[None, :] < rank[:, None], totals[None, :], 0.0), axis=1)
     row = jnp.arange(ROWS)
-    before = jnp.sum(jnp.where(row[None, None, :] < row[None, :, None], masses[:, None, :], 0.0), axis=2)
-    reach = star_mass + offset[:, None] + before + 0.5 * masses
-    pulls = (everyone[:, 1, :] * reach).reshape(ranks * ROWS)
-    me = lax.axis_index(RAD)
-    pull = lax.dynamic_slice(jnp.pad(pulls, (1, 1)), (me * ROWS,), (ROWS + 2,))
-    enclosed = lax.dynamic_slice(reach.reshape(ranks * ROWS), (me * ROWS,), (ROWS,))
-
-    updated = pl.pallas_call(
+    inside = jnp.sum(jnp.where(row[None, :] < row[:, None], row_mass[None, :], 0.0), axis=1)
+    local = inside + 0.5 * row_mass
+    rates = jnp.concatenate([rates[: 3 * ROWS], local])
+    kind, at = jnp.arange(8)[:, None], row[None, :]
+    picked = jnp.where((kind == 1) & (at == 0) | (kind == 3) & (at == ROWS - 1), 0.5 * row_mass[None, :], 0.0)
+    picked = jnp.where((kind == 2) & (at == 0) | (kind == 4) & (at == ROWS - 1), gravity[None, :], picked)
+    ends = jnp.sum(jnp.where(kind == 0, row_mass[None, :], picked), axis=1)
+    ends, local, rates = lax.optimization_barrier((ends, local, rates))
+    totals = lax.all_gather(lax.all_gather(ends, "core"), "chip").reshape(ranks * 8)
+    rank = lax.axis_index(RAD).astype(jnp.int32)[None]
+    updated, enclosed = pl.pallas_call(
         spread_kernel,
-        out_shape=jax.ShapeDtypeStruct(fields.shape, jnp.float32),
-        in_specs=specs(smem, vmem),
-        out_specs=specs(vmem)[0],
+        out_shape=(
+            jax.ShapeDtypeStruct(fields.shape, jnp.float32),
+            jax.ShapeDtypeStruct(gravity.shape, jnp.float32),
+        ),
+        in_specs=specs(smem, smem, smem, vmem, vmem),
+        out_specs=specs(pl.ANY, vmem),
         scratch_shapes=[
             pltpu.VMEM((RING * BLOCK, 128), jnp.float32),
+            pltpu.VMEM(fields.shape, jnp.float32),
             pltpu.VMEM((256, 128), jnp.float32),
             pltpu.VMEM((128, 128), jnp.float32),
+            pltpu.SemaphoreType.DMA((GROUPS * PARTS,)),
         ],
         compiler_params=params,
         name="spread",
-    )(jnp.concatenate([kappa_az, kappa_rad, pull]), lines)
+    )(rank, rates, totals, local, lines)
     return updated, enclosed
 
 

time: 109 us -> 109 us (level)
  blocking collectives: 28.2 us -> 23.3 us
  waiting for transfers between devices: 34.8 us -> 39.6 us
    all_gather x2 -> x1, blocking collectives: 28.2 us -> 20.8 us  [shards(): lax.all_gather(lax.all_gather(ends, 'core'), 'chip').reshape(ranks * 8)]
    all_to_all x2, waiting for transfers between devices: 34.8 us -> 39.6 us  [dealt(): lax.all_to_all(lines, 'az', 0, 0, tiled=True).reshape(RING * BLOCK, 128)]
    unnamed x0 -> x1, blocking collectives: none -> 2.55 us
    unnamed x10 -> x14, local copies, waits for them, and re-layouts: 2.55 us -> 2.84 us
  transfers between devices with their start and end apart: 3 -> 3, of which waited for: 2 -> 2; matrix products, arithmetic and copies ran while one was open for 2% -> 3% of each run, Pallas kernels for 4% -> 4%
where the time goes in v5:
time: 109 us; the launch traced here: 108 us
  waiting for transfers between devices  39.6 us (36%)
  starting transfers between devices  25.2 us (23%)
  blocking collectives  23.3 us (21%)
  Pallas kernels  13.1 us (12%)
  local copies, waits for them, and re-layouts  3.8 us (3%)
  between operations  2.71 us (2%)
    all_to_all x2, waiting for transfers between devices, dealt(): lax.all_to_all(lines, 'az', 0, 0, tiled=True).reshape(RING * BLOCK, 128)  39.6 us
    all_to_all x2, starting transfers between devices, dealt(): lax.all_to_all(lines, 'az', 0, 0, tiled=True).reshape(RING * BLOCK, 128)  23.2 us
    all_gather x1, blocking collectives, shards(): lax.all_gather(lax.all_gather(ends, 'core'), 'chip').reshape(ranks * 8)  20.8 us
    pallas_call x1, Pallas kernels, shards(): pl.pallas_call(spread_kernel, out_shape=(jax.ShapeDtypeStruct(fields.shap...  4.66 us
    pallas_call x1, Pallas kernels, shards(): pl.pallas_call(shift_kernel, out_shape=(blocks, jax.ShapeDtypeStruct((RIN...  4.07 us
    pallas_call x1, Pallas kernels, shards(): pl.pallas_call(pack_kernel, out_shape=blocks, in_specs=specs(pltpu.HBM, p...  3.04 us
    unnamed x14, local copies, waits for them, and re-layouts  2.84 us
    unnamed x1, blocking collectives  2.55 us
  transfers between devices with their start and end apart: 3, of which 2 were waited for; matrix products, arithmetic and copies ran while one was open for 3% of the time, Pallas kernels for 4%

profile of v5, /device:TPU:8, one launch (start us, length us, event | category | flops | bytes accessed | tf_op | source)
XLA Modules:
  0.0 108.3 jit_solution(9717557709117337528)
XLA Ops:
  0.6 3.0 %pack.1 = f32[64,32,128]{2,1,0:T(8,128)} custom-call(s32[96]{0:T(128)} %given.1, f32[5,2,96,256]{3,2,1,0:T(8,128)} %fields.1), custom_call_target="tpu_custom_call" | custom-call | tf_op jit(solution)/shard_map/pack/pallas_call | solution.py:359
  3.7 18.2 %all-to-all-start = ((f32[64,32,128]{2,1,0:T(8,128)}), f32[64,32,128]{2,1,0:T(8,128)S(1)}, u32[]{:S(2)}, u32[]{:S(2)}) async-start(f32[64,32,128]{2,1,0:T(8,128)} %pack.1), calls=%async_computation | async-start | bytes 2097152 | tf_op jit(solution)/shard_map/all_to_all | solution.py:356
  21.8 0.0 copy-start
  21.9 0.6 copy-done
  22.5 0.1 reshape.56
  22.6 0.2 dynamic-slice_reduce_fusion
  22.8 0.6 fusion.1
  24.6 0.0 copy-start.1
  24.7 0.0 copy-start.2
  24.7 0.0 copy-start.3
  24.7 0.0 copy-start.4
  24.7 0.1 pad_add_fusion.steps
  24.8 0.5 copy-done.1
  25.3 0.0 copy-done.2
  25.3 0.0 copy-done.3
  25.3 0.0 copy-done.4
  25.3 0.1 pad_maximum_fusion
  25.4 31.0 %all-to-all-done = f32[64,32,128]{2,1,0:T(8,128)S(1)} async-done(((f32[64,32,128]{2,1,0:T(8,128)}), f32[64,32,128]{2,1,0:T(8,128)S(1)}, u32[]{:S(2)}, u32[]{:S(2)}) %all-to-all-start) | async-done | bytes 1048608 | tf_op jit(solution)/shard_map/all_to_all | solution.py:356
  56.4 0.6 ends.1
  57.0 1.9 %collective-permute-start = (f32[64,128]{1,0:T(8,128)S(1)}, f32[64,128]{1,0:T(8,128)S(1)}, u32[]{:S(2)}, u32[]{:S(2)}) collective-permute-start(f32[64,128]{1,0:T(8,128)S(1)} %ends.1), channel_id=1, source_target_pairs={{0,1},{1,2},{2,3},{3,4},{4,5},{5,6},{6,7},{8,9},{9,10},{10,11},{11... | collective-permute-start | bytes 98312 | tf_op jit(solution)/shard_map/ppermute | solution.py:393
  59.0 4.1 %shift.1 = (f32[64,32,128]{2,1,0:T(8,128)}, f32[512,128]{1,0:T(8,128)S(1)}, f32[8,128]{1,0:T(8,128)S(1)}) custom-call(s32[5]{0:T(128)S(1)} %pad_add_fusion.steps, f32[2048,128]{1,0:T(8,128)S(1)} %bitcast.11), custom_call_target="tpu_custom_call" | custom-call | tf_op jit(solution)/shard_map/shift/pallas_call | solution.py:394
  63.0 0.0 collective-permute-done.ends
  63.0 0.8 join.1
  63.8 5.1 %all-to-all-start.1 = ((f32[64,32,128]{2,1,0:T(8,128)}), f32[64,32,128]{2,1,0:T(8,128)S(1)}, u32[]{:S(2)}, u32[]{:S(2)}) async-start(f32[64,32,128]{2,1,0:T(8,128)} %join.1), calls=%async_computation.1 | async-start | bytes 2097152 | tf_op jit(solution)/shard_map/all_to_all | solution.py:356
  68.9 1.3 %dynamic-slice = u32[1]{0:T(128)} dynamic-slice(u32[512]{0:T(512)} %constant.53, u32[]{:T(128)S(6)} %add.13), dynamic_slice_sizes={1} | dynamic-slice | bytes 12
  70.9 0.1 broadcast_multiply_fusion.1
  70.9 0.1 select_reduce_fusion
  71.1 0.1 pad_maximum_fusion.1.rates
  71.1 0.2 select_reduce_fusion.1
  71.3 0.2 dynamic-update-slice
  71.6 2.5 %all-reduce = f32[16]{0:T(128)S(1)} all-reduce(f32[16]{0:T(128)S(1)} %dynamic-update-slice), channel_id=2, replica_groups=mesh['az'=64,'chip'=4,'core'=2] {'core'}, use_global_device_ids=true, to_apply=%add | all-reduce | flops 16 | bytes 128
  74.1 0.1 reshape.66
  74.2 20.8 %all-gather.2 = f32[4,2,8]{2,1,0:T(2,128)S(1)} all-gather(f32[1,2,8]{2,1,0:T(2,128)S(1)} %reshape.66), channel_id=3, replica_groups=mesh['az'=64,'chip'=4,'core'=2] {'chip'}, dimensions={0}, use_global_device_ids=true | all-gather | bytes 320 | tf_op jit(solution)/shard_map/all_gather | solution.py:433
  95.0 0.1 reshape.58.totals
  95.1 8.5 %all-to-all-done.1 = f32[64,32,128]{2,1,0:T(8,128)S(1)} async-done(((f32[64,32,128]{2,1,0:T(8,128)}), f32[64,32,128]{2,1,0:T(8,128)S(1)}, u32[]{:S(2)}, u32[]{:S(2)}) %all-to-all-start.1) | async-done | bytes 1048608 | tf_op jit(solution)/shard_map/all_to_all | solution.py:356
  103.6 4.7 %spread.1 = (f32[5,2,96,256]{3,2,1,0:T(8,128)}, f32[96]{0:T(128)}) custom-call(s32[1]{0:T(128)} %bitcast.rank, f32[384]{0:T(512)S(1)} %pad_maximum_fusion.1.rates, f32[64]{0:T(128)S(1)} %reshape.58.totals, f32[96]{0:T(128)S(1)} %get-tuple-element.15.local, f32[2048,128]{1,0:T(8,128)S(1)} %bitcast.12), custom_call_target="tpu_custom_call" | custom-call | tf_op jit(solution)/shard_map/spread/pallas_call | solution.py:435
  (6 shorter events, 0.0 us)
Async XLA Ops:
  3.7 52.8 %all-to-all-start = ((f32[64,32,128]{2,1,0:T(8,128)}), f32[64,32,128]{2,1,0:T(8,128)S(1)}, u32[]{:S(2)}, u32[]{:S(2)}) async-start(f32[64,32,128]{2,1,0:T(8,128)} %pack.1), calls=%async_computation | async-start | bytes 2097152 | tf_op jit(solution)/shard_map/all_to_all | solution.py:356
  21.8 0.7 copy-start
  24.6 0.7 copy-start.1
  24.7 0.7 copy-start.2
  24.7 0.7 copy-start.3
  24.7 0.7 copy-start.4
  57.0 6.0 %collective-permute-start = (f32[64,128]{1,0:T(8,128)S(1)}, f32[64,128]{1,0:T(8,128)S(1)}, u32[]{:S(2)}, u32[]{:S(2)}) collective-permute-start(f32[64,128]{1,0:T(8,128)S(1)} %ends.1), channel_id=1, source_target_pairs={{0,1},{1,2},{2,3},{3,4},{4,5},{5,6},{6,7},{8,9},{9,10},{10,11},{11... | collective-permute-start | bytes 98312 | tf_op jit(solution)/shard_map/ppermute | solution.py:393
  63.8 39.8 %all-to-all-start.1 = ((f32[64,32,128]{2,1,0:T(8,128)}), f32[64,32,128]{2,1,0:T(8,128)S(1)}, u32[]{:S(2)}, u32[]{:S(2)}) async-start(f32[64,32,128]{2,1,0:T(8,128)} %join.1), calls=%async_computation.1 | async-start | bytes 2097152 | tf_op jit(solution)/shard_map/all_to_all | solution.py:356

commit v6 on v5

--- a/solution.py
+++ b/solution.py
@@ -17,7 +17,7 @@
 BLOCK = 2 * HALF
 PIECES = 2 * RING
 PARTS = SPAN // 8
-STEP = 8
+STEP = 32
 VMEM_LIMIT = 24 * 1024 * 1024
 
 TILES = ((0, 1, 5), (1, 2, 2))
@@ -82,13 +82,16 @@
         for group in range(GROUPS):
             if (part, group) not in arrived:
                 copies[part, group].wait()
+            taken = {}
             for place, field in enumerate(ORDER):
                 for layer in range(2):
                     for half in range(2):
                         first = 16 * BLOCK * part + BLOCK * layer + HALF * half + 5 * group + place
-                        lines[pl.ds(first, 8, stride=2 * BLOCK), :] = cells[
+                        taken[first] = cells[
                             field, layer, pl.ds(SPAN * group + 8 * part, 8), pl.ds(128 * half, 128)
                         ]
+            for first, value in taken.items():
+                lines[pl.ds(first, 8, stride=2 * BLOCK), :] = value
         send(16 * part, 16, 0, 8)
         send(16 * part, 16, 16, 32)
     halves = [cells[0, z, :, pl.ds(128 * h, 128)] for z in range(2) for h in range(2)]
@@ -126,10 +129,10 @@
     lane, line = iotas()
     blocks = moved.reshape(RING, BLOCK, 128)
 
-    def copy_of(step):
-        part = pl.ds(step * (STEP // 2), STEP // 2)
+    def copy_of(quarter):
+        part = pl.ds(quarter * (RING // 4), RING // 4)
         return pltpu.make_async_copy(
-            blocks.at[part, pl.ds(0, 24), :], begun.at[part, pl.ds(0, 24), :], sems.at[step]
+            blocks.at[part, pl.ds(0, 24), :], begun.at[part, pl.ds(0, 24), :], sems.at[quarter]
         )
 
     whole, part, early = [], [], []
@@ -179,14 +182,18 @@
                 else:
                     at = pl.multiple_of((first_piece + i) * HALF + 8 * tile, 8)
                     moved[pl.ds(at, 8), :] = values[i][tile]
-        copy_of(step).start()
         return before, tuple(edges)
 
     before = tuple(
         tuple(turned(piece_of(PIECES - 1, tile, group), group) for group in TILES[tile][:2]) for tile in range(2)
     )
     zero = jnp.zeros((8, 128), jnp.float32)
-    _, edges = lax.fori_loop(0, PIECES // STEP, several, (before, (zero, zero)))
+    state = before, (zero, zero)
+    steps_each = PIECES // STEP // 4
+    for quarter in range(4):
+        state = lax.fori_loop(steps_each * quarter, steps_each * (quarter + 1), several, state)
+        copy_of(quarter).start()
+    _, edges = state
     square[...] = jnp.concatenate([edges[0], edges[1], jnp.zeros((112, 128), jnp.float32)], axis=0).T
     left = pltpu.roll(square[pl.ds(0, RING, stride=2), :], 96, 1)
     right = square[pl.ds(1, RING, stride=2), :]
@@ -196,12 +203,11 @@
     parts = lines[pl.ds(15, RING, stride=BLOCK), :]
     mass[...] = jnp.broadcast_to(jnp.sum(parts, axis=0, keepdims=True), (8, 128))
 
-    @pl.loop(0, PIECES // STEP)
-    def _(step):
-        copy_of(step).wait()
-
-
-def spread_kernel(rank, rates, totals, local, lines, updated, enclosed, done, out, ends, square, sems):
+    for quarter in range(4):
+        copy_of(quarter).wait()
+
+
+def spread_kernel(rank, rates, totals, local, lines, updated, enclosed, done, ends, square):
     lane, line = iotas()
     here = rank[0]
     base = jnp.float32(star_mass)
@@ -303,44 +309,27 @@
     def kept(first):
         return [ends[pl.ds(first + 8 * i, 8), :] for i in range(8)]
 
-    def rows(pair, state):
+    def rows(step, state):
         under, full, partial = state
-        for row in (2 * pair + 1, 2 * pair + 2):
+        for row in range(30):
+            row = 30 * step + row + 1
             over, later = begin(row)
             end(row - 1, partial, under, over)
             under, full, partial = full, over, later
         return under, full, partial
 
-    def copies_of(part):
-        for group in range(GROUPS):
-            at = pl.ds(SPAN * group + 8 * part, 8)
-            yield pltpu.make_async_copy(
-                out.at[:, :, at, :], updated.at[:, :, at, :], sems.at[GROUPS * part + group]
-            )
-
-    def send(part):
-        for place, field in enumerate(ORDER):
-            for layer in range(2):
-                for group in range(GROUPS):
-                    for half in range(2):
-                        first = 16 * BLOCK * part + BLOCK * layer + HALF * half + 5 * group + place
-                        out[field, layer, pl.ds(SPAN * group + 8 * part, 8), pl.ds(128 * half, 128)] = done[
-                            pl.ds(first, 8, stride=2 * BLOCK), :
-                        ]
-        for copy in copies_of(part):
-            copy.start()
-
-    state = under, full, partial
-    for part in range(PARTS):
-        state = lax.fori_loop(4 * part, min(4 * part + 4, SPAN // 2 - 1), rows, state)
-        if part == PARTS - 1:
-            under, full, partial = state
-            end(SPAN - 2, partial, under, kept(64))
-            end(SPAN - 1, kept(128), full, kept(192))
-        send(part)
-    for part in range(PARTS):
-        for copy in copies_of(part):
-            copy.wait()
+    under, full, partial = lax.fori_loop(0, (SPAN - 2) // 30, rows, (under, full, partial))
+    end(SPAN - 2, partial, under, kept(64))
+    end(SPAN - 1, kept(128), full, kept(192))
+    for place, field in enumerate(ORDER):
+        for layer in range(2):
+            taken = {}
+            for group in range(GROUPS):
+                for half in range(2):
+                    first = BLOCK * layer + HALF * half + 5 * group + place
+                    taken[group, half] = done[pl.ds(first, SPAN, stride=2 * BLOCK), :]
+            for (group, half), value in taken.items():
+                updated[field, layer, pl.ds(SPAN * group, SPAN), pl.ds(128 * half, 128)] = value
 
 
 def specs(*kinds):
@@ -403,7 +392,7 @@
         scratch_shapes=[
             pltpu.VMEM((RING * BLOCK, 128), jnp.float32),
             pltpu.VMEM((128, 128), jnp.float32),
-            pltpu.SemaphoreType.DMA((PIECES // STEP,)),
+            pltpu.SemaphoreType.DMA((4,)),
         ],
         compiler_params=params,
         name="shift",
@@ -439,13 +428,11 @@
             jax.ShapeDtypeStruct(gravity.shape, jnp.float32),
         ),
         in_specs=specs(smem, smem, smem, vmem, vmem),
-        out_specs=specs(pl.ANY, vmem),
+        out_specs=specs(vmem, vmem),
         scratch_shapes=[
             pltpu.VMEM((RING * BLOCK, 128), jnp.float32),
-            pltpu.VMEM(fields.shape, jnp.float32),
             pltpu.VMEM((256, 128), jnp.float32),
             pltpu.VMEM((128, 128), jnp.float32),
-            pltpu.SemaphoreType.DMA((GROUPS * PARTS,)),
         ],
         compiler_params=params,
         name="spread",

time: 109 us -> 105 us (0.963)
  Pallas kernels: 13.1 us -> 9.57 us
  blocking collectives: 23.3 us -> 22.1 us
  waiting for transfers between devices: 39.6 us -> 40.7 us
    pallas_call x1, Pallas kernels: 4.07 us -> 2.1 us  [shards(): pl.pallas_call(shift_kernel, out_shape=(blocks, jax.ShapeDtypeStruct((RIN...]
    pallas_call x1, Pallas kernels: 4.66 us -> 3.1 us  [shards(): pl.pallas_call(spread_kernel, out_shape=(jax.ShapeDtypeStruct(fields.shap...]
    ppermute x1, waiting for transfers between devices: 0.01 us -> 1.2 us  [shards(): ends = lax.ppermute(ends, ('az',) + RAD, outward + inward)]
  transfers between devices with their start and end apart: 3 -> 3, of which waited for: 2 -> 3; matrix products, arithmetic and copies ran while one was open for 3% -> 3% of each run, Pallas kernels for 4% -> 2%
where the time goes in v6:
time: 105 us
  waiting for transfers between devices  40.7 us (39%)
  starting transfers between devices  25.2 us (24%)
  blocking collectives  22.1 us (21%)
  Pallas kernels  9.57 us (9%)
  local copies, waits for them, and re-layouts  3.8 us (4%)
  between operations  2.7 us (3%)
    all_to_all x2, waiting for transfers between devices, dealt(): lax.all_to_all(lines, 'az', 0, 0, tiled=True).reshape(RING * BLOCK, 128)  39.5 us
    all_to_all x2, starting transfers between devices, dealt(): lax.all_to_all(lines, 'az', 0, 0, tiled=True).reshape(RING * BLOCK, 128)  23.2 us
    all_gather x1, blocking collectives, shards(): lax.all_gather(lax.all_gather(ends, 'core'), 'chip').reshape(ranks * 8)  19.7 us
    pallas_call x1, Pallas kernels, shards(): pl.pallas_call(spread_kernel, out_shape=(jax.ShapeDtypeStruct(fields.shap...  3.1 us
    pallas_call x1, Pallas kernels, shards(): pl.pallas_call(pack_kernel, out_shape=blocks, in_specs=specs(pltpu.HBM, p...  3.04 us
    unnamed x14, local copies, waits for them, and re-layouts  2.84 us
    unnamed x1, blocking collectives  2.44 us
  transfers between devices with their start and end apart: 3, of which 3 were waited for; matrix products, arithmetic and copies ran while one was open for 3% of the time, Pallas kernels for 2%

profile of v6, /device:TPU:8, one launch (start us, length us, event | category | flops | bytes accessed | tf_op | source)
XLA Modules:
  0.0 104.6 jit_solution(13974161933578632594)
XLA Ops:
  0.6 3.0 %pack.1 = f32[64,32,128]{2,1,0:T(8,128)} custom-call(s32[96]{0:T(128)} %given.1, f32[5,2,96,256]{3,2,1,0:T(8,128)} %fields.1), custom_call_target="tpu_custom_call" | custom-call | tf_op jit(solution)/shard_map/pack/pallas_call | solution.py:348
  3.7 18.2 %all-to-all-start = ((f32[64,32,128]{2,1,0:T(8,128)}), f32[64,32,128]{2,1,0:T(8,128)S(1)}, u32[]{:S(2)}, u32[]{:S(2)}) async-start(f32[64,32,128]{2,1,0:T(8,128)} %pack.1), calls=%async_computation | async-start | bytes 2097152 | tf_op jit(solution)/shard_map/all_to_all | solution.py:345
  21.8 0.0 copy-start
  21.9 0.6 copy-done
  22.5 0.1 reshape.56
  22.6 0.2 dynamic-slice_reduce_fusion
  22.8 0.6 fusion.1
  24.6 0.0 copy-start.1
  24.6 0.0 copy-start.2
  24.7 0.0 copy-start.3
  24.7 0.0 copy-start.4
  24.7 0.1 pad_add_fusion.steps
  24.8 0.5 copy-done.1
  25.3 0.0 copy-done.2
  25.3 0.0 copy-done.3
  25.3 0.0 copy-done.4
  25.3 0.1 pad_maximum_fusion
  25.4 31.0 %all-to-all-done = f32[64,32,128]{2,1,0:T(8,128)S(1)} async-done(((f32[64,32,128]{2,1,0:T(8,128)}), f32[64,32,128]{2,1,0:T(8,128)S(1)}, u32[]{:S(2)}, u32[]{:S(2)}) %all-to-all-start) | async-done | bytes 1048608 | tf_op jit(solution)/shard_map/all_to_all | solution.py:345
  56.4 0.6 ends.1
  57.0 1.9 %collective-permute-start = (f32[64,128]{1,0:T(8,128)S(1)}, f32[64,128]{1,0:T(8,128)S(1)}, u32[]{:S(2)}, u32[]{:S(2)}) collective-permute-start(f32[64,128]{1,0:T(8,128)S(1)} %ends.1), channel_id=1, source_target_pairs={{0,1},{1,2},{2,3},{3,4},{4,5},{5,6},{6,7},{8,9},{9,10},{10,11},{11... | collective-permute-start | bytes 98312 | tf_op jit(solution)/shard_map/ppermute | solution.py:382
  58.9 2.1 %shift.1 = (f32[64,32,128]{2,1,0:T(8,128)}, f32[512,128]{1,0:T(8,128)S(1)}, f32[8,128]{1,0:T(8,128)S(1)}) custom-call(s32[5]{0:T(128)S(1)} %pad_add_fusion.steps, f32[2048,128]{1,0:T(8,128)S(1)} %bitcast.11), custom_call_target="tpu_custom_call" | custom-call | tf_op jit(solution)/shard_map/shift/pallas_call | solution.py:383
  61.1 1.2 %collective-permute-done.ends = f32[64,128]{1,0:T(8,128)S(1)} collective-permute-done((f32[64,128]{1,0:T(8,128)S(1)}, f32[64,128]{1,0:T(8,128)S(1)}, u32[]{:S(2)}, u32[]{:S(2)}) %collective-permute-start) | collective-permute-done | bytes 32800 | tf_op jit(solution)/shard_map/ppermute | solution.py:382
  62.3 0.8 join.1
  63.0 5.1 %all-to-all-start.1 = ((f32[64,32,128]{2,1,0:T(8,128)}), f32[64,32,128]{2,1,0:T(8,128)S(1)}, u32[]{:S(2)}, u32[]{:S(2)}) async-start(f32[64,32,128]{2,1,0:T(8,128)} %join.1), calls=%async_computation.1 | async-start | bytes 2097152 | tf_op jit(solution)/shard_map/all_to_all | solution.py:345
  68.1 1.3 %dynamic-slice = u32[1]{0:T(128)} dynamic-slice(u32[512]{0:T(512)} %constant.53, u32[]{:T(128)S(6)} %add.13), dynamic_slice_sizes={1} | dynamic-slice | bytes 12
  70.1 0.1 broadcast_multiply_fusion.1
  70.2 0.1 select_reduce_fusion
  70.3 0.1 pad_maximum_fusion.1.rates
  70.4 0.2 select_reduce_fusion.1
  70.6 0.2 dynamic-update-slice
  70.8 2.4 %all-reduce = f32[16]{0:T(128)S(1)} all-reduce(f32[16]{0:T(128)S(1)} %dynamic-update-slice), channel_id=2, replica_groups=mesh['az'=64,'chip'=4,'core'=2] {'core'}, use_global_device_ids=true, to_apply=%add | all-reduce | flops 16 | bytes 128
  73.2 0.1 reshape.66
  73.3 19.7 %all-gather.2 = f32[4,2,8]{2,1,0:T(2,128)S(1)} all-gather(f32[1,2,8]{2,1,0:T(2,128)S(1)} %reshape.66), channel_id=3, replica_groups=mesh['az'=64,'chip'=4,'core'=2] {'chip'}, dimensions={0}, use_global_device_ids=true | all-gather | bytes 320 | tf_op jit(solution)/shard_map/all_gather | solution.py:422
  93.0 0.1 reshape.58.totals
  93.1 8.5 %all-to-all-done.1 = f32[64,32,128]{2,1,0:T(8,128)S(1)} async-done(((f32[64,32,128]{2,1,0:T(8,128)}), f32[64,32,128]{2,1,0:T(8,128)S(1)}, u32[]{:S(2)}, u32[]{:S(2)}) %all-to-all-start.1) | async-done | bytes 1048608 | tf_op jit(solution)/shard_map/all_to_all | solution.py:345
  101.5 3.1 %spread.1 = (f32[5,2,96,256]{3,2,1,0:T(8,128)}, f32[96]{0:T(128)}) custom-call(s32[1]{0:T(128)} %bitcast.rank, f32[384]{0:T(512)S(1)} %pad_maximum_fusion.1.rates, f32[64]{0:T(128)S(1)} %reshape.58.totals, f32[96]{0:T(128)S(1)} %get-tuple-element.15.local, f32[2048,128]{1,0:T(8,128)S(1)} %bitcast.12), custom_call_target="tpu_custom_call" | custom-call | tf_op jit(solution)/shard_map/spread/pallas_call | solution.py:424
  (6 shorter events, 0.0 us)
Async XLA Ops:
  3.7 52.8 %all-to-all-start = ((f32[64,32,128]{2,1,0:T(8,128)}), f32[64,32,128]{2,1,0:T(8,128)S(1)}, u32[]{:S(2)}, u32[]{:S(2)}) async-start(f32[64,32,128]{2,1,0:T(8,128)} %pack.1), calls=%async_computation | async-start | bytes 2097152 | tf_op jit(solution)/shard_map/all_to_all | solution.py:345
  21.8 0.7 copy-start
  24.6 0.7 copy-start.1
  24.6 0.7 copy-start.2
  24.7 0.7 copy-start.3
  24.7 0.7 copy-start.4
  57.0 5.2 %collective-permute-start = (f32[64,128]{1,0:T(8,128)S(1)}, f32[64,128]{1,0:T(8,128)S(1)}, u32[]{:S(2)}, u32[]{:S(2)}) collective-permute-start(f32[64,128]{1,0:T(8,128)S(1)} %ends.1), channel_id=1, source_target_pairs={{0,1},{1,2},{2,3},{3,4},{4,5},{5,6},{6,7},{8,9},{9,10},{10,11},{11... | collective-permute-start | bytes 98312 | tf_op jit(solution)/shard_map/ppermute | solution.py:382
  63.0 38.5 %all-to-all-start.1 = ((f32[64,32,128]{2,1,0:T(8,128)}), f32[64,32,128]{2,1,0:T(8,128)S(1)}, u32[]{:S(2)}, u32[]{:S(2)}) async-start(f32[64,32,128]{2,1,0:T(8,128)} %join.1), calls=%async_computation.1 | async-start | bytes 2097152 | tf_op jit(solution)/shard_map/all_to_all | solution.py:345

commit v7 on v6

--- a/solution.py
+++ b/solution.py
@@ -54,21 +54,21 @@
     for at in arrived:
         copies[at].wait()
     shift_copy.wait()
+    turned = {}
+    for side in range(2):
+        row = (ROWS - 1) * (1 - side)
+        part = shifts[row] & 127
+        for layer in range(2):
+            for half in range(2):
+                tile = jnp.zeros((8, 128), jnp.float32)
+                for place, field in enumerate(ORDER):
+                    cell = cells[field, layer, pl.ds(row, 1), pl.ds(128 * half, 128)]
+                    tile = jnp.where(line == place, jnp.broadcast_to(cell, (8, 128)), tile)
+                turned[side, layer, half] = pltpu.roll(tile, part, 1)
     for side, layer, half, first in windows():
-        row = (ROWS - 1) * (1 - side)
-        part, odd = shifts[row] & 127, shifts[row] & 128
-        tile = jnp.zeros((8, 128), jnp.float32)
-        for place, field in enumerate(ORDER):
-            low, high = (
-                pltpu.roll(jnp.broadcast_to(cells[field, layer, pl.ds(row, 1), pl.ds(at, 128)], (8, 128)), part, 1)
-                for at in (0, 128)
-            )
-            chosen = jnp.where((lane < part) ^ (odd != 0) ^ (half == 1), high, low)
-            turned = pltpu.roll(chosen, 16 * (place + 1), 1)
-            for bit in (1, 2, 4):
-                turned = jnp.where(line & bit == 0, turned, pltpu.roll(turned, 128 - 16 * bit, 1))
-            tile = jnp.where(lane >> 4 == place + 1, turned, tile)
-        lines[pl.ds(first, 8, stride=BLOCK), :] = tile
+        shift = shifts[(ROWS - 1) * (1 - side)]
+        swapped = (lane < (shift & 127)) ^ (shift & 128 != 0) ^ (half == 1)
+        lines[pl.ds(first, 8, stride=BLOCK), :] = jnp.where(swapped, turned[side, layer, 1], turned[side, layer, 0])
     blocks = lines.reshape(RING, BLOCK, 128)
     sending = []
 
@@ -110,31 +110,22 @@
     twice[pl.ds(RING, RING), :] = cells
     shift = steps[3]
     lane = lax.broadcasted_iota(jnp.int32, (RING, 128), 1)
-    crossed = (lane & 15) + 16 * (steps[4] & 15) < (shift & 255)
+    crossed = lane + 16 * (steps[4] & 8) < (shift & 255)
     blocks = shift >> 8
     moved[...] = jnp.where(crossed, twice[pl.ds(RING - 1 - blocks, RING), :], twice[pl.ds(RING - blocks, RING), :])
 
 
 def join_kernel(tail, ends, begun, moved, rows, sem):
     rows[...] = tail[...]
-    lane = lax.broadcasted_iota(jnp.int32, (RING, 128), 1)
-    last = pl.ds(7, RING, stride=8)
-    rows[last, :] = jnp.where((lane < 16) | (lane >= 96), tail[last, :], ends[...])
+    rows[pl.ds(7, RING, stride=8), :] = ends[...]
     copy = pltpu.make_async_copy(rows.reshape(RING, 8, 128), moved.at[:, pl.ds(24, 8), :], sem)
     copy.start()
     copy.wait()
 
 
-def shift_kernel(steps, lines, begun, tail, mass, moved, square, sems):
+def shift_kernel(steps, lines, begun, tail, mass, square):
     lane, line = iotas()
-    blocks = moved.reshape(RING, BLOCK, 128)
-
-    def copy_of(quarter):
-        part = pl.ds(quarter * (RING // 4), RING // 4)
-        return pltpu.make_async_copy(
-            blocks.at[part, pl.ds(0, 24), :], begun.at[part, pl.ds(0, 24), :], sems.at[quarter]
-        )
-
+    moved = begun.reshape(RING * BLOCK, 128)
     whole, part, early = [], [], []
     for group in range(GROUPS):
         shift = steps[group]
@@ -192,19 +183,15 @@
     steps_each = PIECES // STEP // 4
     for quarter in range(4):
         state = lax.fori_loop(steps_each * quarter, steps_each * (quarter + 1), several, state)
-        copy_of(quarter).start()
     _, edges = state
     square[...] = jnp.concatenate([edges[0], edges[1], jnp.zeros((112, 128), jnp.float32)], axis=0).T
-    left = pltpu.roll(square[pl.ds(0, RING, stride=2), :], 96, 1)
+    left = square[pl.ds(0, RING, stride=2), :]
     right = square[pl.ds(1, RING, stride=2), :]
     left = jnp.concatenate([left[RING - 1 :], left[: RING - 1]], axis=0)
     right = jnp.concatenate([right[1:], right[:1]], axis=0)
-    tail[pl.ds(7, RING, stride=8), :] = left + right
+    moved[pl.ds(15, RING, stride=BLOCK), :] = left + pltpu.roll(right, 16, 1)
     parts = lines[pl.ds(15, RING, stride=BLOCK), :]
     mass[...] = jnp.broadcast_to(jnp.sum(parts, axis=0, keepdims=True), (8, 128))
-
-    for quarter in range(4):
-        copy_of(quarter).wait()
 
 
 def spread_kernel(rank, rates, totals, local, lines, updated, enclosed, done, ends, square):
@@ -221,10 +208,10 @@
     )
     enclosed[...] = local[...] + base
 
-    borders = lines[pl.ds(31, RING, stride=BLOCK), :]
-    square[pl.ds(0, RING, stride=2), :] = pltpu.roll(borders, 32, 1)
-    square[pl.ds(1, RING - 1, stride=2), :] = lines[pl.ds(BLOCK + 31, RING - 1, stride=BLOCK), :]
-    square[pl.ds(127, 1), :] = lines[pl.ds(31, 1), :]
+    borders = lines[pl.ds(15, RING, stride=BLOCK), :]
+    square[pl.ds(0, RING, stride=2), :] = borders
+    borders = pltpu.roll(borders, 112, 1)
+    square[pl.ds(1, RING, stride=2), :] = jnp.concatenate([borders[1:], borders[:1]], axis=0)
     across = square[...].T
     edges = across[0:8], across[8:16]
     under_edges = tuple(pltpu.roll(value, 1, 0) for value in edges)
@@ -281,17 +268,11 @@
                     at = 4 * tile + 2 * layer + half
                     done[pl.ds(place_of(row, tile, layer, half), 8), :] = partial[at] + rad * (under[at] + over[at])
 
-    ends[...] = jnp.zeros(ends.shape, jnp.float32)
-    for side, layer, half, first in windows():
-        tile = lines[pl.ds(first, 8, stride=BLOCK), :]
-        for place in range(5):
-            turned = pltpu.roll(pltpu.roll(tile, 112 - 16 * place, 1), 0, 1, stride=16, stride_axis=0)
-            cells = jnp.sum(jnp.where(lane >> 4 == line, turned, 0.0), axis=0, keepdims=True)
-            ends[pl.ds(8 * (4 * side + 2 * layer + half) + place, 1), :] = cells
-
     def outer(side):
         rate = jnp.where(takes[0][0], outer_pull[side], 0.0)
-        return [source(ends[pl.ds(32 * side + 8 * i, 8), :], rate) for i in range(4)]
+        return [
+            source(lines[pl.ds(first, 8, stride=BLOCK), :], rate) for at, _, _, first in windows() if at == side
+        ]
 
     last, last_partial = begin(SPAN - 1)
     full, partial = begin(0)
@@ -388,12 +369,8 @@
             jax.ShapeDtypeStruct((8, 128), jnp.float32),
         ),
         in_specs=specs(smem, vmem),
-        out_specs=specs(pl.ANY, vmem, vmem),
-        scratch_shapes=[
-            pltpu.VMEM((RING * BLOCK, 128), jnp.float32),
-            pltpu.VMEM((128, 128), jnp.float32),
-            pltpu.SemaphoreType.DMA((4,)),
-        ],
+        out_specs=specs(vmem, vmem, vmem),
+        scratch_shapes=[pltpu.VMEM((128, 128), jnp.float32)],
         compiler_params=params,
         name="shift",
     )(steps, whole)

time: 105 us -> 105 us (level)
  no operation moved by 1% of the time
where the time goes in v7:
time: 105 us; the launch traced here: 104 us
  waiting for transfers between devices  40.2 us (38%)
  starting transfers between devices  25.2 us (24%)
  blocking collectives  22.6 us (22%)
  Pallas kernels  9.43 us (9%)
  local copies, waits for them, and re-layouts  3.8 us (4%)
  between operations  2.69 us (3%)
    all_to_all x2, waiting for transfers between devices, dealt(): lax.all_to_all(lines, 'az', 0, 0, tiled=True).reshape(RING * BLOCK, 128)  39.5 us
    all_to_all x2, starting transfers between devices, dealt(): lax.all_to_all(lines, 'az', 0, 0, tiled=True).reshape(RING * BLOCK, 128)  23.2 us
    all_gather x1, blocking collectives, shards(): lax.all_gather(lax.all_gather(ends, 'core'), 'chip').reshape(ranks * 8)  20.2 us
    pallas_call x1, Pallas kernels, shards(): pl.pallas_call(spread_kernel, out_shape=(jax.ShapeDtypeStruct(fields.shap...  2.84 us
    unnamed x14, local copies, waits for them, and re-layouts  2.84 us
    pallas_call x1, Pallas kernels, shards(): pl.pallas_call(pack_kernel, out_shape=blocks, in_specs=specs(pltpu.HBM, p...  2.65 us
    pallas_call x1, Pallas kernels, shards(): pl.pallas_call(shift_kernel, out_shape=(blocks, jax.ShapeDtypeStruct((RIN...  2.6 us
    unnamed x1, blocking collectives  2.44 us
  transfers between devices with their start and end apart: 3, of which 3 were waited for; matrix products, arithmetic and copies ran while one was open for 3% of the time, Pallas kernels for 2%

profile of v7, /device:TPU:8, one launch (start us, length us, event | category | flops | bytes accessed | tf_op | source)
XLA Modules:
  0.0 104.5 jit_solution(18008889852123409368)
XLA Ops:
  0.6 2.7 %pack.1 = f32[64,32,128]{2,1,0:T(8,128)} custom-call(s32[96]{0:T(128)} %given.1, f32[5,2,96,256]{3,2,1,0:T(8,128)} %fields.1), custom_call_target="tpu_custom_call" | custom-call | tf_op jit(solution)/shard_map/pack/pallas_call | solution.py:329
  3.3 18.2 %all-to-all-start = ((f32[64,32,128]{2,1,0:T(8,128)}), f32[64,32,128]{2,1,0:T(8,128)S(1)}, u32[]{:S(2)}, u32[]{:S(2)}) async-start(f32[64,32,128]{2,1,0:T(8,128)} %pack.1), calls=%async_computation | async-start | bytes 2097152 | tf_op jit(solution)/shard_map/all_to_all | solution.py:326
  21.5 0.0 copy-start
  21.5 0.6 copy-done
  22.1 0.1 reshape.56
  22.2 0.2 dynamic-slice_reduce_fusion
  22.4 0.6 fusion.1
  24.3 0.0 copy-start.1
  24.3 0.0 copy-start.2
  24.3 0.0 copy-start.3
  24.3 0.0 copy-start.4
  24.3 0.1 pad_add_fusion.steps
  24.4 0.5 copy-done.1
  24.9 0.0 copy-done.2
  24.9 0.0 copy-done.3
  24.9 0.0 copy-done.4
  25.0 0.1 pad_maximum_fusion
  25.0 31.0 %all-to-all-done = f32[64,32,128]{2,1,0:T(8,128)S(1)} async-done(((f32[64,32,128]{2,1,0:T(8,128)}), f32[64,32,128]{2,1,0:T(8,128)S(1)}, u32[]{:S(2)}, u32[]{:S(2)}) %all-to-all-start) | async-done | bytes 1048608 | tf_op jit(solution)/shard_map/all_to_all | solution.py:326
  56.0 0.6 ends.1
  56.6 1.9 %collective-permute-start = (f32[64,128]{1,0:T(8,128)S(1)}, f32[64,128]{1,0:T(8,128)S(1)}, u32[]{:S(2)}, u32[]{:S(2)}) collective-permute-start(f32[64,128]{1,0:T(8,128)S(1)} %ends.1), channel_id=1, source_target_pairs={{0,1},{1,2},{2,3},{3,4},{4,5},{5,6},{6,7},{8,9},{9,10},{10,11},{11... | collective-permute-start | bytes 98312 | tf_op jit(solution)/shard_map/ppermute | solution.py:363
  58.6 2.6 %shift.1 = (f32[64,32,128]{2,1,0:T(8,128)}, f32[512,128]{1,0:T(8,128)S(1)}, f32[8,128]{1,0:T(8,128)S(1)}) custom-call(s32[5]{0:T(128)S(1)} %pad_add_fusion.steps, f32[2048,128]{1,0:T(8,128)S(1)} %bitcast.11), custom_call_target="tpu_custom_call" | custom-call | tf_op jit(solution)/shard_map/shift/pallas_call | solution.py:364
  61.2 0.7 collective-permute-done.ends
  61.9 0.7 join.1
  62.6 5.1 %all-to-all-start.1 = ((f32[64,32,128]{2,1,0:T(8,128)}), f32[64,32,128]{2,1,0:T(8,128)S(1)}, u32[]{:S(2)}, u32[]{:S(2)}) async-start(f32[64,32,128]{2,1,0:T(8,128)} %join.1), calls=%async_computation.1 | async-start | bytes 2097152 | tf_op jit(solution)/shard_map/all_to_all | solution.py:326
  67.7 1.3 %dynamic-slice = u32[1]{0:T(128)} dynamic-slice(u32[512]{0:T(512)} %constant.53, u32[]{:T(128)S(6)} %add.13), dynamic_slice_sizes={1} | dynamic-slice | bytes 12
  69.7 0.1 broadcast_multiply_fusion.1
  69.8 0.1 select_reduce_fusion
  69.9 0.1 pad_maximum_fusion.1.rates
  70.0 0.2 select_reduce_fusion.1
  70.2 0.2 dynamic-update-slice
  70.4 2.4 %all-reduce = f32[16]{0:T(128)S(1)} all-reduce(f32[16]{0:T(128)S(1)} %dynamic-update-slice), channel_id=2, replica_groups=mesh['az'=64,'chip'=4,'core'=2] {'core'}, use_global_device_ids=true, to_apply=%add | all-reduce | flops 16 | bytes 128
  72.9 0.1 reshape.66
  72.9 20.2 %all-gather.2 = f32[4,2,8]{2,1,0:T(2,128)S(1)} all-gather(f32[1,2,8]{2,1,0:T(2,128)S(1)} %reshape.66), channel_id=3, replica_groups=mesh['az'=64,'chip'=4,'core'=2] {'chip'}, dimensions={0}, use_global_device_ids=true | all-gather | bytes 320 | tf_op jit(solution)/shard_map/all_gather | solution.py:399
  93.1 0.1 reshape.58.totals
  93.2 8.5 %all-to-all-done.1 = f32[64,32,128]{2,1,0:T(8,128)S(1)} async-done(((f32[64,32,128]{2,1,0:T(8,128)}), f32[64,32,128]{2,1,0:T(8,128)S(1)}, u32[]{:S(2)}, u32[]{:S(2)}) %all-to-all-start.1) | async-done | bytes 1048608 | tf_op jit(solution)/shard_map/all_to_all | solution.py:326
  101.6 2.8 %spread.1 = (f32[5,2,96,256]{3,2,1,0:T(8,128)}, f32[96]{0:T(128)}) custom-call(s32[1]{0:T(128)} %bitcast.rank, f32[384]{0:T(512)S(1)} %pad_maximum_fusion.1.rates, f32[64]{0:T(128)S(1)} %reshape.58.totals, f32[96]{0:T(128)S(1)} %get-tuple-element.15.local, f32[2048,128]{1,0:T(8,128)S(1)} %bitcast.12), custom_call_target="tpu_custom_call" | custom-call | tf_op jit(solution)/shard_map/spread/pallas_call | solution.py:401
  (6 shorter events, 0.0 us)
Async XLA Ops:
  3.3 52.8 %all-to-all-start = ((f32[64,32,128]{2,1,0:T(8,128)}), f32[64,32,128]{2,1,0:T(8,128)S(1)}, u32[]{:S(2)}, u32[]{:S(2)}) async-start(f32[64,32,128]{2,1,0:T(8,128)} %pack.1), calls=%async_computation | async-start | bytes 2097152 | tf_op jit(solution)/shard_map/all_to_all | solution.py:326
  21.5 0.7 copy-start
  24.3 0.7 copy-start.1
  24.3 0.7 copy-start.2
  24.3 0.7 copy-start.3
  24.3 0.7 copy-start.4
  56.6 5.2 %collective-permute-start = (f32[64,128]{1,0:T(8,128)S(1)}, f32[64,128]{1,0:T(8,128)S(1)}, u32[]{:S(2)}, u32[]{:S(2)}) collective-permute-start(f32[64,128]{1,0:T(8,128)S(1)} %ends.1), channel_id=1, source_target_pairs={{0,1},{1,2},{2,3},{3,4},{4,5},{5,6},{6,7},{8,9},{9,10},{10,11},{11... | collective-permute-start | bytes 98312 | tf_op jit(solution)/shard_map/ppermute | solution.py:363
  62.6 39.0 %all-to-all-start.1 = ((f32[64,32,128]{2,1,0:T(8,128)}), f32[64,32,128]{2,1,0:T(8,128)S(1)}, u32[]{:S(2)}, u32[]{:S(2)}) async-start(f32[64,32,128]{2,1,0:T(8,128)} %join.1), calls=%async_computation.1 | async-start | bytes 2097152 | tf_op jit(solution)/shard_map/all_to_all | solution.py:326

commit v8 on v7

--- a/solution.py
+++ b/solution.py
@@ -104,20 +104,16 @@
         copy.wait()
 
 
-def ends_kernel(steps, lines, moved, twice):
-    cells = lines[pl.ds(31, RING, stride=BLOCK), :]
-    twice[pl.ds(0, RING), :] = cells
-    twice[pl.ds(RING, RING), :] = cells
-    shift = steps[3]
+def join_kernel(steps, near, tail, ends, begun, moved, rows, twice, sem):
+    twice[pl.ds(0, RING), :] = ends[...]
+    twice[pl.ds(RING, RING), :] = ends[...]
+    rows[...] = tail[...]
     lane = lax.broadcasted_iota(jnp.int32, (RING, 128), 1)
-    crossed = lane + 16 * (steps[4] & 8) < (shift & 255)
-    blocks = shift >> 8
-    moved[...] = jnp.where(crossed, twice[pl.ds(RING - 1 - blocks, RING), :], twice[pl.ds(RING - blocks, RING), :])
-
-
-def join_kernel(tail, ends, begun, moved, rows, sem):
-    rows[...] = tail[...]
-    rows[pl.ds(7, RING, stride=8), :] = ends[...]
+    crossed = lane + 16 * (steps[3] & 8) < (near[0] & 255)
+    blocks = near[0] >> 8
+    rows[pl.ds(7, RING, stride=8), :] = jnp.where(
+        crossed, twice[pl.ds(RING - 1 - blocks, RING), :], twice[pl.ds(RING - blocks, RING), :]
+    )
     copy = pltpu.make_async_copy(rows.reshape(RING, 8, 128), moved.at[:, pl.ds(24, 8), :], sem)
     copy.start()
     copy.wait()
@@ -345,22 +341,14 @@
     place = lax.axis_index("az").astype(jnp.int32)
     mine = lax.dynamic_slice(shifts.reshape(GROUPS, SPAN), (0, place // 2), (GROUPS, 1))[:, 0]
     end = jnp.where(place < RING // 2, shifts[ROWS - 1 :], shifts[:1])
-    steps = jnp.concatenate([mine, end, place[None]])
+    steps = jnp.concatenate([mine, place[None]])
     rates = jnp.concatenate([kappa_az, kappa_rad, gravity, cycle_area])
     steps, rates = lax.optimization_barrier((steps, rates))
     gravity, cycle_area = rates[2 * ROWS : 3 * ROWS], rates[3 * ROWS :]
-    ends = pl.pallas_call(
-        ends_kernel,
-        out_shape=jax.ShapeDtypeStruct((RING, 128), jnp.float32),
-        in_specs=specs(smem, vmem),
-        out_specs=specs(vmem)[0],
-        scratch_shapes=[pltpu.VMEM((2 * RING, 128), jnp.float32)],
-        compiler_params=params,
-        name="ends",
-    )(steps, whole)
     outward = [(q * ranks + i, q * ranks + i + 1) for q in range(RING // 2) for i in range(ranks - 1)]
     inward = [(q * ranks + i + 1, q * ranks + i) for q in range(RING // 2, RING) for i in range(ranks - 1)]
-    ends = lax.ppermute(ends, ("az",) + RAD, outward + inward)
+    near = lax.ppermute(end, ("az",) + RAD, outward + inward)
+    ends = lax.ppermute(whole.reshape(RING, BLOCK, 128)[:, BLOCK - 1], ("az",) + RAD, outward + inward)
     begun, tail, mass = pl.pallas_call(
         shift_kernel,
         out_shape=(
@@ -377,13 +365,17 @@
     moved = pl.pallas_call(
         join_kernel,
         out_shape=blocks,
-        in_specs=specs(vmem, vmem, pl.ANY),
+        in_specs=specs(smem, smem, vmem, vmem, pl.ANY),
         out_specs=specs(pl.ANY)[0],
-        scratch_shapes=[pltpu.VMEM((RING * 8, 128), jnp.float32), pltpu.SemaphoreType.DMA],
-        input_output_aliases={2: 0},
+        scratch_shapes=[
+            pltpu.VMEM((RING * 8, 128), jnp.float32),
+            pltpu.VMEM((2 * RING, 128), jnp.float32),
+            pltpu.SemaphoreType.DMA,
+        ],
+        input_output_aliases={4: 0},
         compiler_params=params,
         name="join",
-    )(tail, ends, begun)
+    )(steps, near, tail, ends, begun)
     lines = dealt(moved)
 
     row_mass = cycle_area * mass[0, :ROWS] / (2.0 * RING * 256)

time: 105 us -> 106 us (level)
  starting transfers between devices: 25.2 us -> 27.9 us
  waiting for transfers between devices: 40.2 us -> 37.6 us
    ppermute x1 -> x2, starting transfers between devices: 1.92 us -> 4.65 us  [the longest x1 2.73 us: shards(): near = lax.ppermute(end, ('az',) + RAD, outward + inward)]
    all_to_all x2, waiting for transfers between devices: 39.5 us -> 37 us  [dealt(): lax.all_to_all(lines, 'az', 0, 0, tiled=True).reshape(RING * BLOCK, 128)]
  transfers between devices with their start and end apart: 3 -> 4, of which waited for: 3 -> 3; matrix products, arithmetic and copies ran while one was open for 3% -> 3% of each run, Pallas kernels for 2% -> 2%
where the time goes in v8:
time: 106 us; the launch traced here: 105 us
  waiting for transfers between devices  37.6 us (35%)
  starting transfers between devices  27.9 us (26%)
  blocking collectives  22.7 us (21%)
  Pallas kernels  10 us (9%)
  local copies, waits for them, and re-layouts  3.74 us (4%)
  between operations  2.65 us (2%)
    all_to_all x2, waiting for transfers between devices, dealt(): lax.all_to_all(lines, 'az', 0, 0, tiled=True).reshape(RING * BLOCK, 128)  37 us
    all_to_all x2, starting transfers between devices, dealt(): lax.all_to_all(lines, 'az', 0, 0, tiled=True).reshape(RING * BLOCK, 128)  23.2 us
    all_gather x1, blocking collectives, shards(): lax.all_gather(lax.all_gather(ends, 'core'), 'chip').reshape(ranks * 8)  20.2 us
    pallas_call x1, Pallas kernels, shards(): pl.pallas_call(spread_kernel, out_shape=(jax.ShapeDtypeStruct(fields.shap...  2.84 us
    unnamed x14, local copies, waits for them, and re-layouts  2.76 us
    ppermute x1, starting transfers between devices, shards(): near = lax.ppermute(end, ('az',) + RAD, outward + inward)  2.73 us
    pallas_call x1, Pallas kernels, shards(): pl.pallas_call(pack_kernel, out_shape=blocks, in_specs=specs(pltpu.HBM, p...  2.65 us
    pallas_call x1, Pallas kernels, shards(): pl.pallas_call(shift_kernel, out_shape=(blocks, jax.ShapeDtypeStruct((RIN...  2.59 us
  transfers between devices with their start and end apart: 4, of which 3 were waited for; matrix products, arithmetic and copies ran while one was open for 3% of the time, Pallas kernels for 2%

profile of v8, /device:TPU:8, one launch (start us, length us, event | category | flops | bytes accessed | tf_op | source)
XLA Modules:
  0.0 105.2 jit_solution(939544107620997516)
XLA Ops:
  0.6 2.7 %pack.1 = f32[64,32,128]{2,1,0:T(8,128)} custom-call(s32[96]{0:T(128)} %given.1, f32[5,2,96,256]{3,2,1,0:T(8,128)} %fields.1), custom_call_target="tpu_custom_call" | custom-call | tf_op jit(solution)/shard_map/pack/pallas_call | solution.py:325
  3.3 18.2 %all-to-all-start = ((f32[64,32,128]{2,1,0:T(8,128)}), f32[64,32,128]{2,1,0:T(8,128)S(1)}, u32[]{:S(2)}, u32[]{:S(2)}) async-start(f32[64,32,128]{2,1,0:T(8,128)} %pack.1), calls=%async_computation | async-start | bytes 2097152 | tf_op jit(solution)/shard_map/all_to_all | solution.py:322
  21.5 0.0 copy-start
  21.5 0.6 copy-done
  22.1 0.6 fusion.1
  24.0 2.7 %collective-permute-start = (s32[1]{0:T(128)}, s32[1]{0:T(128)}, u32[]{:S(2)}, u32[]{:S(2)}) collective-permute-start(s32[1]{0:T(128)} %select_n.39), channel_id=1, source_target_pairs={{0,1},{1,2},{2,3},{3,4},{4,5},{5,6},{6,7},{8,9},{9,10},{10,11},{11... | collective-permute-start | bytes 20 | tf_op jit(solution)/shard_map/ppermute | solution.py:350
  26.7 0.1 reshape.56
  26.8 0.0 copy-start.1
  26.8 0.0 copy-start.2
  26.8 0.0 copy-start.3
  26.8 0.0 copy-start.4
  26.8 0.2 dynamic-slice_reduce_fusion
  27.0 0.5 copy-done.1
  27.4 0.0 copy-done.2
  27.4 0.0 copy-done.3
  27.5 0.0 copy-done.4
  27.5 0.1 pad_maximum_fusion
  27.6 28.5 %all-to-all-done = f32[64,32,128]{2,1,0:T(8,128)S(1)} async-done(((f32[64,32,128]{2,1,0:T(8,128)}), f32[64,32,128]{2,1,0:T(8,128)S(1)}, u32[]{:S(2)}, u32[]{:S(2)}) %all-to-all-start) | async-done | bytes 1048608 | tf_op jit(solution)/shard_map/all_to_all | solution.py:322
  56.1 1.9 %collective-permute-start.1 = (f32[64,128]{1,0:T(8,128)S(1)}, f32[64,128]{1,0:T(8,128)S(1)}, u32[]{:S(2)}, u32[]{:S(2)}) collective-permute-start(f32[64,128]{1,0:T(8,128)S(1)} %bitcast.15), channel_id=1, source_target_pairs={{0,1},{1,2},{2,3},{3,4},{4,5},{5,6},{6,7},{8,9},{9,10},{10,11},{11... | collective-permute-start | bytes 98312 | tf_op jit(solution)/shard_map/ppermute | solution.py:351
  58.0 0.1 pad_add_fusion.steps
  58.1 2.6 %shift.1 = (f32[64,32,128]{2,1,0:T(8,128)}, f32[512,128]{1,0:T(8,128)S(1)}, f32[8,128]{1,0:T(8,128)S(1)}) custom-call(s32[4]{0:T(128)S(1)} %pad_add_fusion.steps, f32[2048,128]{1,0:T(8,128)S(1)} %bitcast.13), custom_call_target="tpu_custom_call" | custom-call | tf_op jit(solution)/shard_map/shift/pallas_call | solution.py:352
  60.7 0.0 collective-permute-done.near
  60.7 0.6 collective-permute-done.1.ends
  61.3 1.9 %join.1 = f32[64,32,128]{2,1,0:T(8,128)} custom-call(s32[4]{0:T(128)S(1)} %pad_add_fusion.steps, s32[1]{0:T(128)} %collective-permute-done.near, f32[512,128]{1,0:T(8,128)S(1)} %get-tuple-element.16.tail, f32[64,128]{1,0:T(8,128)S(1)} %collective-permute-done.1.ends, f32[64,32,128]{2,1,0:T(8,128)} %get-tuple-element.17.begun), custom_call_target="tpu_custom_call", output_to_operand_aliasing={{}: (4, {})} | custom-call | tf_op jit(solution)/shard_map/join/pallas_call | solution.py:365
  63.2 5.1 %all-to-all-start.1 = ((f32[64,32,128]{2,1,0:T(8,128)}), f32[64,32,128]{2,1,0:T(8,128)S(1)}, u32[]{:S(2)}, u32[]{:S(2)}) async-start(f32[64,32,128]{2,1,0:T(8,128)} %join.1), calls=%async_computation.1 | async-start | bytes 2097152 | tf_op jit(solution)/shard_map/all_to_all | solution.py:322
  68.3 1.3 %dynamic-slice = u32[1]{0:T(128)} dynamic-slice(u32[512]{0:T(512)} %constant.53, u32[]{:T(128)S(6)} %add.13), dynamic_slice_sizes={1} | dynamic-slice | bytes 12
  70.3 0.1 broadcast_multiply_fusion.1
  70.4 0.1 select_reduce_fusion
  70.5 0.1 pad_maximum_fusion.1.rates
  70.6 0.2 select_reduce_fusion.1
  70.8 0.2 dynamic-update-slice
  71.0 2.4 %all-reduce = f32[16]{0:T(128)S(1)} all-reduce(f32[16]{0:T(128)S(1)} %dynamic-update-slice), channel_id=2, replica_groups=mesh['az'=64,'chip'=4,'core'=2] {'core'}, use_global_device_ids=true, to_apply=%add | all-reduce | flops 16 | bytes 128
  73.5 0.1 reshape.66
  73.6 20.2 %all-gather.2 = f32[4,2,8]{2,1,0:T(2,128)S(1)} all-gather(f32[1,2,8]{2,1,0:T(2,128)S(1)} %reshape.66), channel_id=3, replica_groups=mesh['az'=64,'chip'=4,'core'=2] {'chip'}, dimensions={0}, use_global_device_ids=true | all-gather | bytes 320 | tf_op jit(solution)/shard_map/all_gather | solution.py:391
  93.8 0.1 reshape.58.totals
  93.9 8.5 %all-to-all-done.1 = f32[64,32,128]{2,1,0:T(8,128)S(1)} async-done(((f32[64,32,128]{2,1,0:T(8,128)}), f32[64,32,128]{2,1,0:T(8,128)S(1)}, u32[]{:S(2)}, u32[]{:S(2)}) %all-to-all-start.1) | async-done | bytes 1048608 | tf_op jit(solution)/shard_map/all_to_all | solution.py:322
  102.3 2.8 %spread.1 = (f32[5,2,96,256]{3,2,1,0:T(8,128)}, f32[96]{0:T(128)}) custom-call(s32[1]{0:T(128)} %bitcast.rank, f32[384]{0:T(512)S(1)} %pad_maximum_fusion.1.rates, f32[64]{0:T(128)S(1)} %reshape.58.totals, f32[96]{0:T(128)S(1)} %get-tuple-element.15.local, f32[2048,128]{1,0:T(8,128)S(1)} %bitcast.14), custom_call_target="tpu_custom_call" | custom-call | tf_op jit(solution)/shard_map/spread/pallas_call | solution.py:393
  (7 shorter events, 0.1 us)
Async XLA Ops:
  3.3 52.8 %all-to-all-start = ((f32[64,32,128]{2,1,0:T(8,128)}), f32[64,32,128]{2,1,0:T(8,128)S(1)}, u32[]{:S(2)}, u32[]{:S(2)}) async-start(f32[64,32,128]{2,1,0:T(8,128)} %pack.1), calls=%async_computation | async-start | bytes 2097152 | tf_op jit(solution)/shard_map/all_to_all | solution.py:322
  21.5 0.7 copy-start
  24.0 36.7 %collective-permute-start = (s32[1]{0:T(128)}, s32[1]{0:T(128)}, u32[]{:S(2)}, u32[]{:S(2)}) collective-permute-start(s32[1]{0:T(128)} %select_n.39), channel_id=1, source_target_pairs={{0,1},{1,2},{2,3},{3,4},{4,5},{5,6},{6,7},{8,9},{9,10},{10,11},{11... | collective-permute-start | bytes 20 | tf_op jit(solution)/shard_map/ppermute | solution.py:350
  26.8 0.7 copy-start.1
  26.8 0.7 copy-start.2
  26.8 0.7 copy-start.3
  26.8 0.7 copy-start.4
  56.1 5.2 %collective-permute-start.1 = (f32[64,128]{1,0:T(8,128)S(1)}, f32[64,128]{1,0:T(8,128)S(1)}, u32[]{:S(2)}, u32[]{:S(2)}) collective-permute-start(f32[64,128]{1,0:T(8,128)S(1)} %bitcast.15), channel_id=1, source_target_pairs={{0,1},{1,2},{2,3},{3,4},{4,5},{5,6},{6,7},{8,9},{9,10},{10,11},{11... | collective-permute-start | bytes 98312 | tf_op jit(solution)/shard_map/ppermute | solution.py:351
  63.2 39.1 %all-to-all-start.1 = ((f32[64,32,128]{2,1,0:T(8,128)}), f32[64,32,128]{2,1,0:T(8,128)S(1)}, u32[]{:S(2)}, u32[]{:S(2)}) async-start(f32[64,32,128]{2,1,0:T(8,128)} %join.1), calls=%async_computation.1 | async-start | bytes 2097152 | tf_op jit(solution)/shard_map/all_to_all | solution.py:322

commit v9 on v7

--- a/solution.py
+++ b/solution.py
@@ -115,17 +115,29 @@
     moved[...] = jnp.where(crossed, twice[pl.ds(RING - 1 - blocks, RING), :], twice[pl.ds(RING - blocks, RING), :])
 
 
-def join_kernel(tail, ends, begun, moved, rows, sem):
+def join_kernel(brim, tail, ends, begun, moved, rows, sems):
+    edges = pltpu.make_async_copy(brim.reshape(RING, 8, 128), moved.at[:, pl.ds(8, 8), :], sems.at[0])
+    edges.start()
     rows[...] = tail[...]
     rows[pl.ds(7, RING, stride=8), :] = ends[...]
-    copy = pltpu.make_async_copy(rows.reshape(RING, 8, 128), moved.at[:, pl.ds(24, 8), :], sem)
-    copy.start()
-    copy.wait()
-
-
-def shift_kernel(steps, lines, begun, tail, mass, square):
+    last = pltpu.make_async_copy(rows.reshape(RING, 8, 128), moved.at[:, pl.ds(24, 8), :], sems.at[1])
+    last.start()
+    edges.wait()
+    last.wait()
+
+
+def shift_kernel(steps, lines, begun, brim, tail, mass, moved, square, sems):
     lane, line = iotas()
-    moved = begun.reshape(RING * BLOCK, 128)
+    blocks = moved.reshape(RING, BLOCK, 128)
+
+    def copies_of(quarter):
+        part = pl.ds(quarter * (RING // 4), RING // 4)
+        for half in range(2):
+            rows = pl.ds(HALF * half, 8)
+            yield pltpu.make_async_copy(
+                blocks.at[part, rows, :], begun.at[part, rows, :], sems.at[2 * quarter + half]
+            )
+
     whole, part, early = [], [], []
     for group in range(GROUPS):
         shift = steps[group]
@@ -167,11 +179,11 @@
                 edges[tile] = jnp.where(lane >> 1 == ring, pltpu.roll(both, (2 * ring + 1) & 127, 1), edges[tile])
         for i in range(STEP):
             for tile in range(2):
-                if i % 2 == 1 and tile == 1:
+                if tile == 1:
                     at = pl.multiple_of((first_piece + i) // 2 * 8, 8)
-                    tail[pl.ds(at, 8), :] = values[i][tile]
+                    (brim, tail)[i % 2][pl.ds(at, 8), :] = values[i][tile]
                 else:
-                    at = pl.multiple_of((first_piece + i) * HALF + 8 * tile, 8)
+                    at = pl.multiple_of((first_piece + i) * HALF, 8)
                     moved[pl.ds(at, 8), :] = values[i][tile]
         return before, tuple(edges)
 
@@ -183,15 +195,20 @@
     steps_each = PIECES // STEP // 4
     for quarter in range(4):
         state = lax.fori_loop(steps_each * quarter, steps_each * (quarter + 1), several, state)
+        for copy in copies_of(quarter):
+            copy.start()
     _, edges = state
     square[...] = jnp.concatenate([edges[0], edges[1], jnp.zeros((112, 128), jnp.float32)], axis=0).T
     left = square[pl.ds(0, RING, stride=2), :]
     right = square[pl.ds(1, RING, stride=2), :]
     left = jnp.concatenate([left[RING - 1 :], left[: RING - 1]], axis=0)
     right = jnp.concatenate([right[1:], right[:1]], axis=0)
-    moved[pl.ds(15, RING, stride=BLOCK), :] = left + pltpu.roll(right, 16, 1)
+    brim[pl.ds(7, RING, stride=8), :] = left + pltpu.roll(right, 16, 1)
     parts = lines[pl.ds(15, RING, stride=BLOCK), :]
     mass[...] = jnp.broadcast_to(jnp.sum(parts, axis=0, keepdims=True), (8, 128))
+    for quarter in range(4):
+        for copy in copies_of(quarter):
+            copy.wait()
 
 
 def spread_kernel(rank, rates, totals, local, lines, updated, enclosed, done, ends, square):
@@ -361,29 +378,34 @@
     outward = [(q * ranks + i, q * ranks + i + 1) for q in range(RING // 2) for i in range(ranks - 1)]
     inward = [(q * ranks + i + 1, q * ranks + i) for q in range(RING // 2, RING) for i in range(ranks - 1)]
     ends = lax.ppermute(ends, ("az",) + RAD, outward + inward)
-    begun, tail, mass = pl.pallas_call(
+    begun, brim, tail, mass = pl.pallas_call(
         shift_kernel,
         out_shape=(
             blocks,
             jax.ShapeDtypeStruct((RING * 8, 128), jnp.float32),
+            jax.ShapeDtypeStruct((RING * 8, 128), jnp.float32),
             jax.ShapeDtypeStruct((8, 128), jnp.float32),
         ),
         in_specs=specs(smem, vmem),
-        out_specs=specs(vmem, vmem, vmem),
-        scratch_shapes=[pltpu.VMEM((128, 128), jnp.float32)],
+        out_specs=specs(pl.ANY, vmem, vmem, vmem),
+        scratch_shapes=[
+            pltpu.VMEM((RING * BLOCK, 128), jnp.float32),
+            pltpu.VMEM((128, 128), jnp.float32),
+            pltpu.SemaphoreType.DMA((8,)),
+        ],
         compiler_params=params,
         name="shift",
     )(steps, whole)
     moved = pl.pallas_call(
         join_kernel,
         out_shape=blocks,
-        in_specs=specs(vmem, vmem, pl.ANY),
+        in_specs=specs(vmem, vmem, vmem, pl.ANY),
         out_specs=specs(pl.ANY)[0],
-        scratch_shapes=[pltpu.VMEM((RING * 8, 128), jnp.float32), pltpu.SemaphoreType.DMA],
-        input_output_aliases={2: 0},
+        scratch_shapes=[pltpu.VMEM((RING * 8, 128), jnp.float32), pltpu.SemaphoreType.DMA((2,))],
+        input_output_aliases={3: 0},
         compiler_params=params,
         name="join",
-    )(tail, ends, begun)
+    )(brim, tail, ends, begun)
     lines = dealt(moved)
 
     row_mass = cycle_area * mass[0, :ROWS] / (2.0 * RING * 256)

time: 105 us -> 105 us (level)
  no operation moved by 1% of the time
where the time goes in v9:
time: 105 us; the launch traced here: 104 us
  waiting for transfers between devices  40.5 us (39%)
  starting transfers between devices  25.2 us (24%)
  blocking collectives  22.3 us (21%)
  Pallas kernels  9.21 us (9%)
  local copies, waits for them, and re-layouts  3.8 us (4%)
  between operations  2.7 us (3%)
    all_to_all x2, waiting for transfers between devices, dealt(): lax.all_to_all(lines, 'az', 0, 0, tiled=True).reshape(RING * BLOCK, 128)  39.5 us
    all_to_all x2, starting transfers between devices, dealt(): lax.all_to_all(lines, 'az', 0, 0, tiled=True).reshape(RING * BLOCK, 128)  23.2 us
    all_gather x1, blocking collectives, shards(): lax.all_gather(lax.all_gather(ends, 'core'), 'chip').reshape(ranks * 8)  19.8 us
    pallas_call x1, Pallas kernels, shards(): pl.pallas_call(spread_kernel, out_shape=(jax.ShapeDtypeStruct(fields.shap...  2.84 us
    unnamed x14, local copies, waits for them, and re-layouts  2.84 us
    pallas_call x1, Pallas kernels, shards(): pl.pallas_call(pack_kernel, out_shape=blocks, in_specs=specs(pltpu.HBM, p...  2.65 us
    unnamed x1, blocking collectives  2.44 us
    pallas_call x1, Pallas kernels, shards(): pl.pallas_call(shift_kernel, out_shape=(blocks, jax.ShapeDtypeStruct((RIN...  2.25 us
  transfers between devices with their start and end apart: 3, of which 3 were waited for; matrix products, arithmetic and copies ran while one was open for 3% of the time, Pallas kernels for 2%

profile of v9, /device:TPU:8, one launch (start us, length us, event | category | flops | bytes accessed | tf_op | source)
XLA Modules:
  0.0 104.3 jit_solution(1167015812467313832)
XLA Ops:
  0.6 2.7 %pack.1 = f32[64,32,128]{2,1,0:T(8,128)} custom-call(s32[96]{0:T(128)} %given.1, f32[5,2,96,256]{3,2,1,0:T(8,128)} %fields.1), custom_call_target="tpu_custom_call" | custom-call | tf_op jit(solution)/shard_map/pack/pallas_call | solution.py:346
  3.3 18.2 %all-to-all-start = ((f32[64,32,128]{2,1,0:T(8,128)}), f32[64,32,128]{2,1,0:T(8,128)S(1)}, u32[]{:S(2)}, u32[]{:S(2)}) async-start(f32[64,32,128]{2,1,0:T(8,128)} %pack.1), calls=%async_computation | async-start | bytes 2097152 | tf_op jit(solution)/shard_map/all_to_all | solution.py:343
  21.5 0.0 copy-start
  21.5 0.6 copy-done
  22.1 0.1 reshape.56
  22.2 0.2 dynamic-slice_reduce_fusion
  22.4 0.6 fusion.1
  24.3 0.0 copy-start.1
  24.3 0.0 copy-start.2
  24.3 0.0 copy-start.3
  24.3 0.0 copy-start.4
  24.3 0.1 pad_add_fusion.steps
  24.4 0.5 copy-done.1
  24.9 0.0 copy-done.2
  24.9 0.0 copy-done.3
  24.9 0.0 copy-done.4
  25.0 0.1 pad_maximum_fusion
  25.0 31.0 %all-to-all-done = f32[64,32,128]{2,1,0:T(8,128)S(1)} async-done(((f32[64,32,128]{2,1,0:T(8,128)}), f32[64,32,128]{2,1,0:T(8,128)S(1)}, u32[]{:S(2)}, u32[]{:S(2)}) %all-to-all-start) | async-done | bytes 1048608 | tf_op jit(solution)/shard_map/all_to_all | solution.py:343
  56.0 0.6 ends.1
  56.6 1.9 %collective-permute-start = (f32[64,128]{1,0:T(8,128)S(1)}, f32[64,128]{1,0:T(8,128)S(1)}, u32[]{:S(2)}, u32[]{:S(2)}) collective-permute-start(f32[64,128]{1,0:T(8,128)S(1)} %ends.1), channel_id=1, source_target_pairs={{0,1},{1,2},{2,3},{3,4},{4,5},{5,6},{6,7},{8,9},{9,10},{10,11},{11... | collective-permute-start | bytes 98312 | tf_op jit(solution)/shard_map/ppermute | solution.py:380
  58.6 2.3 %shift.1 = (f32[64,32,128]{2,1,0:T(8,128)}, f32[512,128]{1,0:T(8,128)S(1)}, f32[512,128]{1,0:T(8,128)S(1)}, f32[8,128]{1,0:T(8,128)S(1)}) custom-call(s32[5]{0:T(128)S(1)} %pad_add_fusion.steps, f32[2048,128]{1,0:T(8,128)S(1)} %bitcast.11), custom_call_target="tpu_custom_call" | custom-call | tf_op jit(solution)/shard_map/shift/pallas_call | solution.py:381
  60.8 1.0 collective-permute-done.ends
  61.9 0.9 join.1
  62.8 5.1 %all-to-all-start.1 = ((f32[64,32,128]{2,1,0:T(8,128)}), f32[64,32,128]{2,1,0:T(8,128)S(1)}, u32[]{:S(2)}, u32[]{:S(2)}) async-start(f32[64,32,128]{2,1,0:T(8,128)} %join.1), calls=%async_computation.1 | async-start | bytes 2097152 | tf_op jit(solution)/shard_map/all_to_all | solution.py:343
  67.8 1.3 %dynamic-slice = u32[1]{0:T(128)} dynamic-slice(u32[512]{0:T(512)} %constant.53, u32[]{:T(128)S(6)} %add.13), dynamic_slice_sizes={1} | dynamic-slice | bytes 12
  69.8 0.1 broadcast_multiply_fusion.1
  69.9 0.1 select_reduce_fusion
  70.0 0.1 pad_maximum_fusion.1.rates
  70.1 0.2 select_reduce_fusion.1
  70.3 0.2 dynamic-update-slice
  70.5 2.4 %all-reduce = f32[16]{0:T(128)S(1)} all-reduce(f32[16]{0:T(128)S(1)} %dynamic-update-slice), channel_id=2, replica_groups=mesh['az'=64,'chip'=4,'core'=2] {'core'}, use_global_device_ids=true, to_apply=%add | all-reduce | flops 16 | bytes 128
  73.0 0.1 reshape.66
  73.1 19.8 %all-gather.2 = f32[4,2,8]{2,1,0:T(2,128)S(1)} all-gather(f32[1,2,8]{2,1,0:T(2,128)S(1)} %reshape.66), channel_id=3, replica_groups=mesh['az'=64,'chip'=4,'core'=2] {'chip'}, dimensions={0}, use_global_device_ids=true | all-gather | bytes 320 | tf_op jit(solution)/shard_map/all_gather | solution.py:421
  92.9 0.1 reshape.58.totals
  93.0 8.5 %all-to-all-done.1 = f32[64,32,128]{2,1,0:T(8,128)S(1)} async-done(((f32[64,32,128]{2,1,0:T(8,128)}), f32[64,32,128]{2,1,0:T(8,128)S(1)}, u32[]{:S(2)}, u32[]{:S(2)}) %all-to-all-start.1) | async-done | bytes 1048608 | tf_op jit(solution)/shard_map/all_to_all | solution.py:343
  101.4 2.8 %spread.1 = (f32[5,2,96,256]{3,2,1,0:T(8,128)}, f32[96]{0:T(128)}) custom-call(s32[1]{0:T(128)} %bitcast.rank, f32[384]{0:T(512)S(1)} %pad_maximum_fusion.1.rates, f32[64]{0:T(128)S(1)} %reshape.58.totals, f32[96]{0:T(128)S(1)} %get-tuple-element.16.local, f32[2048,128]{1,0:T(8,128)S(1)} %bitcast.12), custom_call_target="tpu_custom_call" | custom-call | tf_op jit(solution)/shard_map/spread/pallas_call | solution.py:423
  (6 shorter events, 0.0 us)
Async XLA Ops:
  3.3 52.8 %all-to-all-start = ((f32[64,32,128]{2,1,0:T(8,128)}), f32[64,32,128]{2,1,0:T(8,128)S(1)}, u32[]{:S(2)}, u32[]{:S(2)}) async-start(f32[64,32,128]{2,1,0:T(8,128)} %pack.1), calls=%async_computation | async-start | bytes 2097152 | tf_op jit(solution)/shard_map/all_to_all | solution.py:343
  21.5 0.7 copy-start
  24.3 0.7 copy-start.1
  24.3 0.7 copy-start.2
  24.3 0.7 copy-start.3
  24.3 0.7 copy-start.4
  56.6 5.2 %collective-permute-start = (f32[64,128]{1,0:T(8,128)S(1)}, f32[64,128]{1,0:T(8,128)S(1)}, u32[]{:S(2)}, u32[]{:S(2)}) collective-permute-start(f32[64,128]{1,0:T(8,128)S(1)} %ends.1), channel_id=1, source_target_pairs={{0,1},{1,2},{2,3},{3,4},{4,5},{5,6},{6,7},{8,9},{9,10},{10,11},{11... | collective-permute-start | bytes 98312 | tf_op jit(solution)/shard_map/ppermute | solution.py:380
  62.8 38.7 %all-to-all-start.1 = ((f32[64,32,128]{2,1,0:T(8,128)}), f32[64,32,128]{2,1,0:T(8,128)S(1)}, u32[]{:S(2)}, u32[]{:S(2)}) async-start(f32[64,32,128]{2,1,0:T(8,128)} %join.1), calls=%async_computation.1 | async-start | bytes 2097152 | tf_op jit(solution)/shard_map/all_to_all | solution.py:343

commit v10 on v7

--- a/solution.py
+++ b/solution.py
@@ -244,10 +244,11 @@
 
     def begin(row):
         cells = {spot: lines[pl.ds(place_of(row, *spot), 8), :] for spot in spots()}
-        full, partial = [], []
+        full, partial, rads = [], [], []
         for tile in range(2):
             az, rad, rate = spread(0, row, tile), spread(ROWS, row, tile), pulls(row, tile)
             keep = 1.0 - 2.0 * (az + rad)
+            rads.append(rad)
             border = edges[tile] - rate * under_edges[tile]
             for layer in range(2):
                 low, high = (source(cells[tile, layer, half], rate) for half in range(2))
@@ -258,11 +259,11 @@
                 high_sum = jnp.where(lane == 0, low_up, high_up) + jnp.where(lane == 127, side, high_down)
                 full += [low, high]
                 partial += [keep * low + az * low_sum, keep * high + az * high_sum]
-        return full, partial
-
-    def end(row, partial, under, over):
+        return full, partial, rads
+
+    def end(row, partial, under, over, rads):
         for tile in range(2):
-            rad = spread(ROWS, row, tile)
+            rad = rads[tile]
             for layer in range(2):
                 for half in range(2):
                     at = 4 * tile + 2 * layer + half
@@ -274,8 +275,8 @@
             source(lines[pl.ds(first, 8, stride=BLOCK), :], rate) for at, _, _, first in windows() if at == side
         ]
 
-    last, last_partial = begin(SPAN - 1)
-    full, partial = begin(0)
+    last, last_partial, last_rads = begin(SPAN - 1)
+    full, partial, rads = begin(0)
     turned = [pltpu.roll(value, 5, 0) for value in last]
     under = [jnp.where(line < 5, value, turned[i]) for i, value in enumerate(outer(0))]
     under += [jnp.where(line < 5, turned[i], turned[4 + i]) for i in range(4)]
@@ -291,17 +292,17 @@
         return [ends[pl.ds(first + 8 * i, 8), :] for i in range(8)]
 
     def rows(step, state):
-        under, full, partial = state
+        under, full, partial, rads = state
         for row in range(30):
             row = 30 * step + row + 1
-            over, later = begin(row)
-            end(row - 1, partial, under, over)
-            under, full, partial = full, over, later
-        return under, full, partial
-
-    under, full, partial = lax.fori_loop(0, (SPAN - 2) // 30, rows, (under, full, partial))
-    end(SPAN - 2, partial, under, kept(64))
-    end(SPAN - 1, kept(128), full, kept(192))
+            over, later, coming = begin(row)
+            end(row - 1, partial, under, over, rads)
+            under, full, partial, rads = full, over, later, coming
+        return under, full, partial, rads
+
+    under, full, partial, rads = lax.fori_loop(0, (SPAN - 2) // 30, rows, (under, full, partial, rads))
+    end(SPAN - 2, partial, under, kept(64), rads)
+    end(SPAN - 1, kept(128), full, kept(192), last_rads)
     for place, field in enumerate(ORDER):
         for layer in range(2):
             taken = {}

time: 105 us -> 105 us (level)
  no operation moved by 1% of the time
where the time goes in v10:
time: 105 us; the launch traced here: 104 us
  waiting for transfers between devices  40.2 us (38%)
  starting transfers between devices  25.2 us (24%)
  blocking collectives  22.6 us (22%)
  Pallas kernels  9.41 us (9%)
  local copies, waits for them, and re-layouts  3.8 us (4%)
  between operations  2.69 us (3%)
    all_to_all x2, waiting for transfers between devices, dealt(): lax.all_to_all(lines, 'az', 0, 0, tiled=True).reshape(RING * BLOCK, 128)  39.5 us
    all_to_all x2, starting transfers between devices, dealt(): lax.all_to_all(lines, 'az', 0, 0, tiled=True).reshape(RING * BLOCK, 128)  23.2 us
    all_gather x1, blocking collectives, shards(): lax.all_gather(lax.all_gather(ends, 'core'), 'chip').reshape(ranks * 8)  20.2 us
    unnamed x14, local copies, waits for them, and re-layouts  2.84 us
    pallas_call x1, Pallas kernels, shards(): pl.pallas_call(spread_kernel, out_shape=(jax.ShapeDtypeStruct(fields.shap...  2.83 us
    pallas_call x1, Pallas kernels, shards(): pl.pallas_call(pack_kernel, out_shape=blocks, in_specs=specs(pltpu.HBM, p...  2.65 us
    pallas_call x1, Pallas kernels, shards(): pl.pallas_call(shift_kernel, out_shape=(blocks, jax.ShapeDtypeStruct((RIN...  2.6 us
    unnamed x1, blocking collectives  2.44 us
  transfers between devices with their start and end apart: 3, of which 3 were waited for; matrix products, arithmetic and copies ran while one was open for 3% of the time, Pallas kernels for 2%

profile of v10, /device:TPU:8, one launch (start us, length us, event | category | flops | bytes accessed | tf_op | source)
XLA Modules:
  0.0 104.5 jit_solution(6034165055754721576)
XLA Ops:
  0.6 2.7 %pack.1 = f32[64,32,128]{2,1,0:T(8,128)} custom-call(s32[96]{0:T(128)} %given.1, f32[5,2,96,256]{3,2,1,0:T(8,128)} %fields.1), custom_call_target="tpu_custom_call" | custom-call | tf_op jit(solution)/shard_map/pack/pallas_call | solution.py:330
  3.3 18.2 %all-to-all-start = ((f32[64,32,128]{2,1,0:T(8,128)}), f32[64,32,128]{2,1,0:T(8,128)S(1)}, u32[]{:S(2)}, u32[]{:S(2)}) async-start(f32[64,32,128]{2,1,0:T(8,128)} %pack.1), calls=%async_computation | async-start | bytes 2097152 | tf_op jit(solution)/shard_map/all_to_all | solution.py:327
  21.5 0.0 copy-start
  21.5 0.6 copy-done
  22.1 0.1 reshape.56
  22.2 0.2 dynamic-slice_reduce_fusion
  22.4 0.6 fusion.1
  24.3 0.0 copy-start.1
  24.3 0.0 copy-start.2
  24.3 0.0 copy-start.3
  24.3 0.0 copy-start.4
  24.3 0.1 pad_add_fusion.steps
  24.4 0.5 copy-done.1
  24.9 0.0 copy-done.2
  24.9 0.0 copy-done.3
  24.9 0.0 copy-done.4
  25.0 0.1 pad_maximum_fusion
  25.0 31.0 %all-to-all-done = f32[64,32,128]{2,1,0:T(8,128)S(1)} async-done(((f32[64,32,128]{2,1,0:T(8,128)}), f32[64,32,128]{2,1,0:T(8,128)S(1)}, u32[]{:S(2)}, u32[]{:S(2)}) %all-to-all-start) | async-done | bytes 1048608 | tf_op jit(solution)/shard_map/all_to_all | solution.py:327
  56.0 0.6 ends.1
  56.6 1.9 %collective-permute-start = (f32[64,128]{1,0:T(8,128)S(1)}, f32[64,128]{1,0:T(8,128)S(1)}, u32[]{:S(2)}, u32[]{:S(2)}) collective-permute-start(f32[64,128]{1,0:T(8,128)S(1)} %ends.1), channel_id=1, source_target_pairs={{0,1},{1,2},{2,3},{3,4},{4,5},{5,6},{6,7},{8,9},{9,10},{10,11},{11... | collective-permute-start | bytes 98312 | tf_op jit(solution)/shard_map/ppermute | solution.py:364
  58.6 2.6 %shift.1 = (f32[64,32,128]{2,1,0:T(8,128)}, f32[512,128]{1,0:T(8,128)S(1)}, f32[8,128]{1,0:T(8,128)S(1)}) custom-call(s32[5]{0:T(128)S(1)} %pad_add_fusion.steps, f32[2048,128]{1,0:T(8,128)S(1)} %bitcast.11), custom_call_target="tpu_custom_call" | custom-call | tf_op jit(solution)/shard_map/shift/pallas_call | solution.py:365
  61.2 0.7 collective-permute-done.ends
  61.9 0.7 join.1
  62.6 5.1 %all-to-all-start.1 = ((f32[64,32,128]{2,1,0:T(8,128)}), f32[64,32,128]{2,1,0:T(8,128)S(1)}, u32[]{:S(2)}, u32[]{:S(2)}) async-start(f32[64,32,128]{2,1,0:T(8,128)} %join.1), calls=%async_computation.1 | async-start | bytes 2097152 | tf_op jit(solution)/shard_map/all_to_all | solution.py:327
  67.7 1.3 %dynamic-slice = u32[1]{0:T(128)} dynamic-slice(u32[512]{0:T(512)} %constant.53, u32[]{:T(128)S(6)} %add.13), dynamic_slice_sizes={1} | dynamic-slice | bytes 12
  69.7 0.1 broadcast_multiply_fusion.1
  69.8 0.1 select_reduce_fusion
  69.9 0.1 pad_maximum_fusion.1.rates
  70.0 0.2 select_reduce_fusion.1
  70.2 0.2 dynamic-update-slice
  70.4 2.4 %all-reduce = f32[16]{0:T(128)S(1)} all-reduce(f32[16]{0:T(128)S(1)} %dynamic-update-slice), channel_id=2, replica_groups=mesh['az'=64,'chip'=4,'core'=2] {'core'}, use_global_device_ids=true, to_apply=%add | all-reduce | flops 16 | bytes 128
  72.9 0.1 reshape.66
  72.9 20.2 %all-gather.2 = f32[4,2,8]{2,1,0:T(2,128)S(1)} all-gather(f32[1,2,8]{2,1,0:T(2,128)S(1)} %reshape.66), channel_id=3, replica_groups=mesh['az'=64,'chip'=4,'core'=2] {'chip'}, dimensions={0}, use_global_device_ids=true | all-gather | bytes 320 | tf_op jit(solution)/shard_map/all_gather | solution.py:400
  93.1 0.1 reshape.58.totals
  93.2 8.5 %all-to-all-done.1 = f32[64,32,128]{2,1,0:T(8,128)S(1)} async-done(((f32[64,32,128]{2,1,0:T(8,128)}), f32[64,32,128]{2,1,0:T(8,128)S(1)}, u32[]{:S(2)}, u32[]{:S(2)}) %all-to-all-start.1) | async-done | bytes 1048608 | tf_op jit(solution)/shard_map/all_to_all | solution.py:327
  101.6 2.8 %spread.1 = (f32[5,2,96,256]{3,2,1,0:T(8,128)}, f32[96]{0:T(128)}) custom-call(s32[1]{0:T(128)} %bitcast.rank, f32[384]{0:T(512)S(1)} %pad_maximum_fusion.1.rates, f32[64]{0:T(128)S(1)} %reshape.58.totals, f32[96]{0:T(128)S(1)} %get-tuple-element.15.local, f32[2048,128]{1,0:T(8,128)S(1)} %bitcast.12), custom_call_target="tpu_custom_call" | custom-call | tf_op jit(solution)/shard_map/spread/pallas_call | solution.py:402
  (6 shorter events, 0.0 us)
Async XLA Ops:
  3.3 52.8 %all-to-all-start = ((f32[64,32,128]{2,1,0:T(8,128)}), f32[64,32,128]{2,1,0:T(8,128)S(1)}, u32[]{:S(2)}, u32[]{:S(2)}) async-start(f32[64,32,128]{2,1,0:T(8,128)} %pack.1), calls=%async_computation | async-start | bytes 2097152 | tf_op jit(solution)/shard_map/all_to_all | solution.py:327
  21.5 0.7 copy-start
  24.3 0.7 copy-start.1
  24.3 0.7 copy-start.2
  24.3 0.7 copy-start.3
  24.3 0.7 copy-start.4
  56.6 5.2 %collective-permute-start = (f32[64,128]{1,0:T(8,128)S(1)}, f32[64,128]{1,0:T(8,128)S(1)}, u32[]{:S(2)}, u32[]{:S(2)}) collective-permute-start(f32[64,128]{1,0:T(8,128)S(1)} %ends.1), channel_id=1, source_target_pairs={{0,1},{1,2},{2,3},{3,4},{4,5},{5,6},{6,7},{8,9},{9,10},{10,11},{11... | collective-permute-start | bytes 98312 | tf_op jit(solution)/shard_map/ppermute | solution.py:364
  62.6 39.0 %all-to-all-start.1 = ((f32[64,32,128]{2,1,0:T(8,128)}), f32[64,32,128]{2,1,0:T(8,128)S(1)}, u32[]{:S(2)}, u32[]{:S(2)}) async-start(f32[64,32,128]{2,1,0:T(8,128)} %join.1), calls=%async_computation.1 | async-start | bytes 2097152 | tf_op jit(solution)/shard_map/all_to_all | solution.py:327

commit v11 on v7

--- a/solution.py
+++ b/solution.py
@@ -40,6 +40,8 @@
     lane, line = iotas()
     shift_copy = pltpu.make_async_copy(given, shifts, sems.at[GROUPS * PARTS])
     shift_copy.start()
+    density = pltpu.make_async_copy(fields.at[0], cells.at[0], sems.at[GROUPS * PARTS + 1])
+    density.start()
     copies = {}
     for part, group in sorted(
         ((part, group) for part in range(PARTS) for group in range(GROUPS)),
@@ -47,9 +49,15 @@
     ):
         rows = pl.ds(SPAN * group + 8 * part, 8)
         copies[part, group] = pltpu.make_async_copy(
-            fields.at[:, :, rows, :], cells.at[:, :, rows, :], sems.at[GROUPS * part + group]
+            fields.at[pl.ds(1, 4), :, rows, :], cells.at[pl.ds(1, 4), :, rows, :], sems.at[GROUPS * part + group]
         )
         copies[part, group].start()
+    density.wait()
+    halves = [cells[0, z, :, pl.ds(128 * h, 128)] for z in range(2) for h in range(2)]
+    total = (halves[0] + halves[1]) + (halves[2] + halves[3])
+    square = jnp.concatenate([total, jnp.zeros((128 - ROWS, 128), jnp.float32)], axis=0)
+    mass = jnp.sum(square.T, axis=0, keepdims=True)
+    lines[pl.ds(15, RING, stride=BLOCK), :] = jnp.broadcast_to(mass, (RING, 128))
     arrived = [(0, 0), (PARTS - 1, GROUPS - 1)]
     for at in arrived:
         copies[at].wait()
@@ -92,14 +100,7 @@
                         ]
             for first, value in taken.items():
                 lines[pl.ds(first, 8, stride=2 * BLOCK), :] = value
-        send(16 * part, 16, 0, 8)
-        send(16 * part, 16, 16, 32)
-    halves = [cells[0, z, :, pl.ds(128 * h, 128)] for z in range(2) for h in range(2)]
-    total = (halves[0] + halves[1]) + (halves[2] + halves[3])
-    square = jnp.concatenate([total, jnp.zeros((128 - ROWS, 128), jnp.float32)], axis=0)
-    mass = jnp.sum(square.T, axis=0, keepdims=True)
-    lines[pl.ds(15, RING, stride=BLOCK), :] = jnp.broadcast_to(mass, (RING, 128))
-    send(0, RING, 8, 16)
+        send(16 * part, 16, 0, 32)
     for copy in sending:
         copy.wait()
 
@@ -335,8 +336,8 @@
             pltpu.VMEM(fields.shape, jnp.float32),
             pltpu.VMEM((RING * BLOCK, 128), jnp.float32),
             pltpu.SMEM(shifts.shape, jnp.int32),
-            pltpu.SemaphoreType.DMA((GROUPS * PARTS + 1,)),
-            pltpu.SemaphoreType.DMA((2 * PARTS + 1,)),
+            pltpu.SemaphoreType.DMA((GROUPS * PARTS + 2,)),
+            pltpu.SemaphoreType.DMA((PARTS,)),
         ],
         compiler_params=pltpu.CompilerParams(vmem_limit_bytes=60 * 1024 * 1024),
         name="pack",

time: 105 us -> 105 us (level)
  no operation moved by 1% of the time
where the time goes in v11:
time: 105 us
  waiting for transfers between devices  40.2 us (38%)
  starting transfers between devices  25.2 us (24%)
  blocking collectives  22.6 us (22%)
  Pallas kernels  9.46 us (9%)
  local copies, waits for them, and re-layouts  3.8 us (4%)
  between operations  2.69 us (3%)
    all_to_all x2, waiting for transfers between devices, dealt(): lax.all_to_all(lines, 'az', 0, 0, tiled=True).reshape(RING * BLOCK, 128)  39.5 us
    all_to_all x2, starting transfers between devices, dealt(): lax.all_to_all(lines, 'az', 0, 0, tiled=True).reshape(RING * BLOCK, 128)  23.2 us
    all_gather x1, blocking collectives, shards(): lax.all_gather(lax.all_gather(ends, 'core'), 'chip').reshape(ranks * 8)  20.2 us
    pallas_call x1, Pallas kernels, shards(): pl.pallas_call(spread_kernel, out_shape=(jax.ShapeDtypeStruct(fields.shap...  2.84 us
    unnamed x14, local copies, waits for them, and re-layouts  2.84 us
    pallas_call x1, Pallas kernels, shards(): pl.pallas_call(pack_kernel, out_shape=blocks, in_specs=specs(pltpu.HBM, p...  2.69 us
    pallas_call x1, Pallas kernels, shards(): pl.pallas_call(shift_kernel, out_shape=(blocks, jax.ShapeDtypeStruct((RIN...  2.6 us
    unnamed x1, blocking collectives  2.44 us
  transfers between devices with their start and end apart: 3, of which 3 were waited for; matrix products, arithmetic and copies ran while one was open for 3% of the time, Pallas kernels for 2%

profile of v11, /device:TPU:8, one launch (start us, length us, event | category | flops | bytes accessed | tf_op | source)
XLA Modules:
  0.0 104.5 jit_solution(9488072559336493795)
XLA Ops:
  0.6 2.7 %pack.1 = f32[64,32,128]{2,1,0:T(8,128)} custom-call(s32[96]{0:T(128)} %given.1, f32[5,2,96,256]{3,2,1,0:T(8,128)} %fields.1), custom_call_target="tpu_custom_call" | custom-call | tf_op jit(solution)/shard_map/pack/pallas_call | solution.py:330
  3.3 18.2 %all-to-all-start = ((f32[64,32,128]{2,1,0:T(8,128)}), f32[64,32,128]{2,1,0:T(8,128)S(1)}, u32[]{:S(2)}, u32[]{:S(2)}) async-start(f32[64,32,128]{2,1,0:T(8,128)} %pack.1), calls=%async_computation | async-start | bytes 2097152 | tf_op jit(solution)/shard_map/all_to_all | solution.py:327
  21.5 0.0 copy-start
  21.5 0.6 copy-done
  22.2 0.1 reshape.56
  22.2 0.2 dynamic-slice_reduce_fusion
  22.4 0.6 fusion.1
  24.3 0.0 copy-start.1
  24.3 0.0 copy-start.2
  24.3 0.0 copy-start.3
  24.3 0.0 copy-start.4
  24.3 0.1 pad_add_fusion.steps
  24.4 0.5 copy-done.1
  24.9 0.0 copy-done.2
  25.0 0.0 copy-done.3
  25.0 0.0 copy-done.4
  25.0 0.1 pad_maximum_fusion
  25.1 31.0 %all-to-all-done = f32[64,32,128]{2,1,0:T(8,128)S(1)} async-done(((f32[64,32,128]{2,1,0:T(8,128)}), f32[64,32,128]{2,1,0:T(8,128)S(1)}, u32[]{:S(2)}, u32[]{:S(2)}) %all-to-all-start) | async-done | bytes 1048608 | tf_op jit(solution)/shard_map/all_to_all | solution.py:327
  56.1 0.6 ends.1
  56.7 1.9 %collective-permute-start = (f32[64,128]{1,0:T(8,128)S(1)}, f32[64,128]{1,0:T(8,128)S(1)}, u32[]{:S(2)}, u32[]{:S(2)}) collective-permute-start(f32[64,128]{1,0:T(8,128)S(1)} %ends.1), channel_id=1, source_target_pairs={{0,1},{1,2},{2,3},{3,4},{4,5},{5,6},{6,7},{8,9},{9,10},{10,11},{11... | collective-permute-start | bytes 98312 | tf_op jit(solution)/shard_map/ppermute | solution.py:364
  58.6 2.6 %shift.1 = (f32[64,32,128]{2,1,0:T(8,128)}, f32[512,128]{1,0:T(8,128)S(1)}, f32[8,128]{1,0:T(8,128)S(1)}) custom-call(s32[5]{0:T(128)S(1)} %pad_add_fusion.steps, f32[2048,128]{1,0:T(8,128)S(1)} %bitcast.11), custom_call_target="tpu_custom_call" | custom-call | tf_op jit(solution)/shard_map/shift/pallas_call | solution.py:365
  61.2 0.7 collective-permute-done.ends
  61.9 0.7 join.1
  62.7 5.1 %all-to-all-start.1 = ((f32[64,32,128]{2,1,0:T(8,128)}), f32[64,32,128]{2,1,0:T(8,128)S(1)}, u32[]{:S(2)}, u32[]{:S(2)}) async-start(f32[64,32,128]{2,1,0:T(8,128)} %join.1), calls=%async_computation.1 | async-start | bytes 2097152 | tf_op jit(solution)/shard_map/all_to_all | solution.py:327
  67.8 1.3 %dynamic-slice = u32[1]{0:T(128)} dynamic-slice(u32[512]{0:T(512)} %constant.53, u32[]{:T(128)S(6)} %add.13), dynamic_slice_sizes={1} | dynamic-slice | bytes 12
  69.7 0.1 broadcast_multiply_fusion.1
  69.8 0.1 select_reduce_fusion
  69.9 0.1 pad_maximum_fusion.1.rates
  70.0 0.2 select_reduce_fusion.1
  70.2 0.2 dynamic-update-slice
  70.4 2.4 %all-reduce = f32[16]{0:T(128)S(1)} all-reduce(f32[16]{0:T(128)S(1)} %dynamic-update-slice), channel_id=2, replica_groups=mesh['az'=64,'chip'=4,'core'=2] {'core'}, use_global_device_ids=true, to_apply=%add | all-reduce | flops 16 | bytes 128
  72.9 0.1 reshape.66
  73.0 20.2 %all-gather.2 = f32[4,2,8]{2,1,0:T(2,128)S(1)} all-gather(f32[1,2,8]{2,1,0:T(2,128)S(1)} %reshape.66), channel_id=3, replica_groups=mesh['az'=64,'chip'=4,'core'=2] {'chip'}, dimensions={0}, use_global_device_ids=true | all-gather | bytes 320 | tf_op jit(solution)/shard_map/all_gather | solution.py:400
  93.1 0.1 reshape.58.totals
  93.2 8.5 %all-to-all-done.1 = f32[64,32,128]{2,1,0:T(8,128)S(1)} async-done(((f32[64,32,128]{2,1,0:T(8,128)}), f32[64,32,128]{2,1,0:T(8,128)S(1)}, u32[]{:S(2)}, u32[]{:S(2)}) %all-to-all-start.1) | async-done | bytes 1048608 | tf_op jit(solution)/shard_map/all_to_all | solution.py:327
  101.7 2.8 %spread.1 = (f32[5,2,96,256]{3,2,1,0:T(8,128)}, f32[96]{0:T(128)}) custom-call(s32[1]{0:T(128)} %bitcast.rank, f32[384]{0:T(512)S(1)} %pad_maximum_fusion.1.rates, f32[64]{0:T(128)S(1)} %reshape.58.totals, f32[96]{0:T(128)S(1)} %get-tuple-element.15.local, f32[2048,128]{1,0:T(8,128)S(1)} %bitcast.12), custom_call_target="tpu_custom_call" | custom-call | tf_op jit(solution)/shard_map/spread/pallas_call | solution.py:402
  (6 shorter events, 0.0 us)
Async XLA Ops:
  3.3 52.8 %all-to-all-start = ((f32[64,32,128]{2,1,0:T(8,128)}), f32[64,32,128]{2,1,0:T(8,128)S(1)}, u32[]{:S(2)}, u32[]{:S(2)}) async-start(f32[64,32,128]{2,1,0:T(8,128)} %pack.1), calls=%async_computation | async-start | bytes 2097152 | tf_op jit(solution)/shard_map/all_to_all | solution.py:327
  21.5 0.7 copy-start
  24.3 0.7 copy-start.1
  24.3 0.7 copy-start.2
  24.3 0.7 copy-start.3
  24.3 0.7 copy-start.4
  56.7 5.2 %collective-permute-start = (f32[64,128]{1,0:T(8,128)S(1)}, f32[64,128]{1,0:T(8,128)S(1)}, u32[]{:S(2)}, u32[]{:S(2)}) collective-permute-start(f32[64,128]{1,0:T(8,128)S(1)} %ends.1), channel_id=1, source_target_pairs={{0,1},{1,2},{2,3},{3,4},{4,5},{5,6},{6,7},{8,9},{9,10},{10,11},{11... | collective-permute-start | bytes 98312 | tf_op jit(solution)/shard_map/ppermute | solution.py:364
  62.7 39.0 %all-to-all-start.1 = ((f32[64,32,128]{2,1,0:T(8,128)}), f32[64,32,128]{2,1,0:T(8,128)S(1)}, u32[]{:S(2)}, u32[]{:S(2)}) async-start(f32[64,32,128]{2,1,0:T(8,128)} %join.1), calls=%async_computation.1 | async-start | bytes 2097152 | tf_op jit(solution)/shard_map/all_to_all | solution.py:327
